TPU v7x, 32 devices: a whole 2x2x4 slice. The times are simulated.
32 devices in a mesh: fsdp: 4 (over z), ctx: 2 (over core), tp: 4 (over y, x).
Axes of the slice: x: 2, y: 2, z: 4, core: 2. Of those that a mesh axis runs over, the one named last changes fastest.
Arguments:
- block_input: bfloat16 [4, 2048, 2048], P('fsdp', 'ctx'), may hold values from -6 to 6
- segment_ids: int32 [4, 2048], P('fsdp', 'ctx'), may hold values from 0 to 15, never falling along the last dimension, each value on 1 to 1024 neighbouring positions
- positions: int32 [4, 2048], P('fsdp', 'ctx'), may hold values from 0 to 8191
- out_cotangent: bfloat16 [4, 2048, 2048], P('fsdp', 'ctx'), may hold values from -6 to 6
- norm_gains: float32 [2, 2048], P(None, ('fsdp', 'ctx')), may hold values from 0.5 to 1.5
- qkv_weight: float32 [3, 2048, 2048], P(None, ('fsdp', 'ctx'), 'tp'), may hold values from -0.125 to 0.125
- outproj_weight: float32 [2048, 2048], P(('fsdp', 'ctx'), 'tp'), may hold values from -1 to 1
- gateup_weight: float32 [2, 2048, 8192], P(None, ('fsdp', 'ctx'), 'tp'), may hold values from -0.125 to 0.125
- down_weight: float32 [2048, 8192], P(('fsdp', 'ctx'), 'tp'), may hold values from -0.0625 to 0.0625
- moment_norm: float32 [2, 2048], P(None, ('fsdp', 'ctx')), may hold values from -256 to 256
- moment_qkv: float32 [3, 2048, 2048], P(None, ('fsdp', 'ctx'), 'tp'), may hold values from -112 to 112
- moment_outproj: float32 [2048, 2048], P(('fsdp', 'ctx'), 'tp'), may hold values from -40 to 40
- moment_gateup: float32 [2, 2048, 8192], P(None, ('fsdp', 'ctx'), 'tp'), may hold values from -40 to 40
- moment_down: float32 [2048, 8192], P(('fsdp', 'ctx'), 'tp'), may hold values from -80 to 80
- square_norm: float32 [2, 2048], P(None, ('fsdp', 'ctx')), may hold values from 512 to 5120
- square_qkv: float32 [3, 2048, 2048], P(None, ('fsdp', 'ctx'), 'tp'), may hold values from 81.92 to 819.2
- square_outproj: float32 [2048, 2048], P(('fsdp', 'ctx'), 'tp'), may hold values from 13.1072 to 131.072
- square_gateup: float32 [2, 2048, 8192], P(None, ('fsdp', 'ctx'), 'tp'), may hold values from 13.1072 to 131.072
- square_down: float32 [2048, 8192], P(('fsdp', 'ctx'), 'tp'), may hold values from 52.4288 to 524.288
Outputs:
- block_out: bfloat16 [4, 2048, 2048], P('fsdp', 'ctx')
- input_grad: bfloat16 [4, 2048, 2048], P('fsdp', 'ctx')
- norm_grad: float32 [2, 2048], P(None, ('fsdp', 'ctx'))
- qkv_grad: float32 [3, 2048, 2048], P(None, ('fsdp', 'ctx'), 'tp')
- outproj_grad: float32 [2048, 2048], P(('fsdp', 'ctx'), 'tp')
- gateup_grad: float32 [2, 2048, 8192], P(None, ('fsdp', 'ctx'), 'tp')
- down_grad: float32 [2048, 8192], P(('fsdp', 'ctx'), 'tp')
- new_norm: float32 [2, 2048], P(None, ('fsdp', 'ctx'))
- new_qkv: float32 [3, 2048, 2048], P(None, ('fsdp', 'ctx'), 'tp')
- new_outproj: float32 [2048, 2048], P(('fsdp', 'ctx'), 'tp')
- new_gateup: float32 [2, 2048, 8192], P(None, ('fsdp', 'ctx'), 'tp')
- new_down: float32 [2048, 8192], P(('fsdp', 'ctx'), 'tp')
- new_moment_norm: float32 [2, 2048], P(None, ('fsdp', 'ctx'))
- new_moment_qkv: float32 [3, 2048, 2048], P(None, ('fsdp', 'ctx'), 'tp')
- new_moment_outproj: float32 [2048, 2048], P(('fsdp', 'ctx'), 'tp')
- new_moment_gateup: float32 [2, 2048, 8192], P(None, ('fsdp', 'ctx'), 'tp')
- new_moment_down: float32 [2048, 8192], P(('fsdp', 'ctx'), 'tp')
- new_square_norm: float32 [2, 2048], P(None, ('fsdp', 'ctx'))
- new_square_qkv: float32 [3, 2048, 2048], P(None, ('fsdp', 'ctx'), 'tp')
- new_square_outproj: float32 [2048, 2048], P(('fsdp', 'ctx'), 'tp')
- new_square_gateup: float32 [2, 2048, 8192], P(None, ('fsdp', 'ctx'), 'tp')
- new_square_down: float32 [2048, 8192], P(('fsdp', 'ctx'), 'tp')
Inputs may be any that keep to these rules, and one draw needn't show every extreme that they name: `segment_ids`: within a sequence ids start at 0 and never fall; a document holds at most 1024 tokens and some document holds exactly that many.
All inputs are finite; a program needn't handle non-finite values.
Results may differ from a plain program's by a relative error of at most 0.017.
The roundings to bfloat16 on the way count: a program that leaves them out, or rounds other values in their place, can miss the bound.
Values may be sent and summed in bfloat16 or wider, within the bound.
No kernel may reach another device: no remote copies, remote signals or barrier semaphores. Data moves between devices by JAX's collectives and lax.ppermute only.
A program may use at most 448 MiB of HBM per device.

v0:
```python
import math

import jax
import jax.numpy as jnp
from jax import lax
from jax.sharding import PartitionSpec as P

D = 2048
HEAD_DIM = 64
FF = 8192
STEP = 10


beta_one = 0.9
beta_two = 0.95
adam_eps = 1e-08
decay_rate = 0.1


def rope_tables(where_at):
    half = HEAD_DIM // 2
    freqs = jnp.exp(jnp.arange(half, dtype=jnp.float32) * (-2.0 * math.log(130000.0) / HEAD_DIM))
    angles = where_at.astype(jnp.float32)[..., None] * freqs
    return (jnp.cos(angles), jnp.sin(angles))


def rotate(tensor, cosine, sine):
    half = tensor.shape[-1] // 2
    first = tensor[..., :half]
    second = tensor[..., half:]
    cosine = cosine[..., None, :]
    sine = sine[..., None, :]
    return jnp.concatenate([first * cosine - second * sine, second * cosine + first * sine], -1)


def normalize(values):
    scale = lax.rsqrt(jnp.mean(values * values, -1, keepdims=True) + 1e-05)
    return (values * scale, scale)


def norm_back(upstream, normed, scale, weights):
    scaled = upstream * weights
    return (
        scale * (scaled - normed * jnp.mean(scaled * normed, -1, keepdims=True)),
        jnp.sum(upstream * normed, 0),
    )


def adamw(weight, gradient, moment, square, step_size):
    moment_new = beta_one * moment + (1.0 - beta_one) * gradient
    square_new = beta_two * square + (1.0 - beta_two) * gradient * gradient
    moment_hat = moment_new / (1.0 - beta_one**STEP)
    square_hat = square_new / (1.0 - beta_two**STEP)
    weight_new = weight - step_size * (
        moment_hat / (jnp.sqrt(square_hat) + adam_eps) + decay_rate * weight
    )
    return (weight_new, moment_new, square_new)


def local(
    block_input,
    segment_ids,
    positions,
    out_cotangent,
    norm_gains,
    qkv_weight,
    outproj_weight,
    gateup_weight,
    down_weight,
    moment_norm,
    moment_qkv,
    moment_outproj,
    moment_gateup,
    moment_down,
    square_norm,
    square_qkv,
    square_outproj,
    square_gateup,
    square_down,
):
    bf16 = jnp.bfloat16
    f32 = jnp.float32
    seqs_here, tok_here, width = block_input.shape
    rows_all = seqs_here * tok_here
    share_rows = rows_all // lax.axis_size("tp")
    share_start = lax.axis_index("tp") * share_rows

    def own_rows(values):
        return lax.dynamic_slice_in_dim(values, share_start, share_rows, 0)

    gains16, qkv16, outproj16, gateup16, down16 = (
        lax.all_gather(norm_gains.astype(bf16), ("fsdp", "ctx"), axis=1, tiled=True),
        lax.all_gather(qkv_weight.astype(bf16), ("fsdp", "ctx"), axis=1, tiled=True),
        lax.all_gather(outproj_weight.astype(bf16), ("fsdp", "ctx"), axis=0, tiled=True),
        lax.all_gather(gateup_weight.astype(bf16), ("fsdp", "ctx"), axis=1, tiled=True),
        lax.all_gather(down_weight.astype(bf16), ("fsdp", "ctx"), axis=0, tiled=True),
    )
    gain_attn = gains16[0].astype(f32)
    gain_mlp = gains16[1].astype(f32)
    columns = qkv16.shape[2]
    heads_here = columns // HEAD_DIM
    head_shape = (rows_all, heads_here, HEAD_DIM)
    four_shape = (seqs_here, tok_here, heads_here, HEAD_DIM)
    inputs32 = block_input.reshape(rows_all, width).astype(f32)
    normed_one, scale_one = normalize(inputs32)
    act_one = (normed_one * gain_attn).astype(bf16)
    projected = jnp.einsum("nd,jdc->jnc", act_one, qkv16, preferred_element_type=f32)
    cosine, sine = rope_tables(positions.reshape(rows_all))
    query16 = (
        rotate(projected[0].reshape(head_shape), cosine, sine).astype(bf16).reshape(four_shape)
    )
    key16 = (
        rotate(projected[1].reshape(head_shape), cosine, sine)
        .astype(bf16)
        .reshape(seqs_here, tok_here, columns)
    )
    value16 = projected[2].astype(bf16).reshape(seqs_here, tok_here, columns)
    segment16 = segment_ids.astype(bf16)
    key_all, value_all, segment_all = (
        lax.all_gather(key16, "ctx", axis=1, tiled=True),
        lax.all_gather(value16, "ctx", axis=1, tiled=True),
        lax.all_gather(segment16, "ctx", axis=1, tiled=True),
    )
    seq_len = key_all.shape[1]
    key_all4 = key_all.reshape(seqs_here, seq_len, heads_here, HEAD_DIM)
    value_all4 = value_all.reshape(seqs_here, seq_len, heads_here, HEAD_DIM)
    query_index = lax.axis_index("ctx") * tok_here + jnp.arange(tok_here)
    key_index = jnp.arange(seq_len)
    allowed = (key_index[None, None, :] <= query_index[None, :, None]) & (
        segment_all[:, None, :] == segment16[:, :, None]
    )

    def scores_of():
        raw = jnp.einsum("sqhe,skhe->shqk", query16, key_all4, preferred_element_type=f32) * 0.125
        return jnp.where(allowed[:, None], raw, -jnp.inf)

    scores = scores_of()
    top = jnp.max(scores, -1, keepdims=True)
    log_total = top + jnp.log(jnp.sum(jnp.exp(scores - top), -1, keepdims=True))
    probs16 = jnp.exp(scores - log_total).astype(bf16)
    attended16 = (
        jnp.einsum("shqk,skhe->sqhe", probs16, value_all4, preferred_element_type=f32)
        .astype(bf16)
        .reshape(rows_all, columns)
    )
    attn_partial = jnp.dot(attended16, outproj16.T, preferred_element_type=f32)
    resid = own_rows(inputs32) + lax.psum_scatter(
        attn_partial, "tp", scatter_dimension=0, tiled=True
    )
    normed_two, scale_two = normalize(resid)
    act_two = lax.all_gather((normed_two * gain_mlp).astype(bf16), "tp", axis=0, tiled=True)
    gate_up = jnp.einsum("nd,jdf->jnf", act_two, gateup16, preferred_element_type=f32)
    gate_pre = gate_up[0]
    up_pre = gate_up[1]
    sigma = jax.nn.sigmoid(gate_pre)
    inner16 = (gate_pre * sigma * up_pre).astype(bf16)
    mlp_partial = jnp.dot(inner16, down16.T, preferred_element_type=f32)
    out_share16 = (
        resid
        + lax.psum_scatter(
            mlp_partial.astype(jnp.bfloat16), "tp", scatter_dimension=0, tiled=True
        ).astype(jnp.float32)
    ).astype(bf16)
    cotan16 = out_cotangent.reshape(rows_all, width)
    dinner = jnp.dot(cotan16, down16, preferred_element_type=f32)
    down_local = jnp.einsum("nd,nf->df", cotan16, inner16, preferred_element_type=f32)
    dgate16 = (dinner * up_pre * sigma * (1.0 + gate_pre * (1.0 - sigma))).astype(bf16)
    dup16 = (dinner * gate_pre * sigma).astype(bf16)
    dgateup16 = jnp.stack([dgate16, dup16])
    gateup_local = jnp.einsum("nd,jnf->jdf", act_two, dgateup16, preferred_element_type=f32)
    dact_partial = jnp.einsum("jnf,jdf->nd", dgateup16, gateup16, preferred_element_type=f32)
    dact_two = lax.psum_scatter(dact_partial, "tp", scatter_dimension=0, tiled=True)
    dnorm_two, gain_two_local = norm_back(dact_two, normed_two, scale_two, gain_mlp)
    dresid = own_rows(cotan16).astype(f32) + dnorm_two
    out_full, dresid16 = (
        lax.all_gather(out_share16, "tp", axis=0, tiled=True),
        lax.all_gather(dresid.astype(bf16), "tp", axis=0, tiled=True),
    )
    block_out = out_full.reshape(block_input.shape)
    outproj_local = jnp.einsum("nd,nc->dc", dresid16, attended16, preferred_element_type=f32)
    dattended16 = jnp.dot(dresid16, outproj16, preferred_element_type=f32).astype(bf16)
    dattended4 = dattended16.reshape(four_shape)
    back_scores = scores_of()
    probs_back = jnp.exp(back_scores - log_total)
    probs_back16 = probs_back.astype(bf16)
    dprobs = jnp.einsum("sqhe,skhe->shqk", dattended4, value_all4, preferred_element_type=f32)
    delta = jnp.einsum(
        "sqhe,sqhe->shq", dattended4.astype(f32), attended16.reshape(four_shape).astype(f32)
    )[..., None]
    dscores16 = (probs_back * (dprobs - delta)).astype(bf16)
    dquery = 0.125 * jnp.einsum("shqk,skhe->sqhe", dscores16, key_all4, preferred_element_type=f32)
    count = tok_here * lax.axis_size("ctx")
    dkey_part = 0.125 * jnp.einsum(
        "shqk,sqhe->kshe", dscores16, query16, preferred_element_type=f32
    )
    dvalue_part = jnp.einsum(
        "shqk,sqhe->kshe", probs_back16, dattended4, preferred_element_type=f32
    )
    both = jnp.stack(
        [
            dkey_part.reshape(count, seqs_here, columns),
            dvalue_part.reshape(count, seqs_here, columns),
        ],
        2,
    )
    key_grads = lax.psum_scatter(
        both.reshape(count, seqs_here * 2 * columns), "ctx", scatter_dimension=0, tiled=True
    )
    key_grads = jnp.transpose(key_grads.reshape(tok_here, seqs_here, 2, columns), (2, 1, 0, 3))
    dquery16 = (
        rotate(dquery.reshape(head_shape), cosine, -sine).astype(bf16).reshape(rows_all, columns)
    )
    dkey16 = (
        rotate(key_grads[0].reshape(head_shape), cosine, -sine)
        .astype(bf16)
        .reshape(rows_all, columns)
    )
    dvalue16 = key_grads[1].reshape(rows_all, columns).astype(bf16)
    dproj16 = jnp.stack([dquery16, dkey16, dvalue16])
    qkv_local = jnp.einsum("nd,jnc->jdc", act_one, dproj16, preferred_element_type=f32)
    dact_one_partial = jnp.einsum("jnc,jdc->nd", dproj16, qkv16, preferred_element_type=f32)
    dact_one = lax.psum_scatter(dact_one_partial, "tp", scatter_dimension=0, tiled=True)
    dnorm_one, gain_one_local = norm_back(
        dact_one, own_rows(normed_one), own_rows(scale_one), gain_attn
    )
    grad_share16 = (dresid + dnorm_one).astype(bf16)
    input_grad = lax.all_gather(grad_share16, "tp", axis=0, tiled=True).reshape(block_input.shape)
    gains_local = lax.psum(jnp.stack([gain_one_local, gain_two_local]), "tp")
    norm_grad, qkv_grad, outproj_grad, gateup_grad, down_grad = (
        lax.psum_scatter(gains_local, ("fsdp", "ctx"), scatter_dimension=1, tiled=True),
        lax.psum_scatter(qkv_local, ("fsdp", "ctx"), scatter_dimension=1, tiled=True),
        lax.psum_scatter(outproj_local, ("fsdp", "ctx"), scatter_dimension=0, tiled=True),
        lax.psum_scatter(gateup_local, ("fsdp", "ctx"), scatter_dimension=1, tiled=True),
        lax.psum_scatter(down_local, ("fsdp", "ctx"), scatter_dimension=0, tiled=True),
    )
    new_norm, new_moment_norm, new_square_norm = adamw(
        norm_gains, norm_grad, moment_norm, square_norm, 0.4
    )
    new_qkv, new_moment_qkv, new_square_qkv = adamw(
        qkv_weight, qkv_grad, moment_qkv, square_qkv, 0.4 / math.sqrt(D)
    )
    new_outproj, new_moment_outproj, new_square_outproj = adamw(
        outproj_weight, outproj_grad, moment_outproj, square_outproj, 0.4 / math.sqrt(D // 64)
    )
    new_gateup, new_moment_gateup, new_square_gateup = adamw(
        gateup_weight, gateup_grad, moment_gateup, square_gateup, 0.4 / math.sqrt(D)
    )
    new_down, new_moment_down, new_square_down = adamw(
        down_weight, down_grad, moment_down, square_down, 0.4 / math.sqrt(FF)
    )
    return (
        block_out,
        input_grad,
        norm_grad,
        qkv_grad,
        outproj_grad,
        gateup_grad,
        down_grad,
        new_norm,
        new_qkv,
        new_outproj,
        new_gateup,
        new_down,
        new_moment_norm,
        new_moment_qkv,
        new_moment_outproj,
        new_moment_gateup,
        new_moment_down,
        new_square_norm,
        new_square_qkv,
        new_square_outproj,
        new_square_gateup,
        new_square_down,
    )


def solution(mesh):
    placed = (
        P("fsdp", "ctx", None),
        P("fsdp", "ctx"),
        P("fsdp", "ctx"),
        P("fsdp", "ctx", None),
        P(None, ("fsdp", "ctx")),
        P(None, ("fsdp", "ctx"), "tp"),
        P(("fsdp", "ctx"), "tp"),
        P(None, ("fsdp", "ctx"), "tp"),
        P(("fsdp", "ctx"), "tp"),
        P(None, ("fsdp", "ctx")),
        P(None, ("fsdp", "ctx"), "tp"),
        P(("fsdp", "ctx"), "tp"),
        P(None, ("fsdp", "ctx"), "tp"),
        P(("fsdp", "ctx"), "tp"),
        P(None, ("fsdp", "ctx")),
        P(None, ("fsdp", "ctx"), "tp"),
        P(("fsdp", "ctx"), "tp"),
        P(None, ("fsdp", "ctx"), "tp"),
        P(("fsdp", "ctx"), "tp"),
    )
    return jax.shard_map(
        local,
        mesh=mesh,
        in_specs=placed,
        out_specs=(
            P("fsdp", "ctx", None),
            P("fsdp", "ctx", None),
            P(None, ("fsdp", "ctx")),
            P(None, ("fsdp", "ctx"), "tp"),
            P(("fsdp", "ctx"), "tp"),
            P(None, ("fsdp", "ctx"), "tp"),
            P(("fsdp", "ctx"), "tp"),
            P(None, ("fsdp", "ctx")),
            P(None, ("fsdp", "ctx"), "tp"),
            P(("fsdp", "ctx"), "tp"),
            P(None, ("fsdp", "ctx"), "tp"),
            P(("fsdp", "ctx"), "tp"),
            P(None, ("fsdp", "ctx")),
            P(None, ("fsdp", "ctx"), "tp"),
            P(("fsdp", "ctx"), "tp"),
            P(None, ("fsdp", "ctx"), "tp"),
            P(("fsdp", "ctx"), "tp"),
            P(None, ("fsdp", "ctx")),
            P(None, ("fsdp", "ctx"), "tp"),
            P(("fsdp", "ctx"), "tp"),
            P(None, ("fsdp", "ctx"), "tp"),
            P(("fsdp", "ctx"), "tp"),
        ),
        check_vma=False,
    )
```

profile of v0, /device:TPU:0, one launch (start us, length us, event | category | flops | bytes accessed | tf_op | source)
XLA Modules:
  0.0 1903.2 jit_solution(9971543105118504296)
XLA Ops:
  10.3 13.4 all_gather.38
  28.2 50.1 %all-gather.11.cloned.1.call-done = bf16[3,2048,512]{1,2,0:T(8,128)(2,1)} async-done(((bf16[3,256,512]{1,2,0:T(8,128)(2,1)}), bf16[3,2048,512]{1,2,0:T(8,128)(2,1)}) %all-gather.11.cloned.1.call-update) | async-done | bytes 6291472 | tf_op jit(solution)/shard_map/all_gather | solution.py:93
  102.1 27.3 %fusion.1 = (f32[8,1024]{1,0:T(8,128)S(1)}, f32[8,1024,2048]{2,1,0:T(8,128)}) fusion(pred[1024,2048]{1,0:T(8,128)(4,1)S(1)} %fusion.13, bf16[2048,8,64]{0,2,1:T(8,128)(2,1)} %bitcast.195, bf16[1024,8,32]{0,2,1:T(8,128)(2,1)S(1)} %get-tuple-element.118, bf16[1024,8,32]{0,2,1:T(8,128)(2,1)S(1)} %get-tuple-element.117), kind=kOutput, calls=%fused_computation.5 | convolution fusion | flops 2199904256 | bytes 72384512 | tf_op jit(solution)/shard_map/sqhe,skhe->shqk/dot_general | solution.py:134
  129.3 21.9 %exponential_reduce_fusion = f32[8,1024]{1,0:T(8,128)S(1)} fusion(f32[8,1024,2048]{2,1,0:T(8,128)} %get-tuple-element.133, f32[8,1024]{1,0:T(8,128)S(1)} %get-tuple-element.132, pred[1024,2048]{1,0:T(8,128)(4,1)S(1)} %fusion.13), kind=kLoop, calls=%fused_computation.2 | loop fusion | flops 67100672 | bytes 69271552 | tf_op jit(solution)/shard_map/reduce_sum | solution.py:139
  151.3 25.2 %convolution_convert_fusion = bf16[8,64,1024]{2,1,0:T(8,128)(2,1)S(1)} fusion(bf16[2048,8,64]{0,2,1:T(8,128)(2,1)} %bitcast.209, f32[8,1024,2048]{2,1,0:T(8,128)} %get-tuple-element.133, f32[8,1024]{1,0:T(8,128)S(1)} %log_add_fusion, pred[1024,2048]{1,0:T(8,128)(4,1)S(1)} %fusion.13), kind=kOutput, calls=%fused_computation.79 | convolution fusion | flops 2215116800 | bytes 72384512 | tf_op jit(solution)/shard_map/shqk,skhe->sqhe/dot_general | solution.py:142
  195.3 75.9 %reduce-scatter.13.cloned.1.call-done = f32[256,2048]{1,0:T(8,128)} async-done(((f32[1024,2048]{1,0:T(8,128)}), f32[256,2048]{1,0:T(8,128)}) %reduce-scatter.13.cloned.1.call-update) | async-done | bytes 2097168 | tf_op jit(solution)/shard_map/reduce_scatter | solution.py:147
  278.1 146.4 %all-gather.21.cloned.1.call-done = bf16[2,2048,2048]{2,1,0:T(8,128)(2,1)} async-done(((bf16[2,256,2048]{2,1,0:T(8,128)(2,1)}), bf16[2,2048,2048]{2,1,0:T(8,128)(2,1)}) %all-gather.21.cloned.1.call-update) | async-done | bytes 16777232 | tf_op jit(solution)/shard_map/all_gather | solution.py:95
  424.5 53.5 %all-gather.19.cloned.1.call-done = bf16[1024,2048]{1,0:T(8,128)(2,1)} async-done(((bf16[256,2048]{1,0:T(8,128)(2,1)}), bf16[1024,2048]{1,0:T(8,128)(2,1)}) %all-gather.19.cloned.1.call-update) | async-done | bytes 4194320 | tf_op jit(solution)/shard_map/all_gather | solution.py:151
  478.0 23.5 %convolution_bitcast_fusion.2 = f32[2,1024,2048]{2,1,0:T(8,128)} fusion(bf16[2,2048,2048]{2,1,0:T(8,128)(2,1)} %all-gather.21.cloned.1.call-done, bf16[1024,2048]{1,0:T(8,128)(2,1)} %all-gather.19.cloned.1.call-done), kind=kOutput, calls=%fused_computation.33 | convolution fusion | flops 17179869184 | bytes 37748736 | tf_op jit(solution)/shard_map/nd,jdf->jnf/dot_general | solution.py:152
  501.5 60.8 %all-gather.23.cloned.1.call-done = bf16[2048,2048]{1,0:T(8,128)(2,1)} async-done(((bf16[256,2048]{1,0:T(8,128)(2,1)}), bf16[2048,2048]{1,0:T(8,128)(2,1)}) %all-gather.23.cloned.1.call-update) | async-done | bytes 8388624 | tf_op jit(solution)/shard_map/all_gather | solution.py:96
  562.3 18.2 fusion.27
  583.9 21.7 %fusion.15 = f32[1024,2048]{1,0:T(8,128)} fusion(bf16[2,2048,2048]{2,1,0:T(8,128)(2,1)} %all-gather.21.cloned.1.call-done, bf16[1,1024,2048]{2,1,0:T(8,128)(2,1)S(1)} %get-tuple-element.110, bf16[1,1024,2048]{2,1,0:T(8,128)(2,1)S(1)} %get-tuple-element.109), kind=kOutput, calls=%fused_computation.37 | convolution fusion | flops 17184063488 | bytes 33554432 | tf_op jit(solution)/shard_map/jnf,jdf->nd/dot_general | solution.py:171
  605.9 84.9 %reduce-scatter.17.cloned.1.call-done = f32[256,2048]{1,0:T(8,128)} async-done(((f32[1024,2048]{1,0:T(8,128)}), f32[256,2048]{1,0:T(8,128)}) %reduce-scatter.17.cloned.1.call-update) | async-done | bytes 2097168 | tf_op jit(solution)/shard_map/reduce_scatter | solution.py:172
  696.7 52.8 %all-gather.27.cloned.1.call-done = bf16[1024,2048]{1,0:T(8,128)(2,1)} async-done(((bf16[256,2048]{1,0:T(8,128)(2,1)}), bf16[1024,2048]{1,0:T(8,128)(2,1)}) %all-gather.27.cloned.1.call-update) | async-done | bytes 4194320 | tf_op jit(solution)/shard_map/all_gather | solution.py:177
  755.0 27.3 %fusion.49 = f32[8,64,2048]{2,1,0:T(8,128)} fusion(bf16[1024,8,64]{0,2,1:T(8,128)(2,1)S(1)} %bitcast.213, f32[8,1024,2048]{2,1,0:T(8,128)} %get-tuple-element.133, f32[8,1024]{1,0:T(8,128)S(1)} %log_add_fusion, pred[1024,2048]{1,0:T(8,128)(4,1)S(1)} %copy-done.6), kind=kOutput, calls=%fused_computation.125 | convolution fusion | flops 2214592512 | bytes 74481664 | tf_op jit(solution)/shard_map/shqk,sqhe->kshe/dot_general | solution.py:196
  782.3 40.8 %multiply_convert_fusion = bf16[8,1024,2048]{2,1,0:T(8,128)(2,1)} fusion(f32[8,1024,2048]{2,1,0:T(8,128)} %get-tuple-element.133, f32[8,1024]{1,0:T(8,128)S(1)} %get-tuple-element.134, f32[8,1024]{1,0:T(8,128)S(1)} %log_add_fusion, pred[1024,2048]{1,0:T(8,128)(4,1)S(1)} %copy-done.6, bf16[1024,8,64]{0,2,1:T(8,128)(2,1)S(1)} %bitcast.214, ...), kind=kOutput, calls=%fused_computation | convolution fusion | flops 2248146944 | bytes 105971712 | tf_op jit(solution)/shard_map/sqhe,skhe->shqk/dot_general | solution.py:186
  823.1 13.6 convolution_multiply_fusion
  843.1 19.1 %multiply_bitcast_fusion = f32[1024,8,64]{0,2,1:T(8,128)S(1)} fusion(bf16[2048,8,64]{0,2,1:T(8,128)(2,1)} %bitcast.196, bf16[8,1024,2048]{2,1,0:T(8,128)(2,1)} %multiply_convert_fusion), kind=kOutput, calls=%fused_computation.71 | convolution fusion | flops 2148007936 | bytes 37748736 | tf_op jit(solution)/shard_map/shqk,skhe->sqhe/dot_general | solution.py:191
  879.7 11.5 convolution_bitcast_fusion.4
  891.2 17.9 fusion.28
  917.2 17.9 convolution_bitcast_fusion.1
  941.9 35.8 %reduce-scatter.21.cloned.1.call-done = f32[256,2048]{1,0:T(8,128)} async-done(((f32[1024,2048]{1,0:T(8,128)}), f32[256,2048]{1,0:T(8,128)}) %reduce-scatter.21.cloned.1.call-update) | async-done | bytes 2097168 | tf_op jit(solution)/shard_map/reduce_scatter | solution.py:222
  981.9 52.0 %reduce-scatter.15.cloned.1.call-done = bf16[256,2048]{1,0:T(8,128)(2,1)} async-done(((bf16[1024,2048]{1,0:T(8,128)(2,1)}), bf16[256,2048]{1,0:T(8,128)(2,1)}) %reduce-scatter.15.cloned.1.call-update) | async-done | bytes 1048592 | tf_op jit(solution)/shard_map/reduce_scatter | solution.py:160
  1040.3 12.2 convolution_bitcast_fusion.3
  1052.7 25.5 %convolution_bitcast_fusion = f32[2,2048,2048]{1,2,0:T(8,128)} fusion(bf16[1,1024,2048]{2,1,0:T(8,128)(2,1)} %copy-done.45, bf16[1,1024,2048]{2,1,0:T(8,128)(2,1)} %copy-done.44, bf16[1024,2048]{1,0:T(8,128)(2,1)} %all-gather.19.cloned.1.call-done), kind=kOutput, calls=%fused_computation.6 | convolution fusion | flops 17184063488 | bytes 46137344 | tf_op jit(solution)/shard_map/nd,jnf->jdf/dot_general | solution.py:170
  1110.9 145.2 %reduce-scatter.29.cloned.1.call-done = f32[256,2048]{0,1:T(8,128)} async-done(((f32[2048,2048]{0,1:T(8,128)}), f32[256,2048]{0,1:T(8,128)}) %reduce-scatter.29.cloned.1.call-update) | async-done | bytes 2097168 | tf_op jit(solution)/shard_map/reduce_scatter | solution.py:234
  1273.5 16.0 reduce-scatter.31.cloned.1.call-done
  1301.4 41.7 %all-gather.25.cloned.1.call-done = bf16[1024,2048]{1,0:T(8,128)(2,1)} async-done(((bf16[256,2048]{1,0:T(8,128)(2,1)}), bf16[1024,2048]{1,0:T(8,128)(2,1)}) %all-gather.25.cloned.1.call-update) | async-done | bytes 4194320 | tf_op jit(solution)/shard_map/all_gather | solution.py:176
  1343.1 55.2 %all-gather.29.cloned.1.call-done = bf16[1024,2048]{1,0:T(8,128)(2,1)} async-done(((bf16[256,2048]{1,0:T(8,128)(2,1)}), bf16[1024,2048]{1,0:T(8,128)(2,1)}) %all-gather.29.cloned.1.call-update) | async-done | bytes 4194320 | tf_op jit(solution)/shard_map/all_gather | solution.py:227
  1398.3 131.7 %reduce-scatter.23.cloned.1.call-done = f32[3,256,512]{1,2,0:T(8,128)} async-done(((f32[3,2048,512]{1,2,0:T(8,128)}), f32[3,256,512]{1,2,0:T(8,128)}) %reduce-scatter.23.cloned.1.call-update) | async-done | bytes 1572880 | tf_op jit(solution)/shard_map/reduce_scatter | solution.py:231
  1544.2 312.0 %reduce-scatter.27.cloned.1.call-done = f32[2,256,2048]{1,2,0:T(8,128)} async-done(((f32[2,2048,2048]{1,2,0:T(8,128)}), f32[2,256,2048]{1,2,0:T(8,128)}) %reduce-scatter.27.cloned.1.call-update) | async-done | bytes 4194320 | tf_op jit(solution)/shard_map/reduce_scatter | solution.py:233
  1856.2 11.4 multiply_subtract_fusion
  (215 shorter events, 225.5 us)
Async XLA Ops:
  7.2 71.1 %all-gather.11.cloned.1.call-start = ((), (), s32[]{:S(2)}) async-start(), calls=%async_computation.10 | async-start | bytes 7077888 | tf_op jit(solution)/shard_map/all_gather | solution.py:93
  9.1 79.4 %copy-start.3 = (f32[3,256,512]{1,2,0:T(8,128)}, f32[3,256,512]{1,2,0:T(8,128)S(1)}, u32[]{:S(2)}) copy-start(f32[3,256,512]{1,2,0:T(8,128)S(1)} %copy.104) | copy-start | bytes 4718596
  10.2 91.8 %all-gather.15.cloned.1.call-start = ((), (), s32[]{:S(2)}) async-start(), calls=%async_computation.12 | async-start | bytes 3145728 | tf_op jit(solution)/shard_map/all_gather | solution.py:120
  28.2 63.0 %copy-start.19 = (f32[1024,32]{0,1:T(8,128)}, f32[1024,32]{0,1:T(8,128)S(1)}, u32[]{:S(2)}) copy-start(f32[1024,32]{0,1:T(8,128)S(1)} %get-tuple-element.131) | copy-start | bytes 393220
  28.2 665.5 %copy-start.24 = (f32[1,2048]{1,0:T(1,128)}, f32[1,2048]{1,0:T(1,128)S(1)}, u32[]{:S(2)}) copy-start(f32[1,2048]{1,0:T(1,128)S(1)} %get-tuple-element.127) | copy-start | bytes 24580
  93.1 58.2 %all-gather.13.cloned.1.call-start = ((), (), s32[]{:S(2)}) async-start(), calls=%async_computation.11 | async-start | bytes 3145728 | tf_op jit(solution)/shard_map/all_gather | solution.py:121
  95.9 80.7 %all-gather.17.cloned.1.call-start = ((), (), s32[]{:S(2)}) async-start(), calls=%async_computation.13 | async-start | bytes 2359296 | tf_op jit(solution)/shard_map/all_gather | solution.py:94
  96.7 174.6 %reduce-scatter.13.cloned.1.call-start = ((), (), s32[]{:S(2)}) async-start(), calls=%async_computation.14 | async-start | bytes 10485760 | tf_op jit(solution)/shard_map/reduce_scatter | solution.py:147
  184.3 240.2 %all-gather.21.cloned.1.call-start = ((), (), s32[]{:S(2)}) async-start(), calls=%async_computation.16 | async-start | bytes 18874368 | tf_op jit(solution)/shard_map/all_gather | solution.py:95
  188.6 289.4 %all-gather.19.cloned.1.call-start = ((), (), s32[]{:S(2)}) async-start(), calls=%async_computation.15 | async-start | bytes 5242880 | tf_op jit(solution)/shard_map/all_gather | solution.py:151
  273.8 419.9 %copy-start = (f32[256,2048]{1,0:T(8,128)}, f32[256,2048]{1,0:T(8,128)S(1)}, u32[]{:S(2)}) copy-start(f32[256,2048]{1,0:T(8,128)S(1)} %get-tuple-element.108) | copy-start | bytes 6291460
  273.8 419.9 %copy-start.29 = (f32[256]{0:T(256)}, f32[256]{0:T(256)S(1)}, u32[]{:S(2)}) copy-start(f32[256]{0:T(256)S(1)} %add_rsqrt_fusion.1) | copy-start | bytes 3076
  275.3 287.1 %all-gather.23.cloned.1.call-start = ((), (), s32[]{:S(2)}) async-start(), calls=%async_computation.17 | async-start | bytes 9437184 | tf_op jit(solution)/shard_map/all_gather | solution.py:96
  278.1 412.7 %reduce-scatter.17.cloned.1.call-start = ((), (), s32[]{:S(2)}) async-start(), calls=%async_computation.20 | async-start | bytes 10485760 | tf_op jit(solution)/shard_map/reduce_scatter | solution.py:172
  605.7 143.8 %all-gather.27.cloned.1.call-start = ((), (), s32[]{:S(2)}) async-start(), calls=%async_computation.21 | async-start | bytes 5242880 | tf_op jit(solution)/shard_map/all_gather | solution.py:177
  696.6 165.6 %reduce-scatter.19.cloned.1.call-start = ((), (), s32[]{:S(2)}) async-start(), calls=%async_computation.22 | async-start | bytes 12582912 | tf_op jit(solution)/shard_map/reduce_scatter | solution.py:206
  843.1 134.6 %reduce-scatter.21.cloned.1.call-start = ((), (), s32[]{:S(2)}) async-start(), calls=%async_computation.23 | async-start | bytes 10485760 | tf_op jit(solution)/shard_map/reduce_scatter | solution.py:222
  891.2 142.8 %reduce-scatter.15.cloned.1.call-start = ((), (), s32[]{:S(2)}) async-start(), calls=%async_computation.18 | async-start | bytes 5242880 | tf_op jit(solution)/shard_map/reduce_scatter | solution.py:160
  909.2 199.1 %reduce-scatter.25.cloned.1.call-start = ((), (), s32[]{:S(2)}) async-start(), calls=%async_computation.26 | async-start | bytes 4718592 | tf_op jit(solution)/shard_map/reduce_scatter | solution.py:232
  917.1 339.0 %reduce-scatter.29.cloned.1.call-start = ((), (), s32[]{:S(2)}) async-start(), calls=%async_computation.28 | async-start | bytes 18874368 | tf_op jit(solution)/shard_map/reduce_scatter | solution.py:234
  935.1 354.4 %reduce-scatter.31.cloned.1.call-start = ((), (), s32[]{:S(2)}) async-start(), calls=%async_computation.29 | async-start | bytes 1179648
  941.9 92.0 %copy-start.1 = (f32[256,2048]{1,0:T(8,128)S(1)}, f32[256,2048]{1,0:T(8,128)}, u32[]{:S(2)}) copy-start(f32[256,2048]{1,0:T(8,128)} %copy-done) | copy-start | bytes 6291460
  941.9 92.0 %copy-start.25 = (f32[1,2048]{1,0:T(1,128)S(1)}, f32[1,2048]{1,0:T(1,128)}, u32[]{:S(2)}) copy-start(f32[1,2048]{1,0:T(1,128)} %copy-done.24) | copy-start | bytes 24580
  941.9 92.0 %copy-start.30 = (f32[256]{0:T(256)S(1)}, f32[256]{0:T(256)}, u32[]{:S(2)}) copy-start(f32[256]{0:T(256)} %copy-done.29) | copy-start | bytes 3076
  941.9 92.0 %copy-start.35 = (f32[256]{0:T(256)S(1)}, f32[256]{0:T(256)}, u32[]{:S(2)}) copy-start(f32[256]{0:T(256)} %copy-done.34) | copy-start | bytes 3076
  981.9 361.2 %all-gather.25.cloned.1.call-start = ((), (), s32[]{:S(2)}) async-start(), calls=%async_computation.19 | async-start | bytes 5242880 | tf_op jit(solution)/shard_map/all_gather | solution.py:176
  1039.6 358.6 %all-gather.29.cloned.1.call-start = ((), (), s32[]{:S(2)}) async-start(), calls=%async_computation.24 | async-start | bytes 5242880 | tf_op jit(solution)/shard_map/all_gather | solution.py:227
  1040.2 489.7 %reduce-scatter.23.cloned.1.call-start = ((), (), s32[]{:S(2)}) async-start(), calls=%async_computation.25 | async-start | bytes 14155776 | tf_op jit(solution)/shard_map/reduce_scatter | solution.py:231
  1052.5 803.7 %reduce-scatter.27.cloned.1.call-start = ((), (), s32[]{:S(2)}) async-start(), calls=%async_computation.27 | async-start | bytes 37748736 | tf_op jit(solution)/shard_map/reduce_scatter | solution.py:233
  1267.5 262.4 %copy-start.4 = (f32[3,256,512]{1,2,0:T(8,128)S(1)}, f32[3,256,512]{1,2,0:T(8,128)}, u32[]{:S(2)}) copy-start(f32[3,256,512]{1,2,0:T(8,128)} %copy-done.3) | copy-start | bytes 4718596
  1267.5 262.4 %copy-start.9 = (f32[3,256,512]{1,2,0:T(8,128)S(1)}, f32[3,256,512]{1,2,0:T(8,128)}, u32[]{:S(2)}) copy-start(f32[3,256,512]{1,2,0:T(8,128)} %copy.112) | copy-start | bytes 4718596
  1300.8 234.0 %copy-start.38 = (f32[2,256]{1,0:T(2,128)}, f32[2,256]{1,0:T(2,128)S(1)}, u32[]{:S(2)}) copy-start(f32[2,256]{1,0:T(2,128)S(1)} %psum.8) | copy-start | bytes 6148
  (34 other events, 665.9 us)
Sparse Core Ops, SparseCore 0:
  10.4 67.8 all-gather.10
  93.2 8.7 all-gather.14
  104.1 11.7 all-gather.12
  117.9 30.2 all-gather.16
  184.4 86.8 reduce-scatter.12
  273.4 151.0 all-gather.20
  427.1 50.8 all-gather.18
  480.2 82.0 all-gather.22
  605.8 84.9 reduce-scatter.16
  696.7 52.6 all-gather.26
  843.2 16.8 reduce-scatter.18
  891.3 86.3 reduce-scatter.20
  981.2 52.6 reduce-scatter.14
  1037.4 49.9 reduce-scatter.24
  1089.7 166.3 reduce-scatter.28
  1258.9 30.4 reduce-scatter.30
  1291.9 51.1 all-gather.24
  1345.5 52.6 all-gather.28
  1400.7 129.2 reduce-scatter.22
  1532.3 323.8 reduce-scatter.26
where the time goes:
time: 1910 us; the launch traced here: 1900 us
  waiting for transfers between devices  1310 us (69%)
  matrix products  332 us (17%)
  local copies, waits for them, and re-layouts  108 us (6%)
  other arithmetic  105 us (5%)
  blocking collectives  25.8 us (1%)
    reduce_scatter x1, waiting for transfers between devices, local(): lax.psum_scatter(gateup_local, ('fsdp', 'ctx'), scatter_dimension=1, tile...  312 us
    all_gather x1, waiting for transfers between devices, local(): lax.all_gather(gateup_weight.astype(bf16), ('fsdp', 'ctx'), axis=1, tiled...  146 us
    reduce_scatter x1, waiting for transfers between devices, local(): lax.psum_scatter(down_local, ('fsdp', 'ctx'), scatter_dimension=0, tiled=...  145 us
    reduce_scatter x1, waiting for transfers between devices, local(): lax.psum_scatter(qkv_local, ('fsdp', 'ctx'), scatter_dimension=1, tiled=T...  132 us
    unnamed x117, local copies, waits for them, and re-layouts  90.4 us
    reduce_scatter x1, waiting for transfers between devices, local(): lax.psum_scatter(dact_partial, 'tp', scatter_dimension=0, tiled=True)  84.9 us
    reduce_scatter x1, waiting for transfers between devices, local(): lax.psum_scatter(attn_partial, 'tp', scatter_dimension=0, tiled=True)  75.9 us
    all_gather x1, waiting for transfers between devices, local(): lax.all_gather(down_weight.astype(bf16), ('fsdp', 'ctx'), axis=0, tiled=T...  60.8 us
  transfers between devices with their start and end apart: 20, of which 15 were waited for; matrix products, arithmetic and copies ran while one was open for 16% of the time, Pallas kernels for 0%

commit v1 on v0

v1 whole, which is shorter than its diff:
```python
import functools
import math

import jax
import jax.numpy as jnp
from jax import lax
from jax.experimental import pallas as pl
from jax.experimental.pallas import tpu as pltpu
from jax.sharding import PartitionSpec as P

D = 2048
HEAD_DIM = 64
FF = 8192
STEP = 10

bf16 = jnp.bfloat16
f32 = jnp.float32

beta_one = 0.9
beta_two = 0.95
adam_eps = 1e-08
decay_rate = 0.1

BLOCK = 256
PAIR = 2 * HEAD_DIM
HIDDEN = -1e30
VMEM = 56 * 1024 * 1024


def rope_tables(where_at):
    half = HEAD_DIM // 2
    freqs = jnp.exp(jnp.arange(half, dtype=f32) * (-2.0 * math.log(130000.0) / HEAD_DIM))
    angles = where_at.astype(f32)[..., None] * freqs
    cosine, sine = jnp.cos(angles), jnp.sin(angles)
    return (
        jnp.concatenate([cosine, cosine, cosine, cosine], -1),
        jnp.concatenate([-sine, sine, -sine, sine], -1),
    )


def turn(values, cosine, sine):
    columns = values.shape[1]
    lane = lax.broadcasted_iota(jnp.int32, (values.shape[0], PAIR), 1)
    low = (lane % HEAD_DIM) < HEAD_DIM // 2
    parts = []
    for at in range(0, columns, PAIR):
        tile = values[:, at : at + PAIR]
        other = jnp.where(
            low,
            pltpu.roll(tile, PAIR - HEAD_DIM // 2, 1),
            pltpu.roll(tile, HEAD_DIM // 2, 1),
        )
        parts.append(tile * cosine + other * sine)
    return parts


def normalize(values):
    scale = lax.rsqrt(jnp.mean(values * values, -1, keepdims=True) + 1e-05)
    return (values * scale, scale)


def norm_back(upstream, normed, scale, weights):
    scaled = upstream * weights
    return (
        scale * (scaled - normed * jnp.mean(scaled * normed, -1, keepdims=True)),
        jnp.sum(upstream * normed, 0),
    )


def dot(one, two, dims=((1,), (0,))):
    return lax.dot_general(one, two, (dims, ((), ())), preferred_element_type=f32)


ROWS = ((1,), (1,))
OVER = ((0,), (0,))


def project_kernel(x_ref, w_ref, cos_ref, sin_ref, out_ref):
    columns = out_ref.shape[1] // 3
    x = x_ref[...]
    for j in range(3):
        made = dot(x, w_ref[:, j * columns : (j + 1) * columns])
        if j < 2:
            for at, part in enumerate(turn(made, cos_ref[...], sin_ref[...])):
                start = j * columns + at * PAIR
                out_ref[:, start : start + PAIR] = part.astype(bf16)
        else:
            out_ref[:, j * columns :] = made.astype(bf16)


def project(act, weight, cosine, sine):
    rows, width = act.shape
    columns = weight.shape[1]
    return pl.pallas_call(
        project_kernel,
        grid=(rows // BLOCK,),
        in_specs=[
            pl.BlockSpec((BLOCK, width), lambda i: (i, 0)),
            pl.BlockSpec((width, columns), lambda i: (0, 0)),
            pl.BlockSpec((BLOCK, PAIR), lambda i: (i, 0)),
            pl.BlockSpec((BLOCK, PAIR), lambda i: (i, 0)),
        ],
        out_specs=pl.BlockSpec((BLOCK, columns), lambda i: (i, 0)),
        out_shape=jax.ShapeDtypeStruct((rows, columns), bf16),
        compiler_params=pltpu.CompilerParams(vmem_limit_bytes=VMEM),
        cost_estimate=pl.CostEstimate(
            flops=2 * rows * width * columns,
            bytes_accessed=2 * (rows * width + width * columns + rows * columns),
            transcendentals=0,
        ),
        name="project_rope",
    )(act, weight, cosine, sine)


def head_halves(pair):
    first = lax.broadcasted_iota(jnp.int32, pair.shape, 1) < HEAD_DIM
    zero = jnp.zeros_like(pair)
    return jnp.where(first, pair, zero), jnp.where(first, zero, pair)


def masked(scores, seg_k, seg_q, offset):
    key = lax.broadcasted_iota(jnp.int32, scores.shape, 0)
    query = lax.broadcasted_iota(jnp.int32, scores.shape, 1)
    seen = (key - query <= offset) & (seg_k == seg_q)
    return jnp.where(seen, scores, HIDDEN)


def attend_kernel(
    blocks_before, low_ref, q_ref, kv_ref, seg_k_ref, seg_q_ref, out_ref, lse_ref, scores, v_turned
):
    i = pl.program_id(0)
    columns = q_ref.shape[1]
    low = low_ref[i]
    high = blocks_before + i + 1

    @pl.when(i == 0)
    def _():
        for at in range(0, columns, PAIR):
            v_turned[at : at + PAIR, :] = kv_ref[:, columns + at : columns + at + PAIR].T

    seg_q = seg_q_ref[...]
    for pair in range(columns // PAIR):
        at = pair * PAIR
        queries = head_halves(q_ref[:, at : at + PAIR])

        def score(j, tops):
            rows = pl.ds(pl.multiple_of(j * BLOCK, BLOCK), BLOCK)
            keys = kv_ref[rows, at : at + PAIR]
            seg_k = seg_k_ref[rows, :]
            new = []
            for h in range(2):
                raw = dot(keys, queries[h], ROWS) * 0.125
                raw = masked(raw, seg_k, seg_q, (blocks_before + i - j) * BLOCK)
                scores[h, rows, :] = raw
                new.append(jnp.maximum(tops[h], jnp.max(raw, 0, keepdims=True)))
            return tuple(new)

        start = jnp.full((1, BLOCK), HIDDEN, f32)
        tops = lax.fori_loop(low, high, score, (start, start))

        def weigh(j, totals):
            rows = pl.ds(pl.multiple_of(j * BLOCK, BLOCK), BLOCK)
            new = []
            for h in range(2):
                power = jnp.exp(scores[h, rows, :] - tops[h])
                scores[h, rows, :] = power
                new.append(totals[h] + jnp.sum(power, 0, keepdims=True))
            return tuple(new)

        start = jnp.zeros((1, BLOCK), f32)
        totals = lax.fori_loop(low, high, weigh, (start, start))
        shares = tuple(1.0 / total for total in totals)

        def mix(j, sums):
            rows = pl.ds(pl.multiple_of(j * BLOCK, BLOCK), BLOCK)
            new = []
            for h in range(2):
                probs = (scores[h, rows, :] * shares[h]).astype(bf16)
                values = v_turned[at + h * HEAD_DIM : at + (h + 1) * HEAD_DIM, rows]
                new.append(sums[h] + dot(values, probs))
            return tuple(new)

        start = jnp.zeros((HEAD_DIM, BLOCK), f32)
        sums = lax.fori_loop(low, high, mix, (start, start))
        out_ref[:, at : at + PAIR] = jnp.concatenate(sums, 0).T.astype(bf16)
        for h in range(2):
            lse_ref[2 * pair + h : 2 * pair + h + 1, :] = tops[h] + jnp.log(totals[h])


def attend(low, query, kv_all, seg_col, seg_row):
    rows, columns = query.shape
    keys = kv_all.shape[0]
    heads = columns // HEAD_DIM
    whole = lambda i, low: (0, 0)
    return pl.pallas_call(
        functools.partial(attend_kernel, (keys - rows) // BLOCK),
        grid_spec=pltpu.PrefetchScalarGridSpec(
            num_scalar_prefetch=1,
            grid=(rows // BLOCK,),
            in_specs=[
                pl.BlockSpec((BLOCK, columns), lambda i, low: (i, 0)),
                pl.BlockSpec((keys, 2 * columns), whole),
                pl.BlockSpec((keys, 1), whole),
                pl.BlockSpec((1, BLOCK), lambda i, low: (0, i)),
            ],
            out_specs=[
                pl.BlockSpec((BLOCK, columns), lambda i, low: (i, 0)),
                pl.BlockSpec((heads, BLOCK), lambda i, low: (0, i)),
            ],
            scratch_shapes=[
                pltpu.VMEM((2, keys, BLOCK), f32),
                pltpu.VMEM((columns, keys), bf16),
            ],
        ),
        out_shape=[
            jax.ShapeDtypeStruct((rows, columns), bf16),
            jax.ShapeDtypeStruct((heads, rows), f32),
        ],
        compiler_params=pltpu.CompilerParams(vmem_limit_bytes=VMEM),
        cost_estimate=pl.CostEstimate(
            flops=2 * rows * keys * columns,
            bytes_accessed=2 * (2 * rows * columns + 2 * keys * columns),
            transcendentals=rows * keys * heads // 4,
        ),
        name="attend",
    )(low, query, kv_all, seg_col, seg_row)


def attend_back_kernel(
    blocks_before,
    low_ref,
    q_ref,
    kv_ref,
    seg_k_ref,
    seg_q_ref,
    lse_ref,
    att_ref,
    datt_ref,
    cos_ref,
    sin_ref,
    dq_ref,
    dkv_ref,
    k_turned,
):
    i = pl.program_id(0)
    columns = q_ref.shape[1]
    low = low_ref[i]
    high = blocks_before + i + 1

    @pl.when(i == 0)
    def _():
        dkv_ref[...] = jnp.zeros_like(dkv_ref)
        for at in range(0, columns, PAIR):
            k_turned[at : at + PAIR, :] = kv_ref[:, at : at + PAIR].T

    seg_q = seg_q_ref[...]
    for pair in range(columns // PAIR):
        at = pair * PAIR
        queries = head_halves(q_ref[:, at : at + PAIR])
        upstream16 = datt_ref[:, at : at + PAIR]
        upstream = head_halves(upstream16)
        both = (upstream16.astype(f32) * att_ref[:, at : at + PAIR].astype(f32)).T
        delta = [
            jnp.sum(both[h * HEAD_DIM : (h + 1) * HEAD_DIM], 0, keepdims=True) for h in range(2)
        ]
        lse = [lse_ref[2 * pair + h : 2 * pair + h + 1, :] for h in range(2)]

        def step(j, sums):
            rows = pl.ds(pl.multiple_of(j * BLOCK, BLOCK), BLOCK)
            keys = kv_ref[rows, at : at + PAIR]
            values = kv_ref[rows, columns + at : columns + at + PAIR]
            seg_k = seg_k_ref[rows, :]
            new = []
            dkey = jnp.zeros((BLOCK, PAIR), f32)
            dvalue = jnp.zeros((BLOCK, PAIR), f32)
            for h in range(2):
                raw = dot(keys, queries[h], ROWS) * 0.125
                raw = masked(raw, seg_k, seg_q, (blocks_before + i - j) * BLOCK)
                probs = jnp.exp(raw - lse[h])
                dprobs = dot(values, upstream[h], ROWS)
                dscores = (probs * (dprobs - delta[h])).astype(bf16)
                dvalue += dot(probs.astype(bf16), upstream[h])
                dkey += dot(dscores, queries[h])
                turned = k_turned[at + h * HEAD_DIM : at + (h + 1) * HEAD_DIM, rows]
                new.append(sums[h] + dot(turned, dscores))
            dkv_ref[rows, at : at + PAIR] += 0.125 * dkey
            dkv_ref[rows, columns + at : columns + at + PAIR] += dvalue
            return tuple(new)

        start = jnp.zeros((HEAD_DIM, BLOCK), f32)
        sums = lax.fori_loop(low, high, step, (start, start))
        dquery = 0.125 * jnp.concatenate(sums, 0).T
        (turned,) = turn(dquery, cos_ref[...], -sin_ref[...])
        dq_ref[:, at : at + PAIR] = turned.astype(bf16)


def attend_back(low, query, kv_all, seg_col, seg_row, lse, attended, dattended, cosine, sine):
    rows, columns = query.shape
    keys = kv_all.shape[0]
    heads = columns // HEAD_DIM
    whole = lambda i, low: (0, 0)
    block = pl.BlockSpec((BLOCK, columns), lambda i, low: (i, 0))
    table = pl.BlockSpec((BLOCK, PAIR), lambda i, low: (i, 0))
    return pl.pallas_call(
        functools.partial(attend_back_kernel, (keys - rows) // BLOCK),
        grid_spec=pltpu.PrefetchScalarGridSpec(
            num_scalar_prefetch=1,
            grid=(rows // BLOCK,),
            in_specs=[
                block,
                pl.BlockSpec((keys, 2 * columns), whole),
                pl.BlockSpec((keys, 1), whole),
                pl.BlockSpec((1, BLOCK), lambda i, low: (0, i)),
                pl.BlockSpec((heads, BLOCK), lambda i, low: (0, i)),
                block,
                block,
                table,
                table,
            ],
            out_specs=[block, pl.BlockSpec((keys, 2 * columns), whole)],
            scratch_shapes=[pltpu.VMEM((columns, keys), bf16)],
        ),
        out_shape=[
            jax.ShapeDtypeStruct((rows, columns), bf16),
            jax.ShapeDtypeStruct((keys, 2 * columns), f32),
        ],
        compiler_params=pltpu.CompilerParams(vmem_limit_bytes=VMEM),
        cost_estimate=pl.CostEstimate(
            flops=5 * rows * keys * columns,
            bytes_accessed=2 * (4 * rows * columns + 2 * keys * columns) + 8 * keys * columns,
            transcendentals=rows * keys * heads // 4,
        ),
        name="attend_back",
    )(low, query, kv_all, seg_col, seg_row, lse, attended, dattended, cosine, sine)


def join_kernel(dq_ref, own_ref, got_ref, cos_ref, sin_ref, out_ref):
    columns = dq_ref.shape[1]
    out_ref[:, :columns] = dq_ref[...]
    total = own_ref[...] + got_ref[...]
    for at, part in enumerate(turn(total[:, :columns], cos_ref[...], -sin_ref[...])):
        start = columns + at * PAIR
        out_ref[:, start : start + PAIR] = part.astype(bf16)
    out_ref[:, 2 * columns :] = total[:, columns:].astype(bf16)


def join(dquery, dkv_all, got, cosine, sine):
    rows, columns = dquery.shape
    before = (dkv_all.shape[0] - rows) // BLOCK
    return pl.pallas_call(
        join_kernel,
        grid=(rows // BLOCK,),
        in_specs=[
            pl.BlockSpec((BLOCK, columns), lambda i: (i, 0)),
            pl.BlockSpec((BLOCK, 2 * columns), lambda i: (before + i, 0)),
            pl.BlockSpec((BLOCK, 2 * columns), lambda i: (i, 0)),
            pl.BlockSpec((BLOCK, PAIR), lambda i: (i, 0)),
            pl.BlockSpec((BLOCK, PAIR), lambda i: (i, 0)),
        ],
        out_specs=pl.BlockSpec((BLOCK, 3 * columns), lambda i: (i, 0)),
        out_shape=jax.ShapeDtypeStruct((rows, 3 * columns), bf16),
        compiler_params=pltpu.CompilerParams(vmem_limit_bytes=VMEM),
        cost_estimate=pl.CostEstimate(
            flops=10 * rows * columns, bytes_accessed=24 * rows * columns, transcendentals=0
        ),
        name="join_dproj",
    )(dquery, dkv_all, got, cosine, sine)


def adamw(weight, gradient, moment, square, step_size):
    moment_new = beta_one * moment + (1.0 - beta_one) * gradient
    square_new = beta_two * square + (1.0 - beta_two) * gradient * gradient
    moment_hat = moment_new / (1.0 - beta_one**STEP)
    square_hat = square_new / (1.0 - beta_two**STEP)
    weight_new = weight - step_size * (
        moment_hat / (jnp.sqrt(square_hat) + adam_eps) + decay_rate * weight
    )
    return (weight_new, moment_new, square_new)


def adam_kernel(step_size, g_ref, w_ref, m_ref, s_ref, go_ref, wo_ref, mo_ref, so_ref):
    gradient = g_ref[...].astype(f32)
    weight, moment, square = adamw(w_ref[0], gradient, m_ref[0], s_ref[0], step_size)
    go_ref[0] = gradient
    wo_ref[0] = weight
    mo_ref[0] = moment
    so_ref[0] = square


def adam(gradient, weight, moment, square, step_size):
    flat = weight.ndim == 2
    if flat:
        weight, moment, square = weight[None], moment[None], square[None]
    count, rows, columns = weight.shape
    tall = min(rows, max(16, 131072 // columns))
    block = pl.BlockSpec((1, tall, columns), lambda j, i: (j, i, 0))
    made = pl.pallas_call(
        functools.partial(adam_kernel, step_size),
        grid=(count, rows // tall),
        in_specs=[pl.BlockSpec((tall, columns), lambda j, i: (i, j)), block, block, block],
        out_specs=[block] * 4,
        out_shape=[jax.ShapeDtypeStruct(weight.shape, f32)] * 4,
        compiler_params=pltpu.CompilerParams(vmem_limit_bytes=VMEM),
        cost_estimate=pl.CostEstimate(
            flops=15 * weight.size, bytes_accessed=30 * weight.size, transcendentals=weight.size
        ),
        name="adamw",
    )(gradient, weight, moment, square)
    return [one[0] for one in made] if flat else made


def side_by_side(weight):
    return jnp.concatenate([weight[j].astype(bf16) for j in range(weight.shape[0])], 1)


def local(
    block_input,
    segment_ids,
    positions,
    out_cotangent,
    norm_gains,
    qkv_weight,
    outproj_weight,
    gateup_weight,
    down_weight,
    moment_norm,
    moment_qkv,
    moment_outproj,
    moment_gateup,
    moment_down,
    square_norm,
    square_qkv,
    square_outproj,
    square_gateup,
    square_down,
):
    seqs_here, tok_here, width = block_input.shape
    assert seqs_here == 1 and tok_here % BLOCK == 0 and lax.axis_size("ctx") == 2
    ranks = lax.axis_size("tp")
    assert ranks & (ranks - 1) == 0
    rank = lax.axis_index("tp")
    half = lax.axis_index("ctx")
    rows_all = tok_here
    share = rows_all // ranks
    rows_axes = ("fsdp", "ctx")

    def part(values, k):
        return lax.dynamic_slice_in_dim(values, (rank ^ k) * share, share, 0)

    def swap(values, k):
        return lax.ppermute(values, "tp", [(i, i ^ k) for i in range(ranks)])

    order = sorted(range(1, ranks), key=lambda k: -bin(k).count("1"))

    def gather(own):
        got = {k: swap(own, k) for k in order}
        return [own] + [got[k] for k in range(1, ranks)]

    def natural(shares):
        whole = jnp.zeros((rows_all,) + shares[0].shape[1:], shares[0].dtype)
        for k, one in enumerate(shares):
            whole = lax.dynamic_update_slice_in_dim(whole, one, (rank ^ k) * share, 0)
        return whole

    def scatter(partials):
        got = {k: swap(partials[k], k) for k in order}
        total = partials[0].astype(f32)
        for k in order:
            total = total + got[k].astype(f32)
        return total

    qkv16 = lax.all_gather(side_by_side(qkv_weight), rows_axes, axis=0, tiled=True)
    outproj16 = lax.all_gather(outproj_weight.astype(bf16), rows_axes, axis=0, tiled=True)
    gateup16 = lax.all_gather(side_by_side(gateup_weight), rows_axes, axis=0, tiled=True)
    down16 = lax.all_gather(down_weight.astype(bf16), rows_axes, axis=0, tiled=True)
    gains16 = lax.all_gather(norm_gains.astype(bf16), rows_axes, axis=1, tiled=True)
    gain_attn = gains16[0].astype(f32)
    gain_mlp = gains16[1].astype(f32)
    columns = outproj16.shape[1]

    seg_own = segment_ids.reshape(rows_all)
    seg_prev = lax.ppermute(seg_own, "ctx", [(0, 1)])
    seg_prev = jnp.where(half == 0, -1, seg_prev)
    seg_all = jnp.concatenate([seg_prev, seg_own])
    last_of_keys = seg_all.reshape(-1, BLOCK)[:, -1]
    first_of_queries = seg_own.reshape(-1, BLOCK)[:, 0]
    low = jnp.sum(
        (last_of_keys[None, :] < first_of_queries[:, None]).astype(jnp.int32), 1, dtype=jnp.int32
    )
    seg_col = seg_all[:, None]
    seg_row = seg_own[None, :]
    cosine, sine = rope_tables(positions.reshape(rows_all))

    tokens16 = block_input.reshape(rows_all, width)
    cotan16 = out_cotangent.reshape(rows_all, width)
    normed_one, _ = normalize(tokens16.astype(f32))
    act_one = (normed_one * gain_attn).astype(bf16)
    projected = project(act_one, qkv16, cosine, sine)
    query16 = projected[:, :columns]
    kv_own = projected[:, columns:]
    kv_prev = lax.ppermute(kv_own, "ctx", [(0, 1)])
    kv_all = jnp.concatenate([kv_prev, kv_own], 0)
    attended16, lse = attend(low, query16, kv_all, seg_col, seg_row)
    attn_parts = [
        dot(part(attended16, k), outproj16, ROWS).astype(bf16) for k in range(ranks)
    ]
    own_tokens = part(tokens16, 0).astype(f32)
    resid = own_tokens + scatter(attn_parts)

    normed_two, scale_two = normalize(resid)
    act_two = jnp.concatenate(gather((normed_two * gain_mlp).astype(bf16)), 0)
    cotan_mixed = jnp.concatenate([part(cotan16, k) for k in range(ranks)], 0)
    gate_up = dot(act_two, gateup16)
    hidden = down16.shape[1]
    gate_pre = gate_up[:, :hidden]
    up_pre = gate_up[:, hidden:]
    sigma = jax.nn.sigmoid(gate_pre)
    inner16 = (gate_pre * sigma * up_pre).astype(bf16)
    down_local = dot(cotan_mixed, inner16, OVER).astype(bf16)
    down_grad = lax.psum_scatter(down_local, rows_axes, scatter_dimension=0, tiled=True)
    dinner = dot(cotan_mixed, down16)
    dgate16 = (dinner * up_pre * sigma * (1.0 + gate_pre * (1.0 - sigma))).astype(bf16)
    dup16 = (dinner * gate_pre * sigma).astype(bf16)
    dgateup16 = jnp.concatenate([dgate16, dup16], 1)
    gateup_local = dot(act_two, dgateup16, OVER).astype(bf16)
    gateup_grad = lax.psum_scatter(gateup_local, rows_axes, scatter_dimension=0, tiled=True)

    def by_share(values):
        return [values[k * share : (k + 1) * share] for k in range(ranks)]

    dact_partial = dot(dgateup16, gateup16, ROWS).astype(bf16)
    dact_two = scatter(by_share(dact_partial))
    dnorm_two, gain_two = norm_back(dact_two, normed_two, scale_two, gain_mlp)
    dresid = part(cotan16, 0).astype(f32) + dnorm_two
    dresid16 = natural(gather(dresid.astype(bf16)))

    dattended16 = dot(dresid16, outproj16).astype(bf16)
    outproj_local = dot(dresid16, attended16, OVER).astype(bf16)
    outproj_grad = lax.psum_scatter(outproj_local, rows_axes, scatter_dimension=0, tiled=True)
    dquery16, dkv_all = attend_back(
        low, query16, kv_all, seg_col, seg_row, lse, attended16, dattended16, cosine, sine
    )
    dkv_got = lax.ppermute(dkv_all[:rows_all], "ctx", [(1, 0)])
    dproj16 = join(dquery16, dkv_all, dkv_got, cosine, sine)
    qkv_local = dot(act_one, dproj16, OVER).astype(bf16)
    qkv_grad = lax.psum_scatter(qkv_local, rows_axes, scatter_dimension=0, tiled=True)
    dact_one = scatter(by_share_natural(dot(dproj16, qkv16, ROWS).astype(bf16), part, ranks))
    normed_own, scale_own = normalize(own_tokens)
    dnorm_one, gain_one = norm_back(dact_one, normed_own, scale_own, gain_attn)
    input_grad = natural(gather((dresid + dnorm_one).astype(bf16)))

    mlp_partial = dot(inner16, down16, ROWS).astype(bf16)
    out_share = resid + scatter(by_share(mlp_partial))
    block_out = natural(gather(out_share.astype(bf16)))

    gains_all = lax.psum(jnp.stack([gain_one, gain_two]), ("fsdp", "ctx", "tp"))
    wide = norm_gains.shape[1]
    place = (lax.axis_index("fsdp") * lax.axis_size("ctx") + half) * wide
    norm_grad = lax.dynamic_slice_in_dim(gains_all, place, wide, 1)

    new_norm, new_moment_norm, new_square_norm = adamw(
        norm_gains, norm_grad, moment_norm, square_norm, 0.4
    )
    down_grad, new_down, new_moment_down, new_square_down = adam(
        down_grad, down_weight, moment_down, square_down, 0.4 / math.sqrt(FF)
    )
    gateup_grad, new_gateup, new_moment_gateup, new_square_gateup = adam(
        gateup_grad, gateup_weight, moment_gateup, square_gateup, 0.4 / math.sqrt(D)
    )
    outproj_grad, new_outproj, new_moment_outproj, new_square_outproj = adam(
        outproj_grad, outproj_weight, moment_outproj, square_outproj, 0.4 / math.sqrt(D // 64)
    )
    qkv_grad, new_qkv, new_moment_qkv, new_square_qkv = adam(
        qkv_grad, qkv_weight, moment_qkv, square_qkv, 0.4 / math.sqrt(D)
    )
    return (
        block_out.reshape(block_input.shape),
        input_grad.reshape(block_input.shape),
        norm_grad,
        qkv_grad,
        outproj_grad,
        gateup_grad,
        down_grad,
        new_norm,
        new_qkv,
        new_outproj,
        new_gateup,
        new_down,
        new_moment_norm,
        new_moment_qkv,
        new_moment_outproj,
        new_moment_gateup,
        new_moment_down,
        new_square_norm,
        new_square_qkv,
        new_square_outproj,
        new_square_gateup,
        new_square_down,
    )


def by_share_natural(values, part, ranks):
    return [part(values, k) for k in range(ranks)]


def solution(mesh):
    tokens = P("fsdp", "ctx", None)
    ids = P("fsdp", "ctx")
    gains = P(None, ("fsdp", "ctx"))
    stacked = P(None, ("fsdp", "ctx"), "tp")
    single = P(("fsdp", "ctx"), "tp")
    parameters = (gains, stacked, single, stacked, single)
    return jax.shard_map(
        local,
        mesh=mesh,
        in_specs=(tokens, ids, ids, tokens) + parameters * 3,
        out_specs=(tokens, tokens) + parameters * 4,
        check_vma=False,
    )
```

time: 1910 us -> 919 us (0.48)
  waiting for transfers between devices: 1310 us -> 442 us
  matrix products: 332 us -> 161 us
  Pallas kernels: 0 us -> 102 us
  local copies, waits for them, and re-layouts: 108 us -> 37.2 us
  other arithmetic: 105 us -> 36.6 us
  blocking collectives: 25.8 us -> 85.3 us
  starting transfers between devices: 1.86 us -> 33.9 us
    reduce_scatter x9 -> x4, waiting for transfers between devices: 837 us -> 0.03 us  [the longest x1 0.01 us: local(): lax.psum_scatter(qkv_local, rows_axes, scatter_dimension=0, tiled=True)]
    all_gather x10 -> x4, waiting for transfers between devices: 460 us -> 134 us  [the longest x1 59 us: local(): lax.all_gather(down_weight.astype(bf16), rows_axes, axis=0, tiled=True)]
    ppermute x0 -> x27, waiting for transfers between devices: none -> 307 us  [the longest x24 283 us: swap(): return lax.ppermute(values, 'tp', [(i, i ^ k) for i in range(ranks)])]
    dot_general x18 -> x14, matrix products: 332 us -> 161 us  [dot(): lax.dot_general(one, two, (dims, ((), ())), preferred_element_type=f32)]
    pallas_call x0 -> x8, Pallas kernels: none -> 102 us  [the longest x4 31.7 us: adam(): pl.pallas_call(functools.partial(adam_kernel, step_size), grid=(count, ro...]
    unnamed x117 -> x59, local copies, waits for them, and re-layouts: 90.4 us -> 13.3 us
    psum x1, blocking collectives: 10.3 us -> 71.6 us  [local(): gains_all = lax.psum(jnp.stack([gain_one, gain_two]), ('fsdp', 'ctx', 'tp'))]
    ppermute x0 -> x27, starting transfers between devices: none -> 33.6 us  [the longest x24 27.2 us: swap(): return lax.ppermute(values, 'tp', [(i, i ^ k) for i in range(ranks)])]
  transfers between devices with their start and end apart: 20 -> 35, of which waited for: 15 -> 20; matrix products, arithmetic and copies ran while one was open for 16% -> 18% of each run, Pallas kernels for 0% -> 10%
where the time goes in v1:
time: 919 us; the launch traced here: 912 us
  waiting for transfers between devices  442 us (48%)
  matrix products  161 us (18%)
  Pallas kernels  102 us (11%)
  blocking collectives  85.3 us (9%)
  local copies, waits for them, and re-layouts  37.2 us (4%)
  other arithmetic  36.6 us (4%)
  starting transfers between devices  33.9 us (4%)
  between operations  14.8 us (2%)
    ppermute x24, waiting for transfers between devices, swap(): return lax.ppermute(values, 'tp', [(i, i ^ k) for i in range(ranks)])  283 us
    dot_general x14, matrix products, dot(): lax.dot_general(one, two, (dims, ((), ())), preferred_element_type=f32)  161 us
    psum x1, blocking collectives, local(): gains_all = lax.psum(jnp.stack([gain_one, gain_two]), ('fsdp', 'ctx', 'tp'))  71.6 us
    all_gather x1, waiting for transfers between devices, local(): lax.all_gather(down_weight.astype(bf16), rows_axes, axis=0, tiled=True)  59 us
    all_gather x1, waiting for transfers between devices, local(): lax.all_gather(side_by_side(qkv_weight), rows_axes, axis=0, tiled=True)  38.7 us
    all_gather x1, waiting for transfers between devices, local(): lax.all_gather(side_by_side(gateup_weight), rows_axes, axis=0, tiled=True)  36.4 us
    pallas_call x4, Pallas kernels, adam(): pl.pallas_call(functools.partial(adam_kernel, step_size), grid=(count, ro...  31.7 us
    pallas_call x1, Pallas kernels, attend_back(): pl.pallas_call(functools.partial(attend_back_kernel, (keys - rows) // BLO...  31.2 us
  transfers between devices with their start and end apart: 35, of which 20 were waited for; matrix products, arithmetic and copies ran while one was open for 18% of the time, Pallas kernels for 10%

profile of v1, /device:TPU:0, one launch (start us, length us, event | category | flops | bytes accessed | tf_op | source)
XLA Modules:
  0.0 912.1 jit_solution(9650783608831973168)
XLA Ops:
  17.0 13.7 %all_gather.15 = bf16[2,2048]{1,0:T(2,128)(2,1)S(1)} all-gather(bf16[2,256]{1,0:T(2,128)(2,1)S(1)} %convert_element_type.174), channel_id=1, replica_groups=mesh['fsdp'=4,'ctx'=2,'tp'=4] {'fsdp','ctx'}, dimensions={1}, use_global_device_ids=true | all-gather | bytes 9216 | tf_op jit(solution)/shard_map/all_gather | solution.py:476
  39.0 38.7 %all-gather.5.cloned.1.call-done.w_ref = bf16[2048,1536]{1,0:T(8,128)(2,1)} async-done(((bf16[256,1536]{1,0:T(8,128)(2,1)}), bf16[2048,1536]{1,0:T(8,128)(2,1)}) %all-gather.5.cloned.1.call-update) | async-done | bytes 6291472 | tf_op jit(solution)/shard_map/all_gather | solution.py:472
  77.7 11.4 %project_rope.1 = bf16[1024,1536]{1,0:T(8,128)(2,1)} custom-call(bf16[1024,2048]{1,0:T(8,128)(2,1)} %fusion.2.x_ref, bf16[2048,1536]{1,0:T(8,128)(2,1)} %all-gather.5.cloned.1.call-done.w_ref, f32[1024,128]{1,0:T(8,128)} %get-tuple-element.105.cos_ref, f32[1024,128]{1,0:T(8,128)} %get-tuple-element.106.sin_ref), custom_call_target="tpu_custom_call" | custom-call | flops 6442450944 | bytes 13631488 | tf_op jit(solution)/shard_map/project_rope/pallas_call | solution.py:94
  105.9 20.9 %attend.1 = (bf16[1024,512]{1,0:T(8,128)(2,1)}, f32[8,1024]{1,0:T(8,128)}) custom-call(s32[4]{0:T(128)} %convert_reduce_fusion.low_ref, bf16[1024,512]{1,0:T(8,128)(2,1)} %slice.98.q_ref, bf16[2048,1024]{1,0:T(8,128)(2,1)} %pad_maximum_fusion.3.kv_ref, s32[2048,1]{1,0:T(8,128)} %copy.50.seg_k_ref, s32[1,1024]{1,0:T(1,128)} %seg_q_ref.3), custom_call_target="tpu_custom_call" | custom-call | flops 2147483648 | bytes 6291456 | tf_op jit(solution)/shard_map/attend/pallas_call | solution.py:195
  139.0 7.4 collective-permute-done.2
  146.4 20.2 %collective-permute-done.3 = bf16[256,2048]{1,0:T(8,128)(2,1)S(1)} collective-permute-done((bf16[256,2048]{1,0:T(8,128)(2,1)}, bf16[256,2048]{1,0:T(8,128)(2,1)S(1)}, u32[]{:S(2)}, u32[]{:S(2)}) %collective-permute-start.3) | collective-permute-done | bytes 1048608 | tf_op jit(solution)/shard_map/ppermute | solution.py:451
  184.1 14.7 %collective-permute-done.5 = bf16[256,2048]{1,0:T(8,128)(2,1)S(1)} collective-permute-done((bf16[256,2048]{1,0:T(8,128)(2,1)S(1)}, bf16[256,2048]{1,0:T(8,128)(2,1)S(1)}, u32[]{:S(2)}, u32[]{:S(2)}) %collective-permute-start.5) | collective-permute-done | bytes 1048608 | tf_op jit(solution)/shard_map/ppermute | solution.py:451
  205.4 18.7 %collective-permute-done.7 = bf16[256,2048]{1,0:T(8,128)(2,1)} collective-permute-done((bf16[256,2048]{1,0:T(8,128)(2,1)S(1)}, bf16[256,2048]{1,0:T(8,128)(2,1)}, u32[]{:S(2)}, u32[]{:S(2)}) %collective-permute-start.7) | collective-permute-done | bytes 1048608 | tf_op jit(solution)/shard_map/ppermute | solution.py:451
  224.1 36.4 %all-gather.9.cloned.1.call-done = bf16[2048,4096]{1,0:T(8,128)(2,1)} async-done(((bf16[256,4096]{1,0:T(8,128)(2,1)}), bf16[2048,4096]{1,0:T(8,128)(2,1)}) %all-gather.9.cloned.1.call-update) | async-done | bytes 16777232 | tf_op jit(solution)/shard_map/all_gather | solution.py:474
  260.5 23.4 %fusion.20 = f32[1024,4096]{1,0:T(8,128)} fusion(bf16[2048,4096]{1,0:T(8,128)(2,1)} %all-gather.9.cloned.1.call-done, bf16[256,2048]{1,0:T(8,128)(2,1)} %collective-permute-done.7, bf16[256,2048]{1,0:T(8,128)(2,1)} %copy-done.26, bf16[256,2048]{1,0:T(8,128)(2,1)} %copy-done.25, bf16[256,2048]{1,0:T(8,128)(2,1)} %copy-done.15), kind=kOutput, calls=%fused_computation.70 | convolution fusion | flops 17196646400 | bytes 37748736 | tf_op jit(solution)/shard_map/dot_general | solution.py:71
  283.9 59.0 %all-gather.11.cloned.1.call-done = bf16[2048,2048]{1,0:T(8,128)(2,1)} async-done(((bf16[256,2048]{1,0:T(8,128)(2,1)}), bf16[2048,2048]{1,0:T(8,128)(2,1)}) %all-gather.11.cloned.1.call-update) | async-done | bytes 8388624 | tf_op jit(solution)/shard_map/all_gather | solution.py:475
  342.8 22.4 %multiply_convert_fusion.1 = (bf16[1024,2048]{1,0:T(8,128)(2,1)}, bf16[1024,2048]{1,0:T(8,128)(2,1)}, bf16[1024,2048]{1,0:T(8,128)(2,1)}) fusion(f32[1024,4096]{1,0:T(8,128)} %fusion.20, bf16[2048,2048]{1,0:T(8,128)(2,1)} %all-gather.11.cloned.1.call-done, bf16[256,2048]{1,0:T(8,128)(2,1)} %get-tuple-element.88, bf16[256,2048]{1,0:T(8,128)(2,1)} %get-tuple-element.89, ...), kind=kOutput, calls=%fused_computation.8 | convolution fusion | flops 8640266240 | bytes 41943040 | tf_op jit(solution)/shard_map/dot_general | solution.py:71
  365.3 23.0 %fusion.4 = bf16[1024,2048]{1,0:T(8,128)(2,1)S(1)} fusion(bf16[2048,4096]{1,0:T(8,128)(2,1)} %all-gather.9.cloned.1.call-done, bf16[1024,2048]{1,0:T(8,128)(2,1)} %get-tuple-element.78, bf16[1024,2048]{1,0:T(8,128)(2,1)} %get-tuple-element.77), kind=kOutput, calls=%fused_computation.17 | convolution fusion | flops 17198743552 | bytes 29360128 | tf_op jit(solution)/shard_map/dot_general | solution.py:71
  392.2 23.4 %collective-permute-done.14 = bf16[256,2048]{1,0:T(8,128)(2,1)S(1)} collective-permute-done((bf16[256,2048]{1,0:T(8,128)(2,1)S(1)}, bf16[256,2048]{1,0:T(8,128)(2,1)S(1)}, u32[]{:S(2)}, u32[]{:S(2)}) %collective-permute-start.14) | collective-permute-done | bytes 1048608 | tf_op jit(solution)/shard_map/ppermute | solution.py:451
  415.7 21.8 %collective-permute-done.15 = bf16[256,2048]{1,0:T(8,128)(2,1)S(1)} collective-permute-done((bf16[256,2048]{1,0:T(8,128)(2,1)S(1)}, bf16[256,2048]{1,0:T(8,128)(2,1)S(1)}, u32[]{:S(2)}, u32[]{:S(2)}) %collective-permute-start.15) | collective-permute-done | bytes 1048608 | tf_op jit(solution)/shard_map/ppermute | solution.py:451
  445.3 22.5 %collective-permute-done.17 = bf16[256,2048]{1,0:T(8,128)(2,1)S(1)} collective-permute-done((bf16[256,2048]{1,0:T(8,128)(2,1)S(1)}, bf16[256,2048]{1,0:T(8,128)(2,1)S(1)}, u32[]{:S(2)}, u32[]{:S(2)}) %collective-permute-start.17) | collective-permute-done | bytes 1048608 | tf_op jit(solution)/shard_map/ppermute | solution.py:451
  467.9 22.5 %collective-permute-done.18 = bf16[256,2048]{1,0:T(8,128)(2,1)S(1)} collective-permute-done((bf16[256,2048]{1,0:T(8,128)(2,1)S(1)}, bf16[256,2048]{1,0:T(8,128)(2,1)S(1)}, u32[]{:S(2)}, u32[]{:S(2)}) %collective-permute-start.18) | collective-permute-done | bytes 1048608 | tf_op jit(solution)/shard_map/ppermute | solution.py:451
  496.5 13.9 %convolution_convert_fusion.1 = bf16[2048,2048]{1,0:T(8,128)(2,1)} fusion(bf16[1024,2048]{1,0:T(8,128)(2,1)} %get-tuple-element.79, bf16[256,2048]{1,0:T(8,128)(2,1)} %get-tuple-element.88, bf16[256,2048]{1,0:T(8,128)(2,1)} %get-tuple-element.89, bf16[256,2048]{1,0:T(8,128)(2,1)} %get-tuple-element.87, bf16[256,2048]{1,0:T(8,128)(2,1)S(1)} %get-tuple-element.86), kind=kOutput, calls=%fused_computation.11 | convolution fusion | flops 8610906112 | bytes 16777216 | tf_op jit(solution)/shard_map/dot_general | solution.py:71
  516.7 31.2 %attend_back.1 = (bf16[1024,512]{1,0:T(8,128)(2,1)}, f32[2048,1024]{1,0:T(8,128)}) custom-call(s32[4]{0:T(128)} %convert_reduce_fusion.low_ref, bf16[1024,512]{1,0:T(8,128)(2,1)} %slice.98.q_ref, bf16[2048,1024]{1,0:T(8,128)(2,1)} %pad_maximum_fusion.3.kv_ref, s32[2048,1]{1,0:T(8,128)} %copy.50.seg_k_ref, s32[1,1024]{1,0:T(1,128)} %seg_q_ref.3, ...), custom_call_target="tpu_custom_call" | custom-call | flops 5368709120 | bytes 16777216 | tf_op jit(solution)/shard_map/attend_back/pallas_call | solution.py:304
  551.7 24.1 %collective-permute-done.20.got_ref = f32[1024,1024]{1,0:T(8,128)S(1)} collective-permute-done((f32[1024,1024]{1,0:T(8,128)S(1)}, f32[1024,1024]{1,0:T(8,128)S(1)}, u32[]{:S(2)}, u32[]{:S(2)}) %collective-permute-start.20) | collective-permute-done | bytes 4194336 | tf_op jit(solution)/shard_map/ppermute | solution.py:543
  584.4 11.6 %convolution_convert_fusion.2 = bf16[2048,1536]{1,0:T(8,128)(2,1)} fusion(bf16[1024,2048]{1,0:T(8,128)(2,1)} %fusion.2.x_ref, bf16[1024,1536]{1,0:T(8,128)(2,1)} %join_dproj.1), kind=kOutput, calls=%fused_computation.12 | convolution fusion | flops 6445596672 | bytes 13631488 | tf_op jit(solution)/shard_map/dot_general | solution.py:71
  597.2 24.6 %convolution_convert_fusion = bf16[2048,4096]{1,0:T(8,128)(2,1)} fusion(bf16[1024,2048]{1,0:T(8,128)(2,1)} %get-tuple-element.78, bf16[1024,2048]{1,0:T(8,128)(2,1)} %get-tuple-element.77, bf16[256,2048]{1,0:T(8,128)(2,1)} %collective-permute-done.7, bf16[256,2048]{1,0:T(8,128)(2,1)} %copy-done.26, bf16[256,2048]{1,0:T(8,128)(2,1)} %copy-done.25, ...), kind=kOutput, calls=%fused_computation | convolution fusion | flops 17221812224 | bytes 29360128 | tf_op jit(solution)/shard_map/dot_general | solution.py:71
  621.8 12.6 %convolution_convert_fusion.4 = bf16[1024,2048]{1,0:T(8,128)(2,1)S(1)} fusion(bf16[1024,2048]{1,0:T(8,128)(2,1)} %get-tuple-element.79, bf16[2048,2048]{1,0:T(8,128)(2,1)} %all-gather.11.cloned.1.call-done), kind=kOutput, calls=%fused_computation.19 | convolution fusion | flops 8592031744 | bytes 16777216 | tf_op jit(solution)/shard_map/dot_general | solution.py:71
  638.2 44.2 %collective-permute-done.10 = bf16[256,2048]{1,0:T(8,128)(2,1)S(1)} collective-permute-done((bf16[256,2048]{1,0:T(8,128)(2,1)S(1)}, bf16[256,2048]{1,0:T(8,128)(2,1)S(1)}, u32[]{:S(2)}, u32[]{:S(2)}) %collective-permute-start.10) | collective-permute-done | bytes 1048608 | tf_op jit(solution)/shard_map/ppermute | solution.py:451
  689.5 7.1 convolution_convert_fusion.3
  705.9 9.0 collective-permute-done.11
  718.1 18.9 %collective-permute-done.21 = bf16[256,2048]{1,0:T(8,128)(2,1)S(1)} collective-permute-done((bf16[256,2048]{1,0:T(8,128)(2,1)}, bf16[256,2048]{1,0:T(8,128)(2,1)S(1)}, u32[]{:S(2)}, u32[]{:S(2)}) %collective-permute-start.21) | collective-permute-done | bytes 1048608 | tf_op jit(solution)/shard_map/ppermute | solution.py:451
  737.0 22.7 %collective-permute-done.22 = bf16[256,2048]{1,0:T(8,128)(2,1)S(1)} collective-permute-done((bf16[256,2048]{1,0:T(8,128)(2,1)}, bf16[256,2048]{1,0:T(8,128)(2,1)S(1)}, u32[]{:S(2)}, u32[]{:S(2)}) %collective-permute-start.22) | collective-permute-done | bytes 1048608 | tf_op jit(solution)/shard_map/ppermute | solution.py:451
  769.9 23.3 %collective-permute-done.12 = bf16[256,2048]{1,0:T(8,128)(2,1)S(1)} collective-permute-done((bf16[256,2048]{1,0:T(8,128)(2,1)}, bf16[256,2048]{1,0:T(8,128)(2,1)S(1)}, u32[]{:S(2)}, u32[]{:S(2)}) %collective-permute-start.12) | collective-permute-done | bytes 1048608 | tf_op jit(solution)/shard_map/ppermute | solution.py:451
  801.2 71.6 %psum.7 = f32[2,2048]{1,0:T(2,128)S(1)} all-reduce(f32[2,2048]{1,0:T(2,128)S(1)} %pad_maximum_fusion.16), channel_id=1, replica_groups=mesh['fsdp'=4,'ctx'=2,'tp'=4] {'fsdp','ctx','tp'}, use_global_device_ids=true, to_apply=%region_8.9 | all-reduce | flops 4096 | bytes 32768 | tf_op jit(solution)/shard_map/psum | solution.py:556
  876.5 7.4 adamw.7
  890.8 14.3 %adamw.6 = (f32[2,256,2048]{2,1,0:T(8,128)}, f32[2,256,2048]{2,1,0:T(8,128)}, f32[2,256,2048]{2,1,0:T(8,128)}, f32[2,256,2048]{2,1,0:T(8,128)}) custom-call(bf16[256,4096]{1,0:T(8,128)(2,1)} %reduce-scatter.9.cloned.1.call-done.g_ref, f32[2,256,2048]{2,1,0:T(8,128)} %w_ref.3, f32[2,256,2048]{2,1,0:T(8,128)} %m_ref.3, f32[2,256,2048]{2,1,0:T(8,128)} %s_ref.3), custom_call_target="tpu_custom_call" | custom-call | flops 15728640 | bytes 31457280 | tf_op jit(solution)/shard_map/adamw/pallas_call | solution.py:397
  (189 shorter events, 160.6 us)
Async XLA Ops:
  7.2 70.5 %all-gather.5.cloned.1.call-start = ((), (), s32[]{:S(2)}) async-start(), calls=%async_computation.4 | async-start | bytes 7077888 | tf_op jit(solution)/shard_map/all_gather | solution.py:472
  9.8 117.0 %all-gather.7.cloned.1.call-start = ((), (), s32[]{:S(2)}) async-start(), calls=%async_computation.5 | async-start | bytes 2359296 | tf_op jit(solution)/shard_map/all_gather | solution.py:473
  10.6 249.8 %all-gather.9.cloned.1.call-start = ((), (), s32[]{:S(2)}) async-start(), calls=%async_computation.6 | async-start | bytes 18874368 | tf_op jit(solution)/shard_map/all_gather | solution.py:474
  14.9 327.9 %all-gather.11.cloned.1.call-start = ((), (), s32[]{:S(2)}) async-start(), calls=%async_computation.7 | async-start | bytes 9437184 | tf_op jit(solution)/shard_map/all_gather | solution.py:475
  16.9 780.1 %reduce-scatter.7.cloned.1.call-start = ((), (), s32[]{:S(2)}) async-start(), calls=%async_computation.9 | async-start | bytes 2359296 | tf_op jit(solution)/shard_map/reduce_scatter | solution.py:539
  136.2 30.4 %collective-permute-start.3 = (bf16[256,2048]{1,0:T(8,128)(2,1)}, bf16[256,2048]{1,0:T(8,128)(2,1)S(1)}, u32[]{:S(2)}, u32[]{:S(2)}) collective-permute-start(bf16[256,2048]{1,0:T(8,128)(2,1)} %convolution_convert_fusion.7), channel_id=1, source_target_pairs={{0,1},{1,0},{2,3},{3,2},{4,5},{5,4},{6,7},{7,6},{8,9},{9,8},{10,11... | collective-permute-start | bytes 3145736 | tf_op jit(solution)/shard_map/ppermute | solution.py:451
  138.4 36.0 %collective-permute-start.4 = (bf16[256,2048]{1,0:T(8,128)(2,1)}, bf16[256,2048]{1,0:T(8,128)(2,1)}, u32[]{:S(2)}, u32[]{:S(2)}) collective-permute-start(bf16[256,2048]{1,0:T(8,128)(2,1)} %convolution_convert_fusion.6), channel_id=1, source_target_pairs={{0,2},{1,3},{2,0},{3,1},{4,6},{5,7},{6,4},{7,5},{8,10},{9,11},{10,... | collective-permute-start | bytes 3145736 | tf_op jit(solution)/shard_map/ppermute | solution.py:451
  178.6 20.1 %collective-permute-start.5 = (bf16[256,2048]{1,0:T(8,128)(2,1)S(1)}, bf16[256,2048]{1,0:T(8,128)(2,1)S(1)}, u32[]{:S(2)}, u32[]{:S(2)}) collective-permute-start(bf16[256,2048]{1,0:T(8,128)(2,1)S(1)} %multiply_convert_fusion.3), channel_id=1, source_target_pairs={{0,1},{1,0},{2,3},{3,2},{4,5},{5,4},{6,7},{7,6},{8,9},{9,8},{10,11... | collective-permute-start | bytes 3145736 | tf_op jit(solution)/shard_map/ppermute | solution.py:451
  180.1 24.3 %collective-permute-start.6 = (bf16[256,2048]{1,0:T(8,128)(2,1)S(1)}, bf16[256,2048]{1,0:T(8,128)(2,1)S(1)}, u32[]{:S(2)}, u32[]{:S(2)}) collective-permute-start(bf16[256,2048]{1,0:T(8,128)(2,1)S(1)} %multiply_convert_fusion.3), channel_id=1, source_target_pairs={{0,2},{1,3},{2,0},{3,1},{4,6},{5,7},{6,4},{7,5},{8,10},{9,11},{10,... | collective-permute-start | bytes 3145736 | tf_op jit(solution)/shard_map/ppermute | solution.py:451
  182.1 42.0 %collective-permute-start.7 = (bf16[256,2048]{1,0:T(8,128)(2,1)S(1)}, bf16[256,2048]{1,0:T(8,128)(2,1)}, u32[]{:S(2)}, u32[]{:S(2)}) collective-permute-start(bf16[256,2048]{1,0:T(8,128)(2,1)S(1)} %multiply_convert_fusion.3), channel_id=1, source_target_pairs={{0,3},{1,2},{2,1},{3,0},{4,7},{5,6},{6,5},{7,4},{8,11},{9,10},{10,... | collective-permute-start | bytes 3145736 | tf_op jit(solution)/shard_map/ppermute | solution.py:451
  388.7 27.0 %collective-permute-start.14 = (bf16[256,2048]{1,0:T(8,128)(2,1)S(1)}, bf16[256,2048]{1,0:T(8,128)(2,1)S(1)}, u32[]{:S(2)}, u32[]{:S(2)}) collective-permute-start(bf16[256,2048]{1,0:T(8,128)(2,1)S(1)} %get-tuple-element.83), channel_id=1, source_target_pairs={{0,3},{1,2},{2,1},{3,0},{4,7},{5,6},{6,5},{7,4},{8,11},{9,10},{10,... | collective-permute-start | bytes 3145736 | tf_op jit(solution)/shard_map/ppermute | solution.py:451
  391.2 46.4 %collective-permute-start.15 = (bf16[256,2048]{1,0:T(8,128)(2,1)S(1)}, bf16[256,2048]{1,0:T(8,128)(2,1)S(1)}, u32[]{:S(2)}, u32[]{:S(2)}) collective-permute-start(bf16[256,2048]{1,0:T(8,128)(2,1)S(1)} %get-tuple-element.85), channel_id=1, source_target_pairs={{0,1},{1,0},{2,3},{3,2},{4,5},{5,4},{6,7},{7,6},{8,9},{9,8},{10,11... | collective-permute-start | bytes 3145736 | tf_op jit(solution)/shard_map/ppermute | solution.py:451
  391.7 45.8 %collective-permute-start.16 = (bf16[256,2048]{1,0:T(8,128)(2,1)S(1)}, bf16[256,2048]{1,0:T(8,128)(2,1)S(1)}, u32[]{:S(2)}, u32[]{:S(2)}) collective-permute-start(bf16[256,2048]{1,0:T(8,128)(2,1)S(1)} %get-tuple-element.84), channel_id=1, source_target_pairs={{0,2},{1,3},{2,0},{3,1},{4,6},{5,7},{6,4},{7,5},{8,10},{9,11},{10,... | collective-permute-start | bytes 3145736 | tf_op jit(solution)/shard_map/ppermute | solution.py:451
  441.8 26.0 %collective-permute-start.17 = (bf16[256,2048]{1,0:T(8,128)(2,1)S(1)}, bf16[256,2048]{1,0:T(8,128)(2,1)S(1)}, u32[]{:S(2)}, u32[]{:S(2)}) collective-permute-start(bf16[256,2048]{1,0:T(8,128)(2,1)S(1)} %get-tuple-element.73), channel_id=1, source_target_pairs={{0,1},{1,0},{2,3},{3,2},{4,5},{5,4},{6,7},{7,6},{8,9},{9,8},{10,11... | collective-permute-start | bytes 3145736 | tf_op jit(solution)/shard_map/ppermute | solution.py:451
  443.3 47.2 %collective-permute-start.18 = (bf16[256,2048]{1,0:T(8,128)(2,1)S(1)}, bf16[256,2048]{1,0:T(8,128)(2,1)S(1)}, u32[]{:S(2)}, u32[]{:S(2)}) collective-permute-start(bf16[256,2048]{1,0:T(8,128)(2,1)S(1)} %get-tuple-element.73), channel_id=1, source_target_pairs={{0,2},{1,3},{2,0},{3,1},{4,6},{5,7},{6,4},{7,5},{8,10},{9,11},{10,... | collective-permute-start | bytes 3145736 | tf_op jit(solution)/shard_map/ppermute | solution.py:451
  444.7 45.9 %collective-permute-start.19 = (bf16[256,2048]{1,0:T(8,128)(2,1)S(1)}, bf16[256,2048]{1,0:T(8,128)(2,1)S(1)}, u32[]{:S(2)}, u32[]{:S(2)}) collective-permute-start(bf16[256,2048]{1,0:T(8,128)(2,1)S(1)} %get-tuple-element.73), channel_id=1, source_target_pairs={{0,3},{1,2},{2,1},{3,0},{4,7},{5,6},{6,5},{7,4},{8,11},{9,10},{10,... | collective-permute-start | bytes 3145736 | tf_op jit(solution)/shard_map/ppermute | solution.py:451
  496.5 380.1 %reduce-scatter.11.cloned.1.call-start = ((), (), s32[]{:S(2)}) async-start(), calls=%async_computation.11 | async-start | bytes 9437184 | tf_op jit(solution)/shard_map/reduce_scatter | solution.py:520
  510.4 373.6 %reduce-scatter.5.cloned.1.call-start = ((), (), s32[]{:S(2)}) async-start(), calls=%async_computation.8 | async-start | bytes 7077888 | tf_op jit(solution)/shard_map/reduce_scatter | solution.py:546
  550.4 25.4 %collective-permute-start.20 = (f32[1024,1024]{1,0:T(8,128)S(1)}, f32[1024,1024]{1,0:T(8,128)S(1)}, u32[]{:S(2)}, u32[]{:S(2)}) collective-permute-start(f32[1024,1024]{1,0:T(8,128)S(1)} %slice.92), channel_id=1, source_target_pairs={{4,0},{5,1},{6,2},{7,3},{12,8},{13,9},{14,10},{15,11},{20,16},{21,... | collective-permute-start | bytes 12582920 | tf_op jit(solution)/shard_map/ppermute | solution.py:543
  596.0 294.8 %reduce-scatter.9.cloned.1.call-start = ((), (), s32[]{:S(2)}) async-start(), calls=%async_computation.10 | async-start | bytes 18874368 | tf_op jit(solution)/shard_map/reduce_scatter | solution.py:526
  634.6 47.8 %collective-permute-start.10 = (bf16[256,2048]{1,0:T(8,128)(2,1)S(1)}, bf16[256,2048]{1,0:T(8,128)(2,1)S(1)}, u32[]{:S(2)}, u32[]{:S(2)}) collective-permute-start(bf16[256,2048]{1,0:T(8,128)(2,1)S(1)} %get-tuple-element.91), channel_id=1, source_target_pairs={{0,2},{1,3},{2,0},{3,1},{4,6},{5,7},{6,4},{7,5},{8,10},{9,11},{10,... | collective-permute-start | bytes 3145736 | tf_op jit(solution)/shard_map/ppermute | solution.py:451
  634.7 47.7 %collective-permute-start.8 = (bf16[256,2048]{1,0:T(8,128)(2,1)S(1)}, bf16[256,2048]{1,0:T(8,128)(2,1)S(1)}, u32[]{:S(2)}, u32[]{:S(2)}) collective-permute-start(bf16[256,2048]{1,0:T(8,128)(2,1)S(1)} %get-tuple-element.90), channel_id=1, source_target_pairs={{0,3},{1,2},{2,1},{3,0},{4,7},{5,6},{6,5},{7,4},{8,11},{9,10},{10,... | collective-permute-start | bytes 3145736 | tf_op jit(solution)/shard_map/ppermute | solution.py:451
  637.3 46.4 %collective-permute-start.9 = (bf16[256,2048]{1,0:T(8,128)(2,1)S(1)}, bf16[256,2048]{1,0:T(8,128)(2,1)S(1)}, u32[]{:S(2)}, u32[]{:S(2)}) collective-permute-start(bf16[256,2048]{1,0:T(8,128)(2,1)S(1)} %get-tuple-element.92), channel_id=1, source_target_pairs={{0,1},{1,0},{2,3},{3,2},{4,5},{5,4},{6,7},{7,6},{8,9},{9,8},{10,11... | collective-permute-start | bytes 3145736 | tf_op jit(solution)/shard_map/ppermute | solution.py:451
  688.4 26.4 %collective-permute-start.11 = (bf16[256,2048]{1,0:T(8,128)(2,1)}, bf16[256,2048]{1,0:T(8,128)(2,1)}, u32[]{:S(2)}, u32[]{:S(2)}) collective-permute-start(bf16[256,2048]{1,0:T(8,128)(2,1)} %get-tuple-element.76), channel_id=1, source_target_pairs={{0,1},{1,0},{2,3},{3,2},{4,5},{5,4},{6,7},{7,6},{8,9},{9,8},{10,11... | collective-permute-start | bytes 3145736 | tf_op jit(solution)/shard_map/ppermute | solution.py:451
  700.5 36.5 %collective-permute-start.21 = (bf16[256,2048]{1,0:T(8,128)(2,1)}, bf16[256,2048]{1,0:T(8,128)(2,1)S(1)}, u32[]{:S(2)}, u32[]{:S(2)}) collective-permute-start(bf16[256,2048]{1,0:T(8,128)(2,1)} %get-tuple-element.80), channel_id=1, source_target_pairs={{0,3},{1,2},{2,1},{3,0},{4,7},{5,6},{6,5},{7,4},{8,11},{9,10},{10,... | collective-permute-start | bytes 3145736 | tf_op jit(solution)/shard_map/ppermute | solution.py:451
  701.2 58.5 %collective-permute-start.22 = (bf16[256,2048]{1,0:T(8,128)(2,1)}, bf16[256,2048]{1,0:T(8,128)(2,1)S(1)}, u32[]{:S(2)}, u32[]{:S(2)}) collective-permute-start(bf16[256,2048]{1,0:T(8,128)(2,1)} %get-tuple-element.82), channel_id=1, source_target_pairs={{0,1},{1,0},{2,3},{3,2},{4,5},{5,4},{6,7},{7,6},{8,9},{9,8},{10,11... | collective-permute-start | bytes 3145736 | tf_op jit(solution)/shard_map/ppermute | solution.py:451
  702.2 57.5 %collective-permute-start.23 = (bf16[256,2048]{1,0:T(8,128)(2,1)}, bf16[256,2048]{1,0:T(8,128)(2,1)S(1)}, u32[]{:S(2)}, u32[]{:S(2)}) collective-permute-start(bf16[256,2048]{1,0:T(8,128)(2,1)} %get-tuple-element.81), channel_id=1, source_target_pairs={{0,2},{1,3},{2,0},{3,1},{4,6},{5,7},{6,4},{7,5},{8,10},{9,11},{10,... | collective-permute-start | bytes 3145736 | tf_op jit(solution)/shard_map/ppermute | solution.py:451
  705.5 87.7 %collective-permute-start.12 = (bf16[256,2048]{1,0:T(8,128)(2,1)}, bf16[256,2048]{1,0:T(8,128)(2,1)S(1)}, u32[]{:S(2)}, u32[]{:S(2)}) collective-permute-start(bf16[256,2048]{1,0:T(8,128)(2,1)} %get-tuple-element.76), channel_id=1, source_target_pairs={{0,2},{1,3},{2,0},{3,1},{4,6},{5,7},{6,4},{7,5},{8,10},{9,11},{10,... | collective-permute-start | bytes 3145736 | tf_op jit(solution)/shard_map/ppermute | solution.py:451
  714.8 81.1 %collective-permute-start.13 = (bf16[256,2048]{1,0:T(8,128)(2,1)}, bf16[256,2048]{1,0:T(8,128)(2,1)S(1)}, u32[]{:S(2)}, u32[]{:S(2)}) collective-permute-start(bf16[256,2048]{1,0:T(8,128)(2,1)} %get-tuple-element.76), channel_id=1, source_target_pairs={{0,3},{1,2},{2,1},{3,0},{4,7},{5,6},{6,5},{7,4},{8,11},{9,10},{10,... | collective-permute-start | bytes 3145736 | tf_op jit(solution)/shard_map/ppermute | solution.py:451
  768.8 104.6 %collective-permute-start.24 = (bf16[256,2048]{1,0:T(8,128)(2,1)}, bf16[256,2048]{1,0:T(8,128)(2,1)S(1)}, u32[]{:S(2)}, u32[]{:S(2)}) collective-permute-start(bf16[256,2048]{1,0:T(8,128)(2,1)} %get-tuple-element.71), channel_id=1, source_target_pairs={{0,1},{1,0},{2,3},{3,2},{4,5},{5,4},{6,7},{7,6},{8,9},{9,8},{10,11... | collective-permute-start | bytes 3145736 | tf_op jit(solution)/shard_map/ppermute | solution.py:451
  794.3 80.2 %collective-permute-start.25 = (bf16[256,2048]{1,0:T(8,128)(2,1)}, bf16[256,2048]{1,0:T(8,128)(2,1)S(1)}, u32[]{:S(2)}, u32[]{:S(2)}) collective-permute-start(bf16[256,2048]{1,0:T(8,128)(2,1)} %get-tuple-element.71), channel_id=1, source_target_pairs={{0,2},{1,3},{2,0},{3,1},{4,6},{5,7},{6,4},{7,5},{8,10},{9,11},{10,... | collective-permute-start | bytes 3145736 | tf_op jit(solution)/shard_map/ppermute | solution.py:451
  800.1 75.4 %collective-permute-start.26 = (bf16[256,2048]{1,0:T(8,128)(2,1)}, bf16[256,2048]{1,0:T(8,128)(2,1)S(1)}, u32[]{:S(2)}, u32[]{:S(2)}) collective-permute-start(bf16[256,2048]{1,0:T(8,128)(2,1)} %get-tuple-element.71), channel_id=1, source_target_pairs={{0,3},{1,2},{2,1},{3,0},{4,7},{5,6},{6,5},{7,4},{8,11},{9,10},{10,... | collective-permute-start | bytes 3145736 | tf_op jit(solution)/shard_map/ppermute | solution.py:451
  (32 other events, 747.4 us)
Sparse Core Ops, SparseCore 0:
  10.3 67.4 all-gather.4
  79.9 27.7 all-gather.6
  109.9 150.5 all-gather.8
  262.5 80.2 all-gather.10
  496.6 33.3 reduce-scatter.6
  532.2 88.2 reduce-scatter.10
  622.8 68.1 reduce-scatter.4
  693.3 167.3 reduce-scatter.8

commit v2 on v1

v2 whole, which is shorter than its diff:
```python
import functools
import math

import jax
import jax.numpy as jnp
from jax import lax
from jax.experimental import pallas as pl
from jax.experimental.pallas import tpu as pltpu
from jax.sharding import PartitionSpec as P

D = 2048
HEAD_DIM = 64
FF = 8192
STEP = 10

bf16 = jnp.bfloat16
f32 = jnp.float32

beta_one = 0.9
beta_two = 0.95
adam_eps = 1e-08
decay_rate = 0.1

BLOCK = 256
PAIR = 2 * HEAD_DIM
TILE = 256
HIDDEN = -1e30
VMEM = 56 * 1024 * 1024


def rope_tables(where_at):
    half = HEAD_DIM // 2
    freqs = jnp.exp(jnp.arange(half, dtype=f32) * (-2.0 * math.log(130000.0) / HEAD_DIM))
    angles = where_at.astype(f32)[..., None] * freqs
    cosine, sine = jnp.cos(angles), jnp.sin(angles)
    return (
        jnp.concatenate([cosine, cosine, cosine, cosine], -1),
        jnp.concatenate([-sine, sine, -sine, sine], -1),
    )


def turn(values, cosine, sine):
    columns = values.shape[1]
    lane = lax.broadcasted_iota(jnp.int32, (values.shape[0], PAIR), 1)
    low = (lane % HEAD_DIM) < HEAD_DIM // 2
    parts = []
    for at in range(0, columns, PAIR):
        tile = values[:, at : at + PAIR]
        other = jnp.where(
            low,
            pltpu.roll(tile, PAIR - HEAD_DIM // 2, 1),
            pltpu.roll(tile, HEAD_DIM // 2, 1),
        )
        parts.append(tile * cosine + other * sine)
    return parts


def normalize(values):
    scale = lax.rsqrt(jnp.mean(values * values, -1, keepdims=True) + 1e-05)
    return (values * scale, scale)


def norm_back(upstream, normed, scale, weights):
    scaled = upstream * weights
    return (
        scale * (scaled - normed * jnp.mean(scaled * normed, -1, keepdims=True)),
        jnp.sum(upstream * normed, 0),
    )


def dot(one, two, dims=((1,), (0,))):
    return lax.dot_general(one, two, (dims, ((), ())), preferred_element_type=f32)


ROWS = ((1,), (1,))
OVER = ((0,), (0,))


ANYWHERE = pl.BlockSpec(memory_space=pl.ANY)


def waiting(kernel, inputs, waits):
    def run(*refs):
        kernel(*refs[:inputs], *refs[inputs + len(waits) :])

    return run


def hold_kernel(values_ref, out_ref):
    out_ref[...] = values_ref[...]


def hold(values, *waits):
    rows, columns = values.shape
    tall = min(rows, BLOCK)
    block = pl.BlockSpec((tall, columns), lambda i: (i, 0))
    return pl.pallas_call(
        waiting(hold_kernel, 1, waits),
        grid=(rows // tall,),
        in_specs=[block] + [ANYWHERE] * len(waits),
        out_specs=block,
        out_shape=jax.ShapeDtypeStruct(values.shape, values.dtype),
        compiler_params=pltpu.CompilerParams(vmem_limit_bytes=VMEM),
        cost_estimate=pl.CostEstimate(flops=0, bytes_accessed=4 * values.size, transcendentals=0),
        name="hold",
    )(values, *waits)


def project_kernel(x_ref, w_ref, cos_ref, sin_ref, q_ref, kv_ref):
    columns = q_ref.shape[1]
    x = x_ref[...]
    for j in range(3):
        made = dot(x, w_ref[:, j * columns : (j + 1) * columns])
        if j < 2:
            for at, part in enumerate(turn(made, cos_ref[...], sin_ref[...])):
                out = q_ref if j == 0 else kv_ref
                out[:, at * PAIR : (at + 1) * PAIR] = part.astype(bf16)
        else:
            kv_ref[:, columns:] = made.astype(bf16)


def project(act, weight, wide, cosine, sine, *waits):
    rows, width = act.shape
    columns = wide // 3
    return pl.pallas_call(
        waiting(project_kernel, 4, waits),
        grid=(rows // BLOCK,),
        in_specs=[
            pl.BlockSpec((BLOCK, width), lambda i: (i, 0)),
            pl.BlockSpec((width, 3 * columns), lambda i: (0, 0)),
            pl.BlockSpec((BLOCK, PAIR), lambda i: (i, 0)),
            pl.BlockSpec((BLOCK, PAIR), lambda i: (i, 0)),
        ]
        + [ANYWHERE] * len(waits),
        out_specs=[
            pl.BlockSpec((BLOCK, columns), lambda i: (i, 0)),
            pl.BlockSpec((BLOCK, 2 * columns), lambda i: (i, 0)),
        ],
        out_shape=[
            jax.ShapeDtypeStruct((rows, columns), bf16),
            jax.ShapeDtypeStruct((rows, 2 * columns), bf16),
        ],
        compiler_params=pltpu.CompilerParams(vmem_limit_bytes=VMEM),
        cost_estimate=pl.CostEstimate(
            flops=6 * rows * width * columns,
            bytes_accessed=2 * (rows * width + 3 * width * columns + 3 * rows * columns),
            transcendentals=0,
        ),
        name="project_rope",
    )(act, weight, cosine, sine, *waits)


def head_halves(pair):
    first = lax.broadcasted_iota(jnp.int32, pair.shape, 1) < HEAD_DIM
    zero = jnp.zeros_like(pair)
    return jnp.where(first, pair, zero), jnp.where(first, zero, pair)


def block_rows(j):
    return pl.ds(pl.multiple_of(j * BLOCK, BLOCK), BLOCK)


def fetch(prev_ref, own_ref, kv, arrived):
    rows = own_ref.shape[0]
    copies = [
        pltpu.make_async_copy(prev_ref, kv.at[:rows], arrived.at[0]),
        pltpu.make_async_copy(own_ref, kv.at[rows:], arrived.at[1]),
    ]
    for copy in copies:
        copy.start()
    for copy in copies:
        copy.wait()


def attend_kernel(
    low_ref,
    q_ref,
    prev_ref,
    own_ref,
    seg_k_ref,
    seg_q_ref,
    out_ref,
    lse_ref,
    scores,
    sums,
    kv,
    v_turned,
    arrived,
):
    i = pl.program_id(0)
    columns = q_ref.shape[1]
    before = own_ref.shape[0] // BLOCK
    low = low_ref[i]
    high = before + i + 1

    @pl.when(i == 0)
    def _():
        fetch(prev_ref, own_ref, kv, arrived)

        def step(j, carry):
            rows = block_rows(j)
            v_turned[:, rows] = kv[rows, columns:].T
            return carry

        lax.fori_loop(low, 2 * before, step, 0)

    key = lax.broadcasted_iota(jnp.int32, (BLOCK, BLOCK), 0)
    query = lax.broadcasted_iota(jnp.int32, (BLOCK, BLOCK), 1)
    heads = columns // HEAD_DIM

    def score(j, tops):
        rows = block_rows(j)
        seen = (key - query <= (before + i - j) * BLOCK) & (seg_k_ref[rows, :] == seg_q_ref[...])
        bias = jnp.where(seen, 0.0, HIDDEN)
        new = []
        for at in range(0, columns, PAIR):
            keys = kv[rows, at : at + PAIR]
            for one in head_halves(q_ref[:, at : at + PAIR] * 0.125):
                h = len(new)
                raw = dot(keys, one, ROWS) + bias
                scores[h, rows, :] = raw
                new.append(jnp.maximum(tops[h], jnp.max(raw, 0, keepdims=True)))
        return tuple(new)

    tops = lax.fori_loop(low, high, score, (jnp.full((1, BLOCK), HIDDEN, f32),) * heads)

    def weigh(j, totals):
        rows = block_rows(j)
        new = []
        for h in range(heads):
            power = jnp.exp(scores[h, rows, :] - tops[h])
            scores[h, rows, :] = power
            new.append(totals[h] + jnp.sum(power, 0, keepdims=True))
        return tuple(new)

    totals = lax.fori_loop(low, high, weigh, (jnp.zeros((1, BLOCK), f32),) * heads)
    shares = tuple(1.0 / total for total in totals)
    sums[...] = jnp.zeros_like(sums)

    def mix(j, carry):
        rows = block_rows(j)
        for h in range(heads):
            probs = (scores[h, rows, :] * shares[h]).astype(bf16)
            lanes = slice(h * HEAD_DIM, (h + 1) * HEAD_DIM)
            sums[lanes, :] += dot(v_turned[lanes, rows], probs)
        return carry

    lax.fori_loop(low, high, mix, 0)
    for at in range(0, columns, PAIR):
        out_ref[:, at : at + PAIR] = sums[at : at + PAIR, :].T.astype(bf16)
    for h in range(heads):
        lse_ref[h : h + 1, :] = tops[h] + jnp.log(totals[h])


def attend(low, query, kv_prev, kv_own, seg_col, seg_row):
    rows, columns = query.shape
    keys = 2 * rows
    heads = columns // HEAD_DIM
    return pl.pallas_call(
        attend_kernel,
        grid_spec=pltpu.PrefetchScalarGridSpec(
            num_scalar_prefetch=1,
            grid=(rows // BLOCK,),
            in_specs=[
                pl.BlockSpec((BLOCK, columns), lambda i, low: (i, 0)),
                pl.BlockSpec(memory_space=pl.ANY),
                pl.BlockSpec(memory_space=pl.ANY),
                pl.BlockSpec((keys, 1), lambda i, low: (0, 0)),
                pl.BlockSpec((1, BLOCK), lambda i, low: (0, i)),
            ],
            out_specs=[
                pl.BlockSpec((BLOCK, columns), lambda i, low: (i, 0)),
                pl.BlockSpec((heads, BLOCK), lambda i, low: (0, i)),
            ],
            scratch_shapes=[
                pltpu.VMEM((heads, keys, BLOCK), f32),
                pltpu.VMEM((columns, BLOCK), f32),
                pltpu.VMEM((keys, 2 * columns), bf16),
                pltpu.VMEM((columns, keys), bf16),
                pltpu.SemaphoreType.DMA((2,)),
            ],
        ),
        out_shape=[
            jax.ShapeDtypeStruct((rows, columns), bf16),
            jax.ShapeDtypeStruct((heads, rows), f32),
        ],
        compiler_params=pltpu.CompilerParams(vmem_limit_bytes=VMEM),
        cost_estimate=pl.CostEstimate(
            flops=8 * rows * keys * columns,
            bytes_accessed=2 * (2 * rows * columns + 2 * keys * columns),
            transcendentals=rows * keys * heads // 4,
        ),
        name="attend",
    )(low, query, kv_prev, kv_own, seg_col, seg_row)


def attend_back_kernel(
    low_ref,
    q_ref,
    prev_ref,
    own_ref,
    seg_k_ref,
    seg_q_ref,
    lse_ref,
    att_ref,
    datt_ref,
    cos_ref,
    sin_ref,
    dq_ref,
    dprev_ref,
    down_ref,
    sums,
    delta,
    kv,
    k_turned,
    dkv,
    arrived,
):
    i = pl.program_id(0)
    columns = q_ref.shape[1]
    before = own_ref.shape[0] // BLOCK
    low = low_ref[i]
    high = before + i + 1

    @pl.when(i == 0)
    def _():
        fetch(prev_ref, own_ref, kv, arrived)
        dkv[...] = jnp.zeros_like(dkv)

        def step(j, carry):
            rows = block_rows(j)
            k_turned[:, rows] = kv[rows, :columns].T
            return carry

        lax.fori_loop(low, 2 * before, step, 0)

    key = lax.broadcasted_iota(jnp.int32, (BLOCK, BLOCK), 0)
    query = lax.broadcasted_iota(jnp.int32, (BLOCK, BLOCK), 1)
    for at in range(0, columns, PAIR):
        both = (datt_ref[:, at : at + PAIR].astype(f32) * att_ref[:, at : at + PAIR].astype(f32)).T
        for h in range(2):
            own = both[h * HEAD_DIM : (h + 1) * HEAD_DIM]
            at_h = at // HEAD_DIM + h
            delta[at_h : at_h + 1, :] = jnp.sum(own, 0, keepdims=True)
    sums[...] = jnp.zeros_like(sums)

    def step(j, carry):
        rows = block_rows(j)
        seen = (key - query <= (before + i - j) * BLOCK) & (seg_k_ref[rows, :] == seg_q_ref[...])
        bias = jnp.where(seen, 0.0, HIDDEN)
        for at in range(0, columns, PAIR):
            keys = kv[rows, at : at + PAIR]
            values = kv[rows, columns + at : columns + at + PAIR]
            queries = head_halves(q_ref[:, at : at + PAIR] * 0.125)
            upstream = head_halves(datt_ref[:, at : at + PAIR])
            dkey = dkv[rows, at : at + PAIR]
            dvalue = dkv[rows, columns + at : columns + at + PAIR]
            for h in range(2):
                at_h = at // HEAD_DIM + h
                lanes = slice(at_h * HEAD_DIM, (at_h + 1) * HEAD_DIM)
                raw = dot(keys, queries[h], ROWS) + bias
                probs = jnp.exp(raw - lse_ref[at_h : at_h + 1, :])
                dprobs = dot(values, upstream[h], ROWS)
                dscores = (probs * (dprobs - delta[at_h : at_h + 1, :])).astype(bf16)
                dvalue += dot(probs.astype(bf16), upstream[h])
                dkey += dot(dscores, queries[h])
                sums[lanes, :] += dot(k_turned[lanes, rows], dscores)
            dkv[rows, at : at + PAIR] = dkey
            dkv[rows, columns + at : columns + at + PAIR] = dvalue
        return carry

    lax.fori_loop(low, high, step, 0)
    for at in range(0, columns, PAIR):
        dquery = 0.125 * sums[at : at + PAIR, :].T
        (turned,) = turn(dquery, cos_ref[...], -sin_ref[...])
        dq_ref[:, at : at + PAIR] = turned.astype(bf16)

    @pl.when(i == pl.num_programs(0) - 1)
    def _():
        rows = own_ref.shape[0]
        copies = [
            pltpu.make_async_copy(dkv.at[:rows], dprev_ref, arrived.at[0]),
            pltpu.make_async_copy(dkv.at[rows:], down_ref, arrived.at[1]),
        ]
        for copy in copies:
            copy.start()
        for copy in copies:
            copy.wait()


def attend_back(
    low, query, kv_prev, kv_own, seg_col, seg_row, lse, attended, dattended, cosine, sine, *waits
):
    rows, columns = query.shape
    keys = 2 * rows
    heads = columns // HEAD_DIM
    block = pl.BlockSpec((BLOCK, columns), lambda i, low: (i, 0))
    table = pl.BlockSpec((BLOCK, PAIR), lambda i, low: (i, 0))
    anywhere = pl.BlockSpec(memory_space=pl.ANY)
    return pl.pallas_call(
        waiting(attend_back_kernel, 11, waits),
        grid_spec=pltpu.PrefetchScalarGridSpec(
            num_scalar_prefetch=1,
            grid=(rows // BLOCK,),
            in_specs=[
                block,
                anywhere,
                anywhere,
                pl.BlockSpec((keys, 1), lambda i, low: (0, 0)),
                pl.BlockSpec((1, BLOCK), lambda i, low: (0, i)),
                pl.BlockSpec((heads, BLOCK), lambda i, low: (0, i)),
                block,
                block,
                table,
                table,
            ]
            + [anywhere] * len(waits),
            out_specs=[block, anywhere, anywhere],
            scratch_shapes=[
                pltpu.VMEM((columns, BLOCK), f32),
                pltpu.VMEM((heads, BLOCK), f32),
                pltpu.VMEM((keys, 2 * columns), bf16),
                pltpu.VMEM((columns, keys), bf16),
                pltpu.VMEM((keys, 2 * columns), f32),
                pltpu.SemaphoreType.DMA((2,)),
            ],
        ),
        out_shape=[
            jax.ShapeDtypeStruct((rows, columns), bf16),
            jax.ShapeDtypeStruct((rows, 2 * columns), f32),
            jax.ShapeDtypeStruct((rows, 2 * columns), f32),
        ],
        compiler_params=pltpu.CompilerParams(vmem_limit_bytes=VMEM),
        cost_estimate=pl.CostEstimate(
            flops=12 * rows * keys * columns,
            bytes_accessed=2 * (4 * rows * columns + 2 * keys * columns) + 8 * keys * columns,
            transcendentals=rows * keys * heads // 4,
        ),
        name="attend_back",
    )(low, query, kv_prev, kv_own, seg_col, seg_row, lse, attended, dattended, cosine, sine, *waits)


def join_kernel(dq_ref, own_ref, got_ref, cos_ref, sin_ref, out_ref):
    columns = dq_ref.shape[1]
    out_ref[:, :columns] = dq_ref[...]
    total = own_ref[...] + got_ref[...]
    for at, part in enumerate(turn(total[:, :columns], cos_ref[...], -sin_ref[...])):
        start = columns + at * PAIR
        out_ref[:, start : start + PAIR] = part.astype(bf16)
    out_ref[:, 2 * columns :] = total[:, columns:].astype(bf16)


def join(dquery, dkv, got, cosine, sine, *waits):
    rows, columns = dquery.shape
    return pl.pallas_call(
        waiting(join_kernel, 5, waits),
        grid=(rows // BLOCK,),
        in_specs=[
            pl.BlockSpec((BLOCK, columns), lambda i: (i, 0)),
            pl.BlockSpec((BLOCK, 2 * columns), lambda i: (i, 0)),
            pl.BlockSpec((BLOCK, 2 * columns), lambda i: (i, 0)),
            pl.BlockSpec((BLOCK, PAIR), lambda i: (i, 0)),
            pl.BlockSpec((BLOCK, PAIR), lambda i: (i, 0)),
        ]
        + [ANYWHERE] * len(waits),
        out_specs=pl.BlockSpec((BLOCK, 3 * columns), lambda i: (i, 0)),
        out_shape=jax.ShapeDtypeStruct((rows, 3 * columns), bf16),
        compiler_params=pltpu.CompilerParams(vmem_limit_bytes=VMEM),
        cost_estimate=pl.CostEstimate(
            flops=10 * rows * columns, bytes_accessed=24 * rows * columns, transcendentals=0
        ),
        name="join_dproj",
    )(dquery, dkv, got, cosine, sine, *waits)


def pack_kernel(gateup_ref, down_ref, out_ref):
    out_ref[:, :TILE] = gateup_ref[0].astype(bf16)
    out_ref[:, TILE : 2 * TILE] = gateup_ref[1].astype(bf16)
    out_ref[:, 2 * TILE :] = down_ref[...].astype(bf16)


def pack(gateup, down, first, count):
    rows = down.shape[0]
    return pl.pallas_call(
        pack_kernel,
        grid=(count,),
        in_specs=[
            pl.BlockSpec((2, rows, TILE), lambda j: (0, 0, first + j)),
            pl.BlockSpec((rows, TILE), lambda j: (0, first + j)),
        ],
        out_specs=pl.BlockSpec((rows, 3 * TILE), lambda j: (0, j)),
        out_shape=jax.ShapeDtypeStruct((rows, 3 * TILE * count), bf16),
        compiler_params=pltpu.CompilerParams(vmem_limit_bytes=VMEM // 2),
        cost_estimate=pl.CostEstimate(
            flops=0, bytes_accessed=18 * TILE * rows * count, transcendentals=0
        ),
        name="pack_weights",
    )(gateup, down)


def hidden_kernel(act_ref, cot_ref, gate_ref, up_ref, down_ref, dgu_ref, inner_ref):
    gate = dot(act_ref[...], gate_ref[...])
    up = dot(act_ref[...], up_ref[...])
    dinner = dot(cot_ref[...], down_ref[...])
    sigma = jax.nn.sigmoid(gate)
    swish = gate * sigma
    inner_ref[...] = (swish * up).astype(bf16)
    dgu_ref[:, :TILE] = (dinner * up * sigma * (1.0 + gate * (1.0 - sigma))).astype(bf16)
    dgu_ref[:, TILE:] = (dinner * swish).astype(bf16)


def packed(width, which):
    return pl.BlockSpec((width, TILE), lambda j: (0, 3 * j + which))


def hidden(act, cotan, weights, *waits):
    rows, width = act.shape
    tiles = weights.shape[1] // (3 * TILE)
    whole = pl.BlockSpec((rows, width), lambda j: (0, 0))
    return pl.pallas_call(
        waiting(hidden_kernel, 5, waits),
        grid=(tiles,),
        in_specs=[whole, whole, packed(width, 0), packed(width, 1), packed(width, 2)]
        + [ANYWHERE] * len(waits),
        out_specs=[
            pl.BlockSpec((rows, 2 * TILE), lambda j: (0, j)),
            pl.BlockSpec((rows, TILE), lambda j: (0, j)),
        ],
        out_shape=[
            jax.ShapeDtypeStruct((rows, 2 * TILE * tiles), bf16),
            jax.ShapeDtypeStruct((rows, TILE * tiles), bf16),
        ],
        compiler_params=pltpu.CompilerParams(vmem_limit_bytes=VMEM),
        cost_estimate=pl.CostEstimate(
            flops=6 * rows * width * TILE * tiles,
            bytes_accessed=4 * rows * width + 6 * (rows + width) * TILE * tiles,
            transcendentals=rows * TILE * tiles,
        ),
        name="hidden_units",
    )(act, cotan, weights, weights, weights, *waits)


def hidden_grad_kernel(act_ref, cot_ref, dgu_ref, inner_ref, out_ref):
    out_ref[:, : 2 * TILE] = dot(act_ref[...], dgu_ref[...]).astype(bf16)
    out_ref[:, 2 * TILE :] = dot(cot_ref[...], inner_ref[...]).astype(bf16)


def hidden_grad(act_turned, cot_turned, dgu, inner, *waits):
    width, rows = act_turned.shape
    tiles = inner.shape[1] // TILE
    whole = pl.BlockSpec((width, rows), lambda j: (0, 0))
    return pl.pallas_call(
        waiting(hidden_grad_kernel, 4, waits),
        grid=(tiles,),
        in_specs=[
            whole,
            whole,
            pl.BlockSpec((rows, 2 * TILE), lambda j: (0, j)),
            pl.BlockSpec((rows, TILE), lambda j: (0, j)),
        ]
        + [ANYWHERE] * len(waits),
        out_specs=pl.BlockSpec((width, 3 * TILE), lambda j: (0, j)),
        out_shape=jax.ShapeDtypeStruct((width, 3 * TILE * tiles), bf16),
        compiler_params=pltpu.CompilerParams(vmem_limit_bytes=VMEM),
        cost_estimate=pl.CostEstimate(
            flops=6 * rows * width * TILE * tiles,
            bytes_accessed=4 * rows * width + 6 * (rows + width) * TILE * tiles,
            transcendentals=0,
        ),
        name="hidden_grad",
    )(act_turned, cot_turned, dgu, inner, *waits)


def back_kernel(at, tall, values_ref, w_ref, *refs):
    made = None
    for t in range(values_ref.shape[1] // tall):
        start = 3 * TILE * t + at
        one = dot(values_ref[:, t * tall : (t + 1) * tall], w_ref[:, start : start + tall], ROWS)
        made = one if made is None else made + one
    for ref in refs[:-1]:
        made += ref[...]
    refs[-1][...] = made.astype(refs[-1].dtype)


def back(values, weights, at, tall, start, dtype, *waits):
    rows, columns = values.shape
    width = weights.shape[0]
    wide = 2 * TILE
    block = pl.BlockSpec((rows, wide), lambda j: (0, j))
    extra = [] if start is None else [start]
    return pl.pallas_call(
        waiting(functools.partial(back_kernel, at, tall), 2 + len(extra), waits),
        grid=(width // wide,),
        in_specs=[
            pl.BlockSpec((rows, columns), lambda j: (0, 0)),
            pl.BlockSpec((wide, weights.shape[1]), lambda j: (j, 0)),
        ]
        + [block] * len(extra)
        + [ANYWHERE] * len(waits),
        out_specs=block,
        out_shape=jax.ShapeDtypeStruct((rows, width), dtype),
        compiler_params=pltpu.CompilerParams(vmem_limit_bytes=VMEM),
        cost_estimate=pl.CostEstimate(
            flops=2 * rows * width * columns,
            bytes_accessed=2 * rows * (columns + 2 * width) + 2 * width * weights.shape[1],
            transcendentals=0,
        ),
        name="from_hidden",
    )(values, weights, *extra, *waits)


def adamw(weight, gradient, moment, square, step_size):
    moment_new = beta_one * moment + (1.0 - beta_one) * gradient
    square_new = beta_two * square + (1.0 - beta_two) * gradient * gradient
    moment_hat = moment_new / (1.0 - beta_one**STEP)
    square_hat = square_new / (1.0 - beta_two**STEP)
    weight_new = weight - step_size * (
        moment_hat / (jnp.sqrt(square_hat) + adam_eps) + decay_rate * weight
    )
    return (weight_new, moment_new, square_new)


def adam_kernel(step_size, g_ref, w_ref, m_ref, s_ref, go_ref, wo_ref, mo_ref, so_ref):
    gradient = g_ref[...].astype(f32)
    weight, moment, square = adamw(w_ref[0], gradient, m_ref[0], s_ref[0], step_size)
    go_ref[0] = gradient
    wo_ref[0] = weight
    mo_ref[0] = moment
    so_ref[0] = square


def adam(gradient, first, weight, moment, square, step_size, *waits):
    flat = weight.ndim == 2
    if flat:
        weight, moment, square = weight[None], moment[None], square[None]
    count, rows, columns = weight.shape
    tall = min(rows, max(16, 131072 // columns))
    block = pl.BlockSpec((1, tall, columns), lambda j, i: (j, i, 0))
    made = pl.pallas_call(
        waiting(functools.partial(adam_kernel, step_size), 4, waits),
        grid=(count, rows // tall),
        in_specs=[pl.BlockSpec((tall, columns), lambda j, i: (i, first + j)), block, block, block]
        + [ANYWHERE] * len(waits),
        out_specs=[block] * 4,
        out_shape=[jax.ShapeDtypeStruct(weight.shape, f32)] * 4,
        compiler_params=pltpu.CompilerParams(vmem_limit_bytes=VMEM),
        cost_estimate=pl.CostEstimate(
            flops=15 * weight.size, bytes_accessed=30 * weight.size, transcendentals=weight.size
        ),
        name="adamw",
    )(gradient, weight, moment, square, *waits)
    return [one[0] for one in made] if flat else made


def adam_hidden_kernel(steps, g_ref, *refs):
    gu, down, refs = refs[:3], refs[3:6], refs[6:]
    gu_out, down_out = refs[-8:-4], refs[-4:]
    gradient = g_ref[...].astype(f32)
    for n in range(2):
        own = gradient[:, n * TILE : (n + 1) * TILE]
        weight, moment, square = adamw(gu[0][n], own, gu[1][n], gu[2][n], steps[0])
        for ref, value in zip(gu_out, (own, weight, moment, square)):
            ref[n] = value
    own = gradient[:, 2 * TILE :]
    weight, moment, square = adamw(down[0][...], own, down[1][...], down[2][...], steps[1])
    for ref, value in zip(down_out, (own, weight, moment, square)):
        ref[...] = value


def adam_hidden(gradient, gateup, down, first, filled):
    rows = gradient.shape[0]
    tiles = gradient.shape[1] // (3 * TILE)
    two = pl.BlockSpec((2, rows, TILE), lambda j: (0, 0, first + j))
    one = pl.BlockSpec((rows, TILE), lambda j: (0, first + j))
    anywhere = pl.BlockSpec(memory_space=pl.ANY)
    filled = list(filled or [])
    return pl.pallas_call(
        functools.partial(adam_hidden_kernel, (0.4 / math.sqrt(D), 0.4 / math.sqrt(FF))),
        grid=(tiles,),
        in_specs=[pl.BlockSpec((rows, 3 * TILE), lambda j: (0, j))]
        + [two] * 3
        + [one] * 3
        + [anywhere] * len(filled),
        out_specs=[two] * 4 + [one] * 4,
        out_shape=[jax.ShapeDtypeStruct(gateup[0].shape, f32)] * 4
        + [jax.ShapeDtypeStruct(down[0].shape, f32)] * 4,
        input_output_aliases={7 + n: n for n in range(len(filled))},
        compiler_params=pltpu.CompilerParams(vmem_limit_bytes=VMEM),
        cost_estimate=pl.CostEstimate(
            flops=45 * rows * TILE * tiles,
            bytes_accessed=90 * rows * TILE * tiles,
            transcendentals=3 * rows * TILE * tiles,
        ),
        name="adamw_hidden",
    )(gradient, *gateup, *down, *filled)


def side_by_side(weight):
    return jnp.concatenate([weight[j].astype(bf16) for j in range(weight.shape[0])], 1)


def edges(rows, parts):
    return [rows * n // parts // 16 * 16 for n in range(parts)] + [rows]


def exchange(values, axis, bit):
    size = lax.axis_size(axis)
    return lax.ppermute(values, axis, [(i, i ^ bit) for i in range(size)])


def bits_of(axis):
    return [1 << n for n in range(lax.axis_size(axis).bit_length() - 1)]


def turns(bits):
    return [bits[n:] + bits[:n] for n in range(len(bits))]


def gather(own, arrived=None):
    bits = bits_of("tp")
    cut = edges(own.shape[0], len(bits))
    held = []
    for n, order in enumerate(turns(bits)):
        held.append(({0: own[cut[n] : cut[n + 1]]}, order))
    for step in range(len(bits)):
        for have, order in held:
            bit = order[step]
            got = {k ^ bit: exchange(v, "tp", bit) for k, v in list(have.items())}
            have.update(got)
            if arrived is not None:
                arrived.setdefault(step, []).extend(got.values())
    return [[have[k] for have, _ in held] for k in range(lax.axis_size("tp"))]


def scatter(partials, arrived=None):
    bits = bits_of("tp")
    cut = edges(partials[0].shape[0], len(bits))
    held = []
    for n, order in enumerate(turns(bits)):
        held.append((dict(enumerate(p[cut[n] : cut[n + 1]] for p in partials)), order))
    for step in range(len(bits)):
        for have, order in held:
            bit = order[step]
            for k in [k for k in have if k & bit]:
                got = exchange(have.pop(k).astype(bf16), "tp", bit)
                if arrived is not None:
                    arrived.setdefault(step, []).append(got)
                have[k ^ bit] = have[k ^ bit].astype(f32) + got.astype(f32)
    return jnp.concatenate([have[0] for have, _ in held], 0)


def to_partners(pieces):
    order = sorted(range(1, len(pieces)), key=lambda k: -bin(k).count("1"))
    got = {k: exchange(pieces[k], "tp", k) for k in order}
    return [pieces[0]] + [got[k] for k in range(1, len(pieces))]


def sum_everywhere(values):
    for axis in ("tp", "ctx", "fsdp"):
        for bit in bits_of(axis):
            values = values + exchange(values, axis, bit)
    return values


def residual_kernel(ranks, att_ref, x_ref, gain_ref, *refs):
    weights, (resid_ref, act_ref, scale_ref) = refs[:-3], refs[-3:]
    columns = att_ref.shape[1] // ranks
    parts = len(weights) // ranks
    made = []
    for n in range(parts):
        one = None
        for k in range(ranks):
            att = att_ref[:, k * columns : (k + 1) * columns]
            more = dot(att, weights[k * parts + n][...], ROWS)
            one = more if one is None else one + more
        made.append(one)
    resid = jnp.concatenate(made, 1) + x_ref[...].astype(f32)
    normed, scale = normalize(resid)
    resid_ref[...] = resid
    act_ref[...] = (normed * gain_ref[...]).astype(bf16)
    scale_ref[...] = scale


def residual(attended, tokens, gain, weights):
    rows, width = tokens.shape
    flat = [piece for pieces in weights for piece in pieces]
    return pl.pallas_call(
        functools.partial(residual_kernel, len(weights)),
        out_shape=[
            jax.ShapeDtypeStruct((rows, width), f32),
            jax.ShapeDtypeStruct((rows, width), bf16),
            jax.ShapeDtypeStruct((rows, 1), f32),
        ],
        compiler_params=pltpu.CompilerParams(vmem_limit_bytes=VMEM),
        cost_estimate=pl.CostEstimate(
            flops=2 * rows * width * width,
            bytes_accessed=2 * width * width + 12 * rows * width,
            transcendentals=0,
        ),
        name="residual",
    )(attended, tokens, gain, *flat)


def attended_back_kernel(ranks, d_ref, *refs):
    weights, outs = refs[:-ranks], refs[-ranks:]
    parts = len(weights) // ranks
    for k in range(ranks):
        one = None
        at = 0
        for n in range(parts):
            weight = weights[k * parts + n][...]
            more = dot(d_ref[:, at : at + weight.shape[0]], weight)
            at += weight.shape[0]
            one = more if one is None else one + more
        outs[k][...] = one.astype(bf16)


def attended_back(dresid, weights, *waits):
    rows, width = dresid.shape
    flat = [piece for pieces in weights for piece in pieces]
    return pl.pallas_call(
        waiting(functools.partial(attended_back_kernel, len(weights)), 1 + len(flat), waits),
        in_specs=[pl.BlockSpec(memory_space=pltpu.VMEM)] * (1 + len(flat)) + [ANYWHERE] * len(waits),
        out_shape=[jax.ShapeDtypeStruct((rows, one[0].shape[1]), bf16) for one in weights],
        compiler_params=pltpu.CompilerParams(vmem_limit_bytes=VMEM),
        cost_estimate=pl.CostEstimate(
            flops=2 * rows * width * width,
            bytes_accessed=2 * width * width + 4 * rows * width,
            transcendentals=0,
        ),
        name="attended_back",
    )(dresid, *flat, *waits)


def local(
    block_input,
    segment_ids,
    positions,
    out_cotangent,
    norm_gains,
    qkv_weight,
    outproj_weight,
    gateup_weight,
    down_weight,
    moment_norm,
    moment_qkv,
    moment_outproj,
    moment_gateup,
    moment_down,
    square_norm,
    square_qkv,
    square_outproj,
    square_gateup,
    square_down,
):
    seqs_here, tok_here, width = block_input.shape
    ranks = lax.axis_size("tp")
    assert seqs_here == 1 and tok_here % BLOCK == 0 and lax.axis_size("ctx") == 2
    assert all(lax.axis_size(axis) & (lax.axis_size(axis) - 1) == 0 for axis in ("tp", "fsdp"))
    rank = lax.axis_index("tp")
    half = lax.axis_index("ctx")
    rows_all = tok_here
    share = rows_all // ranks
    rows_axes = ("fsdp", "ctx")
    tiles = down_weight.shape[1] // TILE
    early = 5 * tiles // 8
    cuts = [(0, early), (early, tiles - early)]

    def part(values, k):
        return lax.dynamic_slice_in_dim(values, (rank ^ k) * share, share, 0)

    def mixed(values):
        return jnp.concatenate([part(values, k) for k in range(ranks)], 0)

    def natural(shares):
        first = shares[0][0]
        whole = jnp.zeros((rows_all,) + first.shape[1:], first.dtype)
        for k, pieces in enumerate(shares):
            at = (rank ^ k) * share
            for piece in pieces:
                whole = lax.dynamic_update_slice_in_dim(whole, piece, at, 0)
                at = at + piece.shape[0]
        return whole

    def flat(shares):
        return jnp.concatenate([piece for pieces in shares for piece in pieces], 0)

    def by_share(values):
        return [values[k * share : (k + 1) * share] for k in range(ranks)]

    attn16 = jnp.concatenate([side_by_side(qkv_weight), outproj_weight.astype(bf16)], 1)
    attn16 = lax.all_gather(attn16, rows_axes, axis=0, tiled=True)
    mlp16 = [
        lax.all_gather(
            pack(gateup_weight, down_weight, first, count), rows_axes, axis=0, tiled=True
        )
        for first, count in cuts
    ]
    gains16 = lax.all_gather(norm_gains.astype(bf16), rows_axes, axis=1, tiled=True)
    gain_attn = gains16[0].astype(f32)
    gain_mlp = gains16[1].astype(f32)
    columns = outproj_weight.shape[1]
    outproj_all = gather(attn16[:, 3 * columns :])

    seg_own = segment_ids.reshape(rows_all)
    seg_prev = lax.ppermute(seg_own, "ctx", [(0, 1)])
    seg_prev = jnp.where(half == 0, -1, seg_prev)
    seg_all = jnp.concatenate([seg_prev, seg_own])
    last_of_keys = seg_all.reshape(-1, BLOCK)[:, -1]
    first_of_queries = seg_own.reshape(-1, BLOCK)[:, 0]
    low = jnp.sum(
        (last_of_keys[None, :] < first_of_queries[:, None]).astype(jnp.int32), 1, dtype=jnp.int32
    )
    seg_col = seg_all[:, None]
    seg_row = seg_own[None, :]
    cosine, sine = rope_tables(positions.reshape(rows_all))

    tokens16 = block_input.reshape(rows_all, width)
    cotan16 = out_cotangent.reshape(rows_all, width)
    cotan_mixed = mixed(cotan16)
    cotan_turned = cotan_mixed.T
    normed_one, _ = normalize(tokens16.astype(f32))
    act_one = (normed_one * gain_attn).astype(bf16)
    query16, kv_own = project(act_one, attn16, 3 * columns, cosine, sine, cotan_turned)
    kv_prev = lax.ppermute(kv_own, "ctx", [(0, 1)])
    attended16, lse = attend(low, query16, kv_prev, kv_own, seg_col, seg_row)
    attended_own = jnp.concatenate(to_partners([part(attended16, k) for k in range(ranks)]), 1)
    own_tokens = part(tokens16, 0).astype(f32)
    resid, act_share, scale_two = residual(
        attended_own, part(tokens16, 0), gain_mlp[None], outproj_all
    )

    act_two = flat(gather(act_share))
    act_turned = act_two.T
    dact = made = None
    hidden_grads = []
    for n, weights in enumerate(mlp16):
        last = n == len(mlp16) - 1
        dtype = bf16 if last else f32
        dgu, inner = hidden(act_two, cotan_mixed, weights, *([] if dact is None else [dact]))
        if last:
            dact = back(dgu, weights, 0, 2 * TILE, dact, dtype)
            local_grad = hidden_grad(act_turned, cotan_turned, dgu, inner, dact)
        else:
            local_grad = hidden_grad(act_turned, cotan_turned, dgu, inner)
            dact = back(dgu, weights, 0, 2 * TILE, dact, dtype, local_grad)
        hidden_grads.append(
            lax.psum_scatter(local_grad, rows_axes, scatter_dimension=0, tiled=True)
        )
        made = back(inner, weights, 2 * TILE, TILE, made, dtype, local_grad)

    dact_two = scatter(by_share(dact))
    normed_two = resid * scale_two
    dnorm_two, gain_two = norm_back(dact_two, normed_two, scale_two, gain_mlp)
    dresid = part(cotan16, 0).astype(f32) + dnorm_two
    dresid16 = dresid.astype(bf16)

    pieces = to_partners(attended_back(dresid16, outproj_all))
    dattended16 = natural([[piece] for piece in pieces])
    dresid_mixed = flat(gather(dresid16))
    dquery16, dkv_prev, dkv_own = attend_back(
        low,
        query16,
        kv_prev,
        kv_own,
        seg_col,
        seg_row,
        lse,
        attended16,
        dattended16,
        cosine,
        sine,
        dresid_mixed,
        made,
    )
    gateup_state = (gateup_weight, moment_gateup, square_gateup)
    down_state = (down_weight, moment_down, square_down)
    filled = adam_hidden(hidden_grads[0], gateup_state, down_state, 0, None)
    dkv_got = lax.ppermute(dkv_prev, "ctx", [(1, 0)])
    outproj_local = dot(dresid_mixed, mixed(attended16), OVER).astype(bf16)
    dproj16 = join(dquery16, dkv_own, dkv_got, cosine, sine, outproj_local, filled[0])
    qkv_local = dot(act_one, dproj16, OVER).astype(bf16)
    attn_grad = lax.psum_scatter(
        jnp.concatenate([qkv_local, outproj_local], 1), rows_axes, scatter_dimension=0, tiled=True
    )
    out_share = resid + scatter(by_share(hold(made, dproj16)))
    dact_one = scatter(
        [dot(part(dproj16, k), attn16[:, : 3 * columns], ROWS).astype(bf16) for k in range(ranks)]
    )
    normed_own, scale_own = normalize(own_tokens)
    dnorm_one, gain_one = norm_back(dact_one, normed_own, scale_own, gain_attn)
    for (first, _), gradient in zip(cuts[1:], hidden_grads[1:]):
        filled = adam_hidden(gradient, gateup_state, down_state, first, filled)

    arrived = {}
    input_grad = natural(gather((dresid + dnorm_one).astype(bf16), arrived))
    block_out = natural(gather(hold(out_share.astype(bf16), filled[0], *arrived[0])))

    gateup_grad, new_gateup, new_moment_gateup, new_square_gateup = filled[:4]
    down_grad, new_down, new_moment_down, new_square_down = filled[4:]
    outproj_grad, new_outproj, new_moment_outproj, new_square_outproj = adam(
        attn_grad,
        3,
        outproj_weight,
        moment_outproj,
        square_outproj,
        0.4 / math.sqrt(D // 64),
        new_down,
    )
    qkv_grad, new_qkv, new_moment_qkv, new_square_qkv = adam(
        attn_grad, 0, qkv_weight, moment_qkv, square_qkv, 0.4 / math.sqrt(D), new_down
    )
    gains_all = sum_everywhere(hold(jnp.stack([gain_one, gain_two]), new_qkv, new_outproj))
    wide = norm_gains.shape[1]
    place = (lax.axis_index("fsdp") * lax.axis_size("ctx") + half) * wide
    norm_grad = lax.dynamic_slice_in_dim(gains_all, place, wide, 1)

    new_norm, new_moment_norm, new_square_norm = adamw(
        norm_gains, norm_grad, moment_norm, square_norm, 0.4
    )
    return (
        block_out.reshape(block_input.shape),
        input_grad.reshape(block_input.shape),
        norm_grad,
        qkv_grad,
        outproj_grad,
        gateup_grad,
        down_grad,
        new_norm,
        new_qkv,
        new_outproj,
        new_gateup,
        new_down,
        new_moment_norm,
        new_moment_qkv,
        new_moment_outproj,
        new_moment_gateup,
        new_moment_down,
        new_square_norm,
        new_square_qkv,
        new_square_outproj,
        new_square_gateup,
        new_square_down,
    )


def solution(mesh):
    tokens = P("fsdp", "ctx", None)
    ids = P("fsdp", "ctx")
    gains = P(None, ("fsdp", "ctx"))
    stacked = P(None, ("fsdp", "ctx"), "tp")
    single = P(("fsdp", "ctx"), "tp")
    parameters = (gains, stacked, single, stacked, single)
    return jax.shard_map(
        local,
        mesh=mesh,
        in_specs=(tokens, ids, ids, tokens) + parameters * 3,
        out_specs=(tokens, tokens) + parameters * 4,
        check_vma=False,
    )
```

time: 919 us -> 748 us (0.81)
  waiting for transfers between devices: 442 us -> 220 us
  Pallas kernels: 102 us -> 254 us
  matrix products: 161 us -> 28.3 us
  blocking collectives: 85.3 us -> 13.7 us
  starting transfers between devices: 33.9 us -> 87.4 us
  local copies, waits for them, and re-layouts: 37.2 us -> 73.7 us
  other arithmetic: 36.6 us -> 47.6 us
    pallas_call x8 -> x23, Pallas kernels: 102 us -> 254 us  [the longest x4 54.7 us: back(): pl.pallas_call(waiting(functools.partial(back_kernel, at, tall), 2 + len(...]
    ppermute x25 -> x60, waiting for transfers between devices: 307 us -> 165 us  [the longest x59 165 us: exchange(): return lax.ppermute(values, axis, [(i, i ^ bit) for i in range(size)])]
    dot_general x14 -> x6, matrix products: 161 us -> 28.3 us  [dot(): lax.dot_general(one, two, (dims, ((), ())), preferred_element_type=f32)]
    all_gather x4 -> x3, waiting for transfers between devices: 134 us -> 51.5 us  [the longest x1 41.2 us: local(): attn16 = lax.all_gather(attn16, rows_axes, axis=0, tiled=True)]
    psum x1 -> x0, blocking collectives: 71.6 us -> none  [local(): gains_all = lax.psum(jnp.stack([gain_one, gain_two]), ('fsdp', 'ctx', 'tp'))]
    ppermute x25 -> x60, starting transfers between devices: 28.5 us -> 82.3 us  [the longest x59 81 us: exchange(): return lax.ppermute(values, axis, [(i, i ^ bit) for i in range(size)])]
    dynamic_update_slice x9 -> x20, local copies, waits for them, and re-layouts: 7.95 us -> 17.6 us  [natural(): whole = lax.dynamic_update_slice_in_dim(whole, piece, at, 0)]
    unnamed x59 -> x108, local copies, waits for them, and re-layouts: 13.3 us -> 19.1 us
  transfers between devices with their start and end apart: 35 -> 68, of which waited for: 20 -> 29; matrix products, arithmetic and copies ran while one was open for 18% -> 19% of each run, Pallas kernels for 10% -> 34%
where the time goes in v2:
time: 748 us; the launch traced here: 740 us
  Pallas kernels  254 us (34%)
  waiting for transfers between devices  220 us (29%)
  starting transfers between devices  87.4 us (12%)
  local copies, waits for them, and re-layouts  73.7 us (10%)
  other arithmetic  47.6 us (6%)
  matrix products  28.3 us (4%)
  between operations  15.5 us (2%)
  blocking collectives  13.7 us (2%)
    ppermute x59, waiting for transfers between devices, exchange(): return lax.ppermute(values, axis, [(i, i ^ bit) for i in range(size)])  165 us
    ppermute x59, starting transfers between devices, exchange(): return lax.ppermute(values, axis, [(i, i ^ bit) for i in range(size)])  81 us
    pallas_call x4, Pallas kernels, back(): pl.pallas_call(waiting(functools.partial(back_kernel, at, tall), 2 + len(...  54.7 us
    all_gather x1, waiting for transfers between devices, local(): attn16 = lax.all_gather(attn16, rows_axes, axis=0, tiled=True)  41.2 us
    pallas_call x2, Pallas kernels, hidden(): pl.pallas_call(waiting(hidden_kernel, 5, waits), grid=(tiles,), in_specs=...  40.3 us
    pallas_call x2, Pallas kernels, hidden_grad(): pl.pallas_call(waiting(hidden_grad_kernel, 4, waits), grid=(tiles,), in_s...  39.5 us
    dot_general x6, matrix products, dot(): lax.dot_general(one, two, (dims, ((), ())), preferred_element_type=f32)  28.3 us
    pallas_call x1, Pallas kernels, attend_back(): pl.pallas_call(waiting(attend_back_kernel, 11, waits), grid_spec=pltpu.Pr...  28 us
  transfers between devices with their start and end apart: 68, of which 29 were waited for; matrix products, arithmetic and copies ran while one was open for 19% of the time, Pallas kernels for 34%

profile of v2, /device:TPU:0, one launch (start us, length us, event | category | flops | bytes accessed | tf_op | source)
XLA Modules:
  0.0 739.9 jit_solution(3790073020384349282)
XLA Ops:
  31.9 13.7 %all_gather.12 = bf16[2,2048]{1,0:T(2,128)(2,1)S(1)} all-gather(bf16[2,256]{1,0:T(2,128)(2,1)S(1)} %convert_element_type.190), channel_id=1, replica_groups=mesh['fsdp'=4,'ctx'=2,'tp'=4] {'fsdp','ctx'}, dimensions={1}, use_global_device_ids=true | all-gather | bytes 9216 | tf_op jit(solution)/shard_map/all_gather | solution.py:899
  53.9 41.2 %all-gather.4.cloned.1.call-done.refs_1_ = bf16[2048,2048]{1,0:T(8,128)(2,1)} async-done(((bf16[256,2048]{1,0:T(8,128)(2,1)}), bf16[2048,2048]{1,0:T(8,128)(2,1)}) %all-gather.4.cloned.1.call-update) | async-done | bytes 8388624 | tf_op jit(solution)/shard_map/all_gather | solution.py:892
  95.1 11.3 %project_rope.1 = (bf16[1024,512]{1,0:T(8,128)(2,1)}, bf16[1024,1024]{1,0:T(8,128)(2,1)}) custom-call(bf16[1024,2048]{1,0:T(8,128)(2,1)} %fusion.2.refs_0_, bf16[2048,2048]{1,0:T(8,128)(2,1)} %all-gather.4.cloned.1.call-done.refs_1_, f32[1024,128]{1,0:T(8,128)} %get-tuple-element.163.refs_2_.refs_9_.refs_3_, ...), custom_call_target="tpu_custom_call" | custom-call | flops 6442450944 | bytes 13631488 | tf_op jit(solution)/shard_map/project_rope/pallas_call | solution.py:125
  120.7 17.3 %collective-permute-done.8.refs_5_.refs_6_ = bf16[1024,512]{1,0:T(8,128)(2,1)} collective-permute-done((bf16[1024,512]{1,0:T(8,128)(2,1)S(1)}, bf16[1024,512]{1,0:T(8,128)(2,1)}, u32[]{:S(2)}, u32[]{:S(2)}) %collective-permute-start.8) | collective-permute-done | bytes 1048608 | tf_op jit(solution)/shard_map/ppermute | solution.py:708
  141.0 14.2 %attend.1 = (bf16[1024,512]{1,0:T(8,128)(2,1)}, f32[8,1024]{1,0:T(8,128)}) custom-call(s32[4]{0:T(128)} %convert_reduce_fusion.low_ref.refs_0_, bf16[1024,512]{1,0:T(8,128)(2,1)} %get-tuple-element.64.q_ref.refs_1_, bf16[1024,1024]{1,0:T(8,128)(2,1)} %collective-permute-done.1.prev_ref.refs_2_, bf16[1024,1024]{1,0:T(8,128)(2,1)} %get-tuple-element.65.own_ref.refs_3_, ...), custom_call_target="tpu_custom_call" | custom-call | flops 8589934592 | bytes 6291456 | tf_op jit(solution)/shard_map/attend/pallas_call | solution.py:259
  157.1 29.8 %collective-permute-done.2 = bf16[256,512]{1,0:T(8,128)(2,1)S(1)} collective-permute-done((bf16[256,512]{1,0:T(8,128)(2,1)S(1)}, bf16[256,512]{1,0:T(8,128)(2,1)S(1)}, u32[]{:S(2)}, u32[]{:S(2)}) %collective-permute-start.2) | collective-permute-done | bytes 262176 | tf_op jit(solution)/shard_map/ppermute | solution.py:708
  187.4 8.7 %collective-permute-done.3 = bf16[256,512]{1,0:T(8,128)(2,1)S(1)} collective-permute-done((bf16[256,512]{1,0:T(8,128)(2,1)S(1)}, bf16[256,512]{1,0:T(8,128)(2,1)S(1)}, u32[]{:S(2)}, u32[]{:S(2)}) %collective-permute-start.3) | collective-permute-done | bytes 262176 | tf_op jit(solution)/shard_map/ppermute | solution.py:708
  206.5 8.2 %residual.1 = (f32[256,2048]{1,0:T(8,128)}, bf16[256,2048]{1,0:T(8,128)(2,1)}, f32[256,1]{1,0:T(8,128)}) custom-call(bf16[256,2048]{1,0:T(8,128)(2,1)} %pad_maximum_fusion.5.att_ref, bf16[256,2048]{1,0:T(8,128)(2,1)} %get-tuple-element.115.x_ref, f32[1,2048]{1,0:T(1,128)} %get-tuple-element.158.gain_ref, bf16[1024,512]{1,0:T(8,128)(2,1)} %copy-done.12, ...), custom_call_target="tpu_custom_call" | custom-call | flops 2147483648 | bytes 14680064 | tf_op jit(solution)/shard_map/residual/pallas_call | solution.py:787
  221.4 9.8 %collective-permute-done.11 = bf16[128,2048]{0,1:T(8,128)(2,1)S(1)} collective-permute-done((bf16[128,2048]{0,1:T(8,128)(2,1)S(1)}, bf16[128,2048]{0,1:T(8,128)(2,1)S(1)}, u32[]{:S(2)}, u32[]{:S(2)}) %collective-permute-start.11) | collective-permute-done | bytes 524320 | tf_op jit(solution)/shard_map/ppermute | solution.py:708
  254.8 23.8 %hidden_units.2 = (bf16[1024,2560]{1,0:T(8,128)(2,1)}, bf16[1024,1280]{1,0:T(8,128)(2,1)}) custom-call(bf16[1024,2048]{1,0:T(8,128)(2,1)} %copy.105.refs_0_, bf16[1024,2048]{1,0:T(8,128)(2,1)} %get-tuple-element.133.refs_1_, bf16[2048,3840]{1,0:T(8,128)(2,1)} %all-gather.8.cloned.1.call-done.refs_2_.refs_3_.refs_4_.refs_1_, ...), custom_call_target="tpu_custom_call" | custom-call | flops 16106127360 | bytes 31981568 | tf_op jit(solution)/shard_map/hidden_units/pallas_call | solution.py:520
  278.5 23.4 %hidden_grad.2.refs_2_ = bf16[2048,3840]{1,0:T(8,128)(2,1)} custom-call(bf16[2048,1024]{1,0:T(8,128)(2,1)} %bitcast.15.refs_0_, bf16[2048,1024]{1,0:T(8,128)(2,1)} %copy.98.refs_4_.refs_1_, bf16[1024,2560]{1,0:T(8,128)(2,1)} %get-tuple-element.69.refs_2_.refs_0_, bf16[1024,1280]{1,0:T(8,128)(2,1)} %get-tuple-element.70.refs_3_.refs_0_), custom_call_target="tpu_custom_call" | custom-call | flops 16106127360 | bytes 31981568 | tf_op jit(solution)/shard_map/hidden_grad/pallas_call | solution.py:552
  302.0 17.3 %from_hidden.4.refs_5_.refs_2_ = f32[1024,2048]{1,0:T(8,128)} custom-call(bf16[1024,2560]{1,0:T(8,128)(2,1)} %get-tuple-element.69.refs_2_.refs_0_, bf16[2048,3840]{1,0:T(8,128)(2,1)} %all-gather.8.cloned.1.call-done.refs_2_.refs_3_.refs_4_.refs_1_, bf16[2048,3840]{1,0:T(8,128)(2,1)} %hidden_grad.2.refs_2_), custom_call_target="tpu_custom_call" | custom-call | flops 10737418240 | bytes 29360128 | tf_op jit(solution)/shard_map/from_hidden/pallas_call | solution.py:591
  319.3 10.3 %all-gather.6.cloned.1.call-done.refs_2_.refs_3_.refs_4_.refs_1_ = bf16[2048,2304]{1,0:T(8,128)(2,1)} async-done(((bf16[256,2304]{1,0:T(8,128)(2,1)}), bf16[2048,2304]{1,0:T(8,128)(2,1)}) %all-gather.6.cloned.1.call-update) | async-done | bytes 9437200 | tf_op jit(solution)/shard_map/all_gather | solution.py:894
  329.6 16.5 %hidden_units.3 = (bf16[1024,1536]{1,0:T(8,128)(2,1)}, bf16[1024,768]{1,0:T(8,128)(2,1)}) custom-call(bf16[1024,2048]{1,0:T(8,128)(2,1)} %copy.105.refs_0_, bf16[1024,2048]{1,0:T(8,128)(2,1)} %get-tuple-element.133.refs_1_, bf16[2048,2304]{1,0:T(8,128)(2,1)} %all-gather.6.cloned.1.call-done.refs_2_.refs_3_.refs_4_.refs_1_, ...), custom_call_target="tpu_custom_call" | custom-call | flops 9663676416 | bytes 22544384 | tf_op jit(solution)/shard_map/hidden_units/pallas_call | solution.py:520
  346.1 13.4 %from_hidden.6.refs_4_ = bf16[1024,2048]{1,0:T(8,128)(2,1)} custom-call(bf16[1024,1536]{1,0:T(8,128)(2,1)} %get-tuple-element.72.refs_0_.refs_2_, bf16[2048,2304]{1,0:T(8,128)(2,1)} %all-gather.6.cloned.1.call-done.refs_2_.refs_3_.refs_4_.refs_1_, f32[1024,2048]{1,0:T(8,128)} %from_hidden.4.refs_5_.refs_2_), custom_call_target="tpu_custom_call" | custom-call | flops 6442450944 | bytes 20971520 | tf_op jit(solution)/shard_map/from_hidden/pallas_call | solution.py:591
  359.5 16.1 %hidden_grad.3.refs_3_ = bf16[2048,2304]{1,0:T(8,128)(2,1)} custom-call(bf16[2048,1024]{1,0:T(8,128)(2,1)} %bitcast.15.refs_0_, bf16[2048,1024]{1,0:T(8,128)(2,1)} %copy.98.refs_4_.refs_1_, bf16[1024,1536]{1,0:T(8,128)(2,1)} %get-tuple-element.72.refs_0_.refs_2_, bf16[1024,768]{1,0:T(8,128)(2,1)} %get-tuple-element.71.refs_3_.refs_0_, ...), custom_call_target="tpu_custom_call" | custom-call | flops 9663676416 | bytes 22544384 | tf_op jit(solution)/shard_map/hidden_grad/pallas_call | solution.py:552
  381.7 11.2 %collective-permute-done.18 = bf16[128,2048]{1,0:T(8,128)(2,1)S(1)} collective-permute-done((bf16[128,2048]{1,0:T(8,128)(2,1)S(1)}, bf16[128,2048]{1,0:T(8,128)(2,1)S(1)}, u32[]{:S(2)}, u32[]{:S(2)}) %collective-permute-start.18) | collective-permute-done | bytes 524320 | tf_op jit(solution)/shard_map/ppermute | solution.py:708
  396.2 7.4 %collective-permute-done.17 = bf16[128,2048]{1,0:T(8,128)(2,1)S(1)} collective-permute-done((bf16[128,2048]{1,0:T(8,128)(2,1)S(1)}, bf16[128,2048]{1,0:T(8,128)(2,1)S(1)}, u32[]{:S(2)}, u32[]{:S(2)}) %collective-permute-start.17) | collective-permute-done | bytes 524320 | tf_op jit(solution)/shard_map/ppermute | solution.py:708
  413.4 13.0 %from_hidden.5.refs_2_ = f32[1024,2048]{1,0:T(8,128)} custom-call(bf16[1024,1280]{1,0:T(8,128)(2,1)} %get-tuple-element.70.refs_3_.refs_0_, bf16[2048,3840]{1,0:T(8,128)(2,1)} %all-gather.8.cloned.1.call-done.refs_2_.refs_3_.refs_4_.refs_1_, bf16[2048,3840]{1,0:T(8,128)(2,1)} %hidden_grad.2.refs_2_), custom_call_target="tpu_custom_call" | custom-call | flops 5368709120 | bytes 26738688 | tf_op jit(solution)/shard_map/from_hidden/pallas_call | solution.py:591
  433.0 6.8 attended_back.1
  442.0 11.0 %from_hidden.7.refs_12_.refs_0_ = bf16[1024,2048]{1,0:T(8,128)(2,1)} custom-call(bf16[1024,768]{1,0:T(8,128)(2,1)} %get-tuple-element.71.refs_3_.refs_0_, bf16[2048,2304]{1,0:T(8,128)(2,1)} %all-gather.6.cloned.1.call-done.refs_2_.refs_3_.refs_4_.refs_1_, f32[1024,2048]{1,0:T(8,128)} %from_hidden.5.refs_2_, bf16[2048,2304]{1,0:T(8,128)(2,1)} %hidden_grad.3.refs_3_), custom_call_target="tpu_custom_call" | custom-call | flops 3221225472 | bytes 19398656 | tf_op jit(solution)/shard_map/from_hidden/pallas_call | solution.py:591
  466.2 7.9 %collective-permute-done.27 = bf16[128,2048]{1,0:T(8,128)(2,1)S(1)} collective-permute-done((bf16[128,2048]{1,0:T(8,128)(2,1)S(1)}, bf16[128,2048]{1,0:T(8,128)(2,1)S(1)}, u32[]{:S(2)}, u32[]{:S(2)}) %collective-permute-start.27) | collective-permute-done | bytes 524320 | tf_op jit(solution)/shard_map/ppermute | solution.py:708
  481.3 28.0 %attend_back.1 = (bf16[1024,512]{1,0:T(8,128)(2,1)}, f32[1024,1024]{1,0:T(8,128)}, f32[1024,1024]{1,0:T(8,128)}) custom-call(s32[4]{0:T(128)} %convert_reduce_fusion.low_ref.refs_0_, bf16[1024,512]{1,0:T(8,128)(2,1)} %get-tuple-element.64.q_ref.refs_1_, bf16[1024,1024]{1,0:T(8,128)(2,1)} %collective-permute-done.1.prev_ref.refs_2_, ...), custom_call_target="tpu_custom_call" | custom-call | flops 12884901888 | bytes 16777216 | tf_op jit(solution)/shard_map/attend_back/pallas_call | solution.py:400
  515.4 13.3 %adamw_hidden.2 = (f32[2,256,2048]{2,1,0:T(8,128)}, f32[2,256,2048]{2,1,0:T(8,128)}, f32[2,256,2048]{2,1,0:T(8,128)}, f32[2,256,2048]{2,1,0:T(8,128)}, f32[256,2...) custom-call(bf16[256,3840]{1,0:T(8,128)(2,1)} %reduce-scatter.4.cloned.1.call-done.g_ref, ...), custom_call_target="tpu_custom_call" | custom-call | flops 14745600 | bytes 29491200 | tf_op jit(solution)/shard_map/adamw_hidden/pallas_call | solution.py:677
  528.7 6.9 join_dproj.1.refs_1_
  535.6 10.5 %convolution_convert_fusion = bf16[2048,1536]{1,0:T(8,128)(2,1)} fusion(bf16[1024,2048]{1,0:T(8,128)(2,1)S(1)} %copy-done.20, bf16[1024,1536]{1,0:T(8,128)(2,1)} %join_dproj.1.refs_1_), kind=kOutput, calls=%fused_computation.6 | convolution fusion | flops 6445596672 | bytes 13631488 | tf_op jit(solution)/shard_map/dot_general | solution.py:72
  546.1 8.3 %pad_maximum_fusion = bf16[2048,2048]{1,0:T(8,128)(2,1)} fusion(bf16[2048,512]{1,0:T(8,128)(2,1)} %convolution_convert_fusion.1.refs_5_, bf16[2048,1536]{1,0:T(8,128)(2,1)} %convolution_convert_fusion), kind=kLoop, calls=%fused_computation.5 | loop fusion | flops 16777216 | bytes 16777216 | tf_op jit(solution)/shard_map/concatenate | solution.py:984
  589.2 9.7 %adamw_hidden.3 = (f32[2,256,2048]{2,1,0:T(8,128)}, f32[2,256,2048]{2,1,0:T(8,128)}, f32[2,256,2048]{2,1,0:T(8,128)}, f32[2,256,2048]{2,1,0:T(8,128)}, f32[256,2...) custom-call(bf16[256,2304]{1,0:T(8,128)(2,1)} %reduce-scatter.6.clon, ...), custom_call_target="tpu_custom_call", output_to_operand_aliasing={{0}: (7, {}), {1}: (8, {}), {2}: (9, {}), {3}: (10, {}), {4... | custom-call | flops 8847360 | bytes 17694720 | tf_op jit(solution)/shard_map/adamw_hidden/pallas_call | solution.py:677
  618.9 11.3 %collective-permute-done.35 = bf16[128,2048]{1,0:T(8,128)(2,1)S(1)} collective-permute-done((bf16[128,2048]{1,0:T(8,128)(2,1)S(1)}, bf16[128,2048]{1,0:T(8,128)(2,1)S(1)}, u32[]{:S(2)}, u32[]{:S(2)}) %collective-permute-start.35) | collective-permute-done | bytes 524320 | tf_op jit(solution)/shard_map/ppermute | solution.py:708
  637.4 13.2 %collective-permute-done.38 = bf16[128,2048]{1,0:T(8,128)(2,1)S(1)} collective-permute-done((bf16[128,2048]{1,0:T(8,128)(2,1)S(1)}, bf16[128,2048]{1,0:T(8,128)(2,1)S(1)}, u32[]{:S(2)}, u32[]{:S(2)}) %collective-permute-start.38) | collective-permute-done | bytes 524320 | tf_op jit(solution)/shard_map/ppermute | solution.py:708
  684.5 6.7 adamw.2
  701.5 19.3 %collective-permute-start.59 = (f32[2,2048]{1,0:T(2,128)S(1)}, f32[2,2048]{1,0:T(2,128)S(1)}, u32[]{:S(2)}, u32[]{:S(2)}) collective-permute-start(f32[2,2048]{1,0:T(2,128)S(1)} %add.244), channel_id=1, source_target_pairs={{0,4},{4,0},{1,5},{5,1},{2,6},{6,2},{3,7},{7,3},{8,12},{12,8},{9,1... | collective-permute-start | bytes 49160 | tf_op jit(solution)/shard_map/ppermute | solution.py:708
  (339 shorter events, 265.1 us)
Async XLA Ops:
  7.2 87.9 %all-gather.4.cloned.1.call-start = ((), (), s32[]{:S(2)}) async-start(), calls=%async_computation.3 | async-start | bytes 9437184 | tf_op jit(solution)/shard_map/all_gather | solution.py:892
  10.2 244.6 %all-gather.8.cloned.1.call-start = ((), (), s32[]{:S(2)}) async-start(), calls=%async_computation.5 | async-start | bytes 17694720 | tf_op jit(solution)/shard_map/all_gather | solution.py:894
  14.4 315.2 %all-gather.6.cloned.1.call-start = ((), (), s32[]{:S(2)}) async-start(), calls=%async_computation.4 | async-start | bytes 10616832 | tf_op jit(solution)/shard_map/all_gather | solution.py:894
  18.4 497.0 %reduce-scatter.4.cloned.1.call-start = ((), (), s32[]{:S(2)}) async-start(), calls=%async_computation.6 | async-start | bytes 17694720 | tf_op jit(solution)/shard_map/reduce_scatter | solution.py:948
  106.4 34.6 %collective-permute-start.1 = (bf16[1024,1024]{1,0:T(8,128)(2,1)}, bf16[1024,1024]{1,0:T(8,128)(2,1)}, u32[]{:S(2)}, u32[]{:S(2)}) collective-permute-start(bf16[1024,1024]{1,0:T(8,128)(2,1)} %get-tuple-element.65.own_ref.refs_3_), channel_id=1, source_target_pairs={{0,4},{1,5},{2,6},{3,7},{8,12},{9,13},{10,14},{11,15},{16,20},{17,... | collective-permute-start | bytes 6291464 | tf_op jit(solution)/shard_map/ppermute | solution.py:925
  111.7 26.3 %collective-permute-start.8 = (bf16[1024,512]{1,0:T(8,128)(2,1)S(1)}, bf16[1024,512]{1,0:T(8,128)(2,1)}, u32[]{:S(2)}, u32[]{:S(2)}) collective-permute-start(bf16[1024,512]{1,0:T(8,128)(2,1)S(1)} %get-tuple-element.119.refs_1_.refs_2_), channel_id=1, source_target_pairs={{0,2},{1,3},{2,0},{3,1},{4,6},{5,7},{6,4},{7,5},{8,10},{9,11},{10,... | collective-permute-start | bytes 3145736 | tf_op jit(solution)/shard_map/ppermute | solution.py:708
  113.3 26.2 %collective-permute-start.5 = (bf16[1024,512]{1,0:T(8,128)(2,1)S(1)}, bf16[1024,512]{1,0:T(8,128)(2,1)}, u32[]{:S(2)}, u32[]{:S(2)}) collective-permute-start(bf16[1024,512]{1,0:T(8,128)(2,1)S(1)} %get-tuple-element.120.refs_0_.refs_1_), channel_id=1, source_target_pairs={{0,1},{1,0},{2,3},{3,2},{4,5},{5,4},{6,7},{7,6},{8,9},{9,8},{10,11... | collective-permute-start | bytes 3145736 | tf_op jit(solution)/shard_map/ppermute | solution.py:708
  119.6 84.8 %collective-permute-start.6 = (bf16[1024,512]{1,0:T(8,128)(2,1)S(1)}, bf16[1024,512]{1,0:T(8,128)(2,1)S(1)}, u32[]{:S(2)}, u32[]{:S(2)}) collective-permute-start(bf16[1024,512]{1,0:T(8,128)(2,1)S(1)} %get-tuple-element.119.refs_1_.refs_2_), channel_id=1, source_target_pairs={{0,1},{1,0},{2,3},{3,2},{4,5},{5,4},{6,7},{7,6},{8,9},{9,8},{10,11... | collective-permute-start | bytes 3145736 | tf_op jit(solution)/shard_map/ppermute | solution.py:708
  120.2 84.2 %collective-permute-start.7 = (bf16[1024,512]{1,0:T(8,128)(2,1)S(1)}, bf16[1024,512]{1,0:T(8,128)(2,1)S(1)}, u32[]{:S(2)}, u32[]{:S(2)}) collective-permute-start(bf16[1024,512]{1,0:T(8,128)(2,1)S(1)} %get-tuple-element.120.refs_0_.refs_1_), channel_id=1, source_target_pairs={{0,2},{1,3},{2,0},{3,1},{4,6},{5,7},{6,4},{7,5},{8,10},{9,11},{10,... | collective-permute-start | bytes 3145736 | tf_op jit(solution)/shard_map/ppermute | solution.py:708
  138.0 66.5 %collective-permute-start.10 = (bf16[1024,512]{1,0:T(8,128)(2,1)}, bf16[1024,512]{1,0:T(8,128)(2,1)S(1)}, u32[]{:S(2)}, u32[]{:S(2)}) collective-permute-start(bf16[1024,512]{1,0:T(8,128)(2,1)} %collective-permute-done.8.refs_5_.refs_6_), channel_id=1, source_target_pairs={{0,1},{1,0},{2,3},{3,2},{4,5},{5,4},{6,7},{7,6},{8,9},{9,8},{10,11... | collective-permute-start | bytes 3145736 | tf_op jit(solution)/shard_map/ppermute | solution.py:708
  139.5 65.0 %collective-permute-start.9 = (bf16[1024,512]{1,0:T(8,128)(2,1)}, bf16[1024,512]{1,0:T(8,128)(2,1)S(1)}, u32[]{:S(2)}, u32[]{:S(2)}) collective-permute-start(bf16[1024,512]{1,0:T(8,128)(2,1)} %collective-permute-done.5.refs_2_.refs_3_), channel_id=1, source_target_pairs={{0,2},{1,3},{2,0},{3,1},{4,6},{5,7},{6,4},{7,5},{8,10},{9,11},{10,... | collective-permute-start | bytes 3145736 | tf_op jit(solution)/shard_map/ppermute | solution.py:708
  156.5 30.4 %collective-permute-start.2 = (bf16[256,512]{1,0:T(8,128)(2,1)S(1)}, bf16[256,512]{1,0:T(8,128)(2,1)S(1)}, u32[]{:S(2)}, u32[]{:S(2)}) collective-permute-start(bf16[256,512]{1,0:T(8,128)(2,1)S(1)} %get-tuple-element.154), channel_id=1, source_target_pairs={{0,1},{1,0},{2,3},{3,2},{4,5},{5,4},{6,7},{7,6},{8,9},{9,8},{10,11... | collective-permute-start | bytes 786440 | tf_op jit(solution)/shard_map/ppermute | solution.py:708
  302.0 287.3 %reduce-scatter.6.cloned.1.call-start = ((), (), s32[]{:S(2)}) async-start(), calls=%async_computation.7 | async-start | bytes 10616832 | tf_op jit(solution)/shard_map/reduce_scatter | solution.py:948
  375.6 305.7 %reduce-scatter.8.cloned.1.call-start = ((), (), s32[]{:S(2)}) async-start(), calls=%async_computation.8 | async-start | bytes 9437184 | tf_op jit(solution)/shard_map/reduce_scatter | solution.py:983
  379.7 23.9 %collective-permute-start.17 = (bf16[128,2048]{1,0:T(8,128)(2,1)S(1)}, bf16[128,2048]{1,0:T(8,128)(2,1)S(1)}, u32[]{:S(2)}, u32[]{:S(2)}) collective-permute-start(bf16[128,2048]{1,0:T(8,128)(2,1)S(1)} %get-tuple-element.129), channel_id=1, source_target_pairs={{0,1},{1,0},{2,3},{3,2},{4,5},{5,4},{6,7},{7,6},{8,9},{9,8},{10,11... | collective-permute-start | bytes 1572872 | tf_op jit(solution)/shard_map/ppermute | solution.py:708
  380.2 23.4 %collective-permute-start.21 = (bf16[128,2048]{1,0:T(8,128)(2,1)S(1)}, bf16[128,2048]{1,0:T(8,128)(2,1)S(1)}, u32[]{:S(2)}, u32[]{:S(2)}) collective-permute-start(bf16[128,2048]{1,0:T(8,128)(2,1)S(1)} %get-tuple-element.130), channel_id=1, source_target_pairs={{0,2},{1,3},{2,0},{3,1},{4,6},{5,7},{6,4},{7,5},{8,10},{9,11},{10,... | collective-permute-start | bytes 1572872 | tf_op jit(solution)/shard_map/ppermute | solution.py:708
  395.7 30.8 %collective-permute-start.20 = (bf16[128,2048]{1,0:T(8,128)(2,1)}, bf16[128,2048]{1,0:T(8,128)(2,1)}, u32[]{:S(2)}, u32[]{:S(2)}) collective-permute-start(bf16[128,2048]{1,0:T(8,128)(2,1)} %get-tuple-element.131), channel_id=1, source_target_pairs={{0,2},{1,3},{2,0},{3,1},{4,6},{5,7},{6,4},{7,5},{8,10},{9,11},{10,... | collective-permute-start | bytes 1572872 | tf_op jit(solution)/shard_map/ppermute | solution.py:708
  431.1 32.1 %collective-permute-start.26 = (bf16[128,2048]{1,0:T(8,128)(2,1)S(1)}, bf16[128,2048]{1,0:T(8,128)(2,1)S(1)}, u32[]{:S(2)}, u32[]{:S(2)}) collective-permute-start(bf16[128,2048]{1,0:T(8,128)(2,1)S(1)} %get-tuple-element.148), channel_id=1, source_target_pairs={{0,1},{1,0},{2,3},{3,2},{4,5},{5,4},{6,7},{7,6},{8,9},{9,8},{10,11... | collective-permute-start | bytes 1572872 | tf_op jit(solution)/shard_map/ppermute | solution.py:708
  431.5 33.3 %collective-permute-start.29 = (bf16[128,2048]{1,0:T(8,128)(2,1)S(1)}, bf16[128,2048]{1,0:T(8,128)(2,1)S(1)}, u32[]{:S(2)}, u32[]{:S(2)}) collective-permute-start(bf16[128,2048]{1,0:T(8,128)(2,1)S(1)} %get-tuple-element.147), channel_id=1, source_target_pairs={{0,2},{1,3},{2,0},{3,1},{4,6},{5,7},{6,4},{7,5},{8,10},{9,11},{10,... | collective-permute-start | bytes 1572872 | tf_op jit(solution)/shard_map/ppermute | solution.py:708
  573.2 28.2 %collective-permute-start.39 = (bf16[128,2048]{1,0:T(8,128)(2,1)}, bf16[128,2048]{1,0:T(8,128)(2,1)}, u32[]{:S(2)}, u32[]{:S(2)}) collective-permute-start(bf16[128,2048]{1,0:T(8,128)(2,1)} %slice.233), channel_id=1, source_target_pairs={{0,1},{1,0},{2,3},{3,2},{4,5},{5,4},{6,7},{7,6},{8,9},{9,8},{10,11... | collective-permute-start | bytes 1572872 | tf_op jit(solution)/shard_map/ppermute | solution.py:708
  576.8 26.1 %collective-permute-start.42 = (bf16[128,2048]{1,0:T(8,128)(2,1)}, bf16[128,2048]{1,0:T(8,128)(2,1)}, u32[]{:S(2)}, u32[]{:S(2)}) collective-permute-start(bf16[128,2048]{1,0:T(8,128)(2,1)} %slice.237), channel_id=1, source_target_pairs={{0,2},{1,3},{2,0},{3,1},{4,6},{5,7},{6,4},{7,5},{8,10},{9,11},{10,... | collective-permute-start | bytes 1572872 | tf_op jit(solution)/shard_map/ppermute | solution.py:708
  580.7 25.1 %collective-permute-start.44 = (bf16[128,2048]{1,0:T(8,128)(2,1)}, bf16[128,2048]{1,0:T(8,128)(2,1)}, u32[]{:S(2)}, u32[]{:S(2)}) collective-permute-start(bf16[128,2048]{1,0:T(8,128)(2,1)} %add_convert_fusion), channel_id=1, source_target_pairs={{0,1},{1,0},{2,3},{3,2},{4,5},{5,4},{6,7},{7,6},{8,9},{9,8},{10,11... | collective-permute-start | bytes 1572872 | tf_op jit(solution)/shard_map/ppermute | solution.py:708
  582.6 24.0 %collective-permute-start.41 = (bf16[128,2048]{1,0:T(8,128)(2,1)}, bf16[128,2048]{1,0:T(8,128)(2,1)}, u32[]{:S(2)}, u32[]{:S(2)}) collective-permute-start(bf16[128,2048]{1,0:T(8,128)(2,1)} %add_convert_fusion.1), channel_id=1, source_target_pairs={{0,2},{1,3},{2,0},{3,1},{4,6},{5,7},{6,4},{7,5},{8,10},{9,11},{10,... | collective-permute-start | bytes 1572872 | tf_op jit(solution)/shard_map/ppermute | solution.py:708
  603.0 33.6 %collective-permute-start.36 = (bf16[128,2048]{1,0:T(8,128)(2,1)}, bf16[128,2048]{1,0:T(8,128)(2,1)S(1)}, u32[]{:S(2)}, u32[]{:S(2)}) collective-permute-start(bf16[128,2048]{1,0:T(8,128)(2,1)} %get-tuple-element.125), channel_id=1, source_target_pairs={{0,2},{1,3},{2,0},{3,1},{4,6},{5,7},{6,4},{7,5},{8,10},{9,11},{10,... | collective-permute-start | bytes 1572872 | tf_op jit(solution)/shard_map/ppermute | solution.py:708
  605.8 24.4 %collective-permute-start.35 = (bf16[128,2048]{1,0:T(8,128)(2,1)S(1)}, bf16[128,2048]{1,0:T(8,128)(2,1)S(1)}, u32[]{:S(2)}, u32[]{:S(2)}) collective-permute-start(bf16[128,2048]{1,0:T(8,128)(2,1)S(1)} %add_convert_fusion.3), channel_id=1, source_target_pairs={{0,2},{1,3},{2,0},{3,1},{4,6},{5,7},{6,4},{7,5},{8,10},{9,11},{10,... | collective-permute-start | bytes 1572872 | tf_op jit(solution)/shard_map/ppermute | solution.py:708
  611.0 41.2 %collective-permute-start.45 = (bf16[128,2048]{1,0:T(8,128)(2,1)}, bf16[128,2048]{1,0:T(8,128)(2,1)S(1)}, u32[]{:S(2)}, u32[]{:S(2)}) collective-permute-start(bf16[128,2048]{1,0:T(8,128)(2,1)} %get-tuple-element.142), channel_id=1, source_target_pairs={{0,1},{1,0},{2,3},{3,2},{4,5},{5,4},{6,7},{7,6},{8,9},{9,8},{10,11... | collective-permute-start | bytes 1572872 | tf_op jit(solution)/shard_map/ppermute | solution.py:708
  616.9 51.3 %collective-permute-start.54 = (bf16[128,2048]{1,0:T(8,128)(2,1)}, bf16[128,2048]{1,0:T(8,128)(2,1)}, u32[]{:S(2)}, u32[]{:S(2)}) collective-permute-start(bf16[128,2048]{1,0:T(8,128)(2,1)} %get-tuple-element.142), channel_id=1, source_target_pairs={{0,2},{1,3},{2,0},{3,1},{4,6},{5,7},{6,4},{7,5},{8,10},{9,11},{10,... | collective-permute-start | bytes 1572872 | tf_op jit(solution)/shard_map/ppermute | solution.py:708
  617.7 47.4 %collective-permute-start.53 = (bf16[128,2048]{1,0:T(8,128)(2,1)}, bf16[128,2048]{1,0:T(8,128)(2,1)}, u32[]{:S(2)}, u32[]{:S(2)}) collective-permute-start(bf16[128,2048]{1,0:T(8,128)(2,1)} %get-tuple-element.141), channel_id=1, source_target_pairs={{0,1},{1,0},{2,3},{3,2},{4,5},{5,4},{6,7},{7,6},{8,9},{9,8},{10,11... | collective-permute-start | bytes 1572872 | tf_op jit(solution)/shard_map/ppermute | solution.py:708
  668.2 30.2 %collective-permute-start.55 = (bf16[128,2048]{1,0:T(8,128)(2,1)S(1)}, bf16[128,2048]{1,0:T(8,128)(2,1)}, u32[]{:S(2)}, u32[]{:S(2)}) collective-permute-start(bf16[128,2048]{1,0:T(8,128)(2,1)S(1)} %copy-done.22), channel_id=1, source_target_pairs={{0,2},{1,3},{2,0},{3,1},{4,6},{5,7},{6,4},{7,5},{8,10},{9,11},{10,... | collective-permute-start | bytes 1572872 | tf_op jit(solution)/shard_map/ppermute | solution.py:708
  671.8 49.1 %collective-permute-start.56 = (bf16[128,2048]{1,0:T(8,128)(2,1)S(1)}, bf16[128,2048]{1,0:T(8,128)(2,1)}, u32[]{:S(2)}, u32[]{:S(2)}) collective-permute-start(bf16[128,2048]{1,0:T(8,128)(2,1)S(1)} %copy-done.24), channel_id=1, source_target_pairs={{0,1},{1,0},{2,3},{3,2},{4,5},{5,4},{6,7},{7,6},{8,9},{9,8},{10,11... | collective-permute-start | bytes 1572872 | tf_op jit(solution)/shard_map/ppermute | solution.py:708
  673.7 51.9 %collective-permute-start.51 = (bf16[128,2048]{1,0:T(8,128)(2,1)S(1)}, bf16[128,2048]{1,0:T(8,128)(2,1)S(1)}, u32[]{:S(2)}, u32[]{:S(2)}) collective-permute-start(bf16[128,2048]{1,0:T(8,128)(2,1)S(1)} %collective-permute-done.47), channel_id=1, source_target_pairs={{0,2},{1,3},{2,0},{3,1},{4,6},{5,7},{6,4},{7,5},{8,10},{9,11},{10,... | collective-permute-start | bytes 1572872 | tf_op jit(solution)/shard_map/ppermute | solution.py:708
  678.7 48.7 %collective-permute-start.52 = (bf16[128,2048]{1,0:T(8,128)(2,1)S(1)}, bf16[128,2048]{1,0:T(8,128)(2,1)S(1)}, u32[]{:S(2)}, u32[]{:S(2)}) collective-permute-start(bf16[128,2048]{1,0:T(8,128)(2,1)S(1)} %collective-permute-done.50), channel_id=1, source_target_pairs={{0,1},{1,0},{2,3},{3,2},{4,5},{5,4},{6,7},{7,6},{8,9},{9,8},{10,11... | collective-permute-start | bytes 1572872 | tf_op jit(solution)/shard_map/ppermute | solution.py:708
  (84 other events, 1261.4 us)
Sparse Core Ops, SparseCore 0:
  10.3 84.7 all-gather.3
  97.3 141.0 all-gather.7
  240.6 88.9 all-gather.5
  331.8 157.3 reduce-scatter.3
  491.3 97.8 reduce-scatter.5
  591.4 87.9 reduce-scatter.7

commit v3 on v2

--- a/solution.py
+++ b/solution.py
@@ -937,25 +937,29 @@
     for n, weights in enumerate(mlp16):
         last = n == len(mlp16) - 1
         dtype = bf16 if last else f32
-        dgu, inner = hidden(act_two, cotan_mixed, weights, *([] if dact is None else [dact]))
+        dgu, inner = hidden(act_two, cotan_mixed, weights, *([] if made is None else [made]))
         if last:
             dact = back(dgu, weights, 0, 2 * TILE, dact, dtype)
-            local_grad = hidden_grad(act_turned, cotan_turned, dgu, inner, dact)
+            arrived = {}
+            dact_two = scatter(by_share(dact), arrived)
+            waits = [one for step in arrived.values() for one in step]
+            local_grad = hidden_grad(act_turned, cotan_turned, dgu, inner, *waits)
         else:
             local_grad = hidden_grad(act_turned, cotan_turned, dgu, inner)
             dact = back(dgu, weights, 0, 2 * TILE, dact, dtype, local_grad)
+            made = back(inner, weights, 2 * TILE, TILE, made, dtype, dact)
         hidden_grads.append(
             lax.psum_scatter(local_grad, rows_axes, scatter_dimension=0, tiled=True)
         )
-        made = back(inner, weights, 2 * TILE, TILE, made, dtype, local_grad)
-
-    dact_two = scatter(by_share(dact))
+
     normed_two = resid * scale_two
     dnorm_two, gain_two = norm_back(dact_two, normed_two, scale_two, gain_mlp)
     dresid = part(cotan16, 0).astype(f32) + dnorm_two
     dresid16 = dresid.astype(bf16)
 
-    pieces = to_partners(attended_back(dresid16, outproj_all))
+    pieces = attended_back(dresid16, outproj_all)
+    made = back(inner, weights, 2 * TILE, TILE, made, dtype, pieces[0])
+    pieces = to_partners(pieces)
     dattended16 = natural([[piece] for piece in pieces])
     dresid_mixed = flat(gather(dresid16))
     dquery16, dkv_prev, dkv_own = attend_back(

time: 748 us -> 742 us (level)
  starting transfers between devices: 87.4 us -> 68.2 us
    ppermute x59, starting transfers between devices: 81 us -> 61.4 us  [exchange(): return lax.ppermute(values, axis, [(i, i ^ bit) for i in range(size)])]
    ppermute x59, waiting for transfers between devices: 165 us -> 177 us  [exchange(): return lax.ppermute(values, axis, [(i, i ^ bit) for i in range(size)])]
    all_gather x2, waiting for transfers between devices: 10.3 us -> 0.01 us  [local(): lax.all_gather(pack(gateup_weight, down_weight, first, count), rows_axes,...]
    unnamed x108 -> x118, local copies, waits for them, and re-layouts: 19.1 us -> 20.6 us
  transfers between devices with their start and end apart: 68 -> 68, of which waited for: 29 -> 29; matrix products, arithmetic and copies ran while one was open for 19% -> 19% of each run, Pallas kernels for 34% -> 35%
where the time goes in v3:
time: 742 us; the launch traced here: 732 us
  Pallas kernels  257 us (35%)
  waiting for transfers between devices  226 us (30%)
  local copies, waits for them, and re-layouts  74.5 us (10%)
  starting transfers between devices  68.2 us (9%)
  other arithmetic  49.4 us (7%)
  matrix products  28.3 us (4%)
  between operations  15.6 us (2%)
  blocking collectives  13.7 us (2%)
    ppermute x59, waiting for transfers between devices, exchange(): return lax.ppermute(values, axis, [(i, i ^ bit) for i in range(size)])  177 us
    ppermute x59, starting transfers between devices, exchange(): return lax.ppermute(values, axis, [(i, i ^ bit) for i in range(size)])  61.4 us
    pallas_call x4, Pallas kernels, back(): pl.pallas_call(waiting(functools.partial(back_kernel, at, tall), 2 + len(...  54.4 us
    all_gather x1, waiting for transfers between devices, local(): attn16 = lax.all_gather(attn16, rows_axes, axis=0, tiled=True)  41.2 us
    pallas_call x2, Pallas kernels, hidden(): pl.pallas_call(waiting(hidden_kernel, 5, waits), grid=(tiles,), in_specs=...  40.6 us
    pallas_call x2, Pallas kernels, hidden_grad(): pl.pallas_call(waiting(hidden_grad_kernel, 4, waits), grid=(tiles,), in_s...  39.5 us
    pallas_call x1, Pallas kernels, attend_back(): pl.pallas_call(waiting(attend_back_kernel, 11, waits), grid_spec=pltpu.Pr...  30.1 us
    dot_general x6, matrix products, dot(): lax.dot_general(one, two, (dims, ((), ())), preferred_element_type=f32)  28.3 us
  transfers between devices with their start and end apart: 68, of which 29 were waited for; matrix products, arithmetic and copies ran while one was open for 19% of the time, Pallas kernels for 35%

profile of v3, /device:TPU:0, one launch (start us, length us, event | category | flops | bytes accessed | tf_op | source)
XLA Modules:
  0.0 732.3 jit_solution(1873816589330847318)
XLA Ops:
  31.9 13.7 %all_gather.12 = bf16[2,2048]{1,0:T(2,128)(2,1)S(1)} all-gather(bf16[2,256]{1,0:T(2,128)(2,1)S(1)} %convert_element_type.190), channel_id=1, replica_groups=mesh['fsdp'=4,'ctx'=2,'tp'=4] {'fsdp','ctx'}, dimensions={1}, use_global_device_ids=true | all-gather | bytes 9216 | tf_op jit(solution)/shard_map/all_gather | solution.py:899
  53.9 41.2 %all-gather.4.cloned.1.call-done.refs_1_ = bf16[2048,2048]{1,0:T(8,128)(2,1)} async-done(((bf16[256,2048]{1,0:T(8,128)(2,1)}), bf16[2048,2048]{1,0:T(8,128)(2,1)}) %all-gather.4.cloned.1.call-update) | async-done | bytes 8388624 | tf_op jit(solution)/shard_map/all_gather | solution.py:892
  95.1 11.3 %project_rope.1 = (bf16[1024,512]{1,0:T(8,128)(2,1)}, bf16[1024,1024]{1,0:T(8,128)(2,1)}) custom-call(bf16[1024,2048]{1,0:T(8,128)(2,1)} %fusion.2.refs_0_, bf16[2048,2048]{1,0:T(8,128)(2,1)} %all-gather.4.cloned.1.call-done.refs_1_, f32[1024,128]{1,0:T(8,128)} %get-tuple-element.163.refs_2_.refs_9_.refs_3_, ...), custom_call_target="tpu_custom_call" | custom-call | flops 6442450944 | bytes 13631488 | tf_op jit(solution)/shard_map/project_rope/pallas_call | solution.py:125
  120.7 17.3 %collective-permute-done.8.refs_5_.refs_6_ = bf16[1024,512]{1,0:T(8,128)(2,1)} collective-permute-done((bf16[1024,512]{1,0:T(8,128)(2,1)S(1)}, bf16[1024,512]{1,0:T(8,128)(2,1)}, u32[]{:S(2)}, u32[]{:S(2)}) %collective-permute-start.8) | collective-permute-done | bytes 1048608 | tf_op jit(solution)/shard_map/ppermute | solution.py:708
  141.0 15.3 %attend.1 = (bf16[1024,512]{1,0:T(8,128)(2,1)}, f32[8,1024]{1,0:T(8,128)}) custom-call(s32[4]{0:T(128)} %convert_reduce_fusion.low_ref.refs_0_, bf16[1024,512]{1,0:T(8,128)(2,1)} %get-tuple-element.64.q_ref.refs_1_, bf16[1024,1024]{1,0:T(8,128)(2,1)} %collective-permute-done.1.prev_ref.refs_2_, bf16[1024,1024]{1,0:T(8,128)(2,1)} %get-tuple-element.65.own_ref.refs_3_, ...), custom_call_target="tpu_custom_call" | custom-call | flops 8589934592 | bytes 6291456 | tf_op jit(solution)/shard_map/attend/pallas_call | solution.py:259
  158.2 28.7 %collective-permute-done.2 = bf16[256,512]{1,0:T(8,128)(2,1)S(1)} collective-permute-done((bf16[256,512]{1,0:T(8,128)(2,1)S(1)}, bf16[256,512]{1,0:T(8,128)(2,1)S(1)}, u32[]{:S(2)}, u32[]{:S(2)}) %collective-permute-start.2) | collective-permute-done | bytes 262176 | tf_op jit(solution)/shard_map/ppermute | solution.py:708
  187.4 8.7 %collective-permute-done.3 = bf16[256,512]{1,0:T(8,128)(2,1)S(1)} collective-permute-done((bf16[256,512]{1,0:T(8,128)(2,1)S(1)}, bf16[256,512]{1,0:T(8,128)(2,1)S(1)}, u32[]{:S(2)}, u32[]{:S(2)}) %collective-permute-start.3) | collective-permute-done | bytes 262176 | tf_op jit(solution)/shard_map/ppermute | solution.py:708
  206.6 8.2 %residual.1 = (f32[256,2048]{1,0:T(8,128)}, bf16[256,2048]{1,0:T(8,128)(2,1)}, f32[256,1]{1,0:T(8,128)}) custom-call(bf16[256,2048]{1,0:T(8,128)(2,1)} %pad_maximum_fusion.5.att_ref, bf16[256,2048]{1,0:T(8,128)(2,1)} %get-tuple-element.115.x_ref, f32[1,2048]{1,0:T(1,128)} %get-tuple-element.158.gain_ref, bf16[1024,512]{1,0:T(8,128)(2,1)} %copy-done.12, ...), custom_call_target="tpu_custom_call" | custom-call | flops 2147483648 | bytes 14680064 | tf_op jit(solution)/shard_map/residual/pallas_call | solution.py:787
  221.5 9.8 %collective-permute-done.11 = bf16[128,2048]{0,1:T(8,128)(2,1)S(1)} collective-permute-done((bf16[128,2048]{0,1:T(8,128)(2,1)S(1)}, bf16[128,2048]{0,1:T(8,128)(2,1)S(1)}, u32[]{:S(2)}, u32[]{:S(2)}) %collective-permute-start.11) | collective-permute-done | bytes 524320 | tf_op jit(solution)/shard_map/ppermute | solution.py:708
  248.3 6.5 copy.105.refs_0_
  254.8 23.7 %hidden_units.2 = (bf16[1024,2560]{1,0:T(8,128)(2,1)}, bf16[1024,1280]{1,0:T(8,128)(2,1)}) custom-call(bf16[1024,2048]{1,0:T(8,128)(2,1)} %copy.105.refs_0_, bf16[1024,2048]{1,0:T(8,128)(2,1)} %get-tuple-element.133.refs_1_, bf16[2048,3840]{1,0:T(8,128)(2,1)} %all-gather.8.cloned.1.call-done.refs_2_.refs_3_.refs_4_.refs_1_, ...), custom_call_target="tpu_custom_call" | custom-call | flops 16106127360 | bytes 31981568 | tf_op jit(solution)/shard_map/hidden_units/pallas_call | solution.py:520
  278.5 23.3 %hidden_grad.2.refs_2_ = bf16[2048,3840]{1,0:T(8,128)(2,1)} custom-call(bf16[2048,1024]{1,0:T(8,128)(2,1)} %bitcast.15.refs_0_, bf16[2048,1024]{1,0:T(8,128)(2,1)} %copy.98.refs_4_.refs_1_, bf16[1024,2560]{1,0:T(8,128)(2,1)} %get-tuple-element.70.refs_2_.refs_0_, bf16[1024,1280]{1,0:T(8,128)(2,1)} %get-tuple-element.69.refs_3_.refs_0_), custom_call_target="tpu_custom_call" | custom-call | flops 16106127360 | bytes 31981568 | tf_op jit(solution)/shard_map/hidden_grad/pallas_call | solution.py:552
  301.9 17.2 %from_hidden.4.refs_2_ = f32[1024,2048]{1,0:T(8,128)} custom-call(bf16[1024,2560]{1,0:T(8,128)(2,1)} %get-tuple-element.70.refs_2_.refs_0_, bf16[2048,3840]{1,0:T(8,128)(2,1)} %all-gather.8.cloned.1.call-done.refs_2_.refs_3_.refs_4_.refs_1_, bf16[2048,3840]{1,0:T(8,128)(2,1)} %hidden_grad.2.refs_2_), custom_call_target="tpu_custom_call" | custom-call | flops 10737418240 | bytes 29360128 | tf_op jit(solution)/shard_map/from_hidden/pallas_call | solution.py:591
  319.2 12.6 %from_hidden.5.refs_5_.refs_2_ = f32[1024,2048]{1,0:T(8,128)} custom-call(bf16[1024,1280]{1,0:T(8,128)(2,1)} %get-tuple-element.69.refs_3_.refs_0_, bf16[2048,3840]{1,0:T(8,128)(2,1)} %all-gather.8.cloned.1.call-done.refs_2_.refs_3_.refs_4_.refs_1_, f32[1024,2048]{1,0:T(8,128)} %from_hidden.4.refs_2_), custom_call_target="tpu_custom_call" | custom-call | flops 5368709120 | bytes 26738688 | tf_op jit(solution)/shard_map/from_hidden/pallas_call | solution.py:591
  331.8 16.9 %hidden_units.3 = (bf16[1024,1536]{1,0:T(8,128)(2,1)}, bf16[1024,768]{1,0:T(8,128)(2,1)}) custom-call(bf16[1024,2048]{1,0:T(8,128)(2,1)} %copy.105.refs_0_, bf16[1024,2048]{1,0:T(8,128)(2,1)} %get-tuple-element.133.refs_1_, bf16[2048,2304]{1,0:T(8,128)(2,1)} %all-gather.6.cloned.1.call-done.refs_2_.refs_3_.refs_4_.refs_1_, ...), custom_call_target="tpu_custom_call" | custom-call | flops 9663676416 | bytes 22544384 | tf_op jit(solution)/shard_map/hidden_units/pallas_call | solution.py:520
  348.6 13.4 %from_hidden.6 = bf16[1024,2048]{1,0:T(8,128)(2,1)} custom-call(bf16[1024,1536]{1,0:T(8,128)(2,1)} %get-tuple-element.73.refs_0_.refs_2_, bf16[2048,2304]{1,0:T(8,128)(2,1)} %all-gather.6.cloned.1.call-done.refs_2_.refs_3_.refs_4_.refs_1_, f32[1024,2048]{1,0:T(8,128)} %from_hidden.4.refs_2_), custom_call_target="tpu_custom_call" | custom-call | flops 6442450944 | bytes 20971520 | tf_op jit(solution)/shard_map/from_hidden/pallas_call | solution.py:591
  366.1 12.8 %collective-permute-done.18.refs_5_ = bf16[128,2048]{1,0:T(8,128)(2,1)S(1)} collective-permute-done((bf16[128,2048]{1,0:T(8,128)(2,1)S(1)}, bf16[128,2048]{1,0:T(8,128)(2,1)S(1)}, u32[]{:S(2)}, u32[]{:S(2)}) %collective-permute-start.18) | collective-permute-done | bytes 524320 | tf_op jit(solution)/shard_map/ppermute | solution.py:708
  386.7 7.7 %collective-permute-done.19.refs_8_ = bf16[128,2048]{1,0:T(8,128)(2,1)S(1)} collective-permute-done((bf16[128,2048]{1,0:T(8,128)(2,1)S(1)}, bf16[128,2048]{1,0:T(8,128)(2,1)S(1)}, u32[]{:S(2)}, u32[]{:S(2)}) %collective-permute-start.19) | collective-permute-done | bytes 524320 | tf_op jit(solution)/shard_map/ppermute | solution.py:708
  407.2 16.2 %hidden_grad.3 = bf16[2048,2304]{1,0:T(8,128)(2,1)} custom-call(bf16[2048,1024]{1,0:T(8,128)(2,1)} %bitcast.15.refs_0_, bf16[2048,1024]{1,0:T(8,128)(2,1)} %copy.98.refs_4_.refs_1_, bf16[1024,1536]{1,0:T(8,128)(2,1)} %get-tuple-element.73.refs_0_.refs_2_, bf16[1024,768]{1,0:T(8,128)(2,1)} %get-tuple-element.71.refs_0_.refs_3_, bf16[128,2048]{1,0:T(8,128)(2,1)} %copy-done.31, ...), custom_call_target="tpu_custom_call" | custom-call | flops 9663676416 | bytes 22544384 | tf_op jit(solution)/shard_map/hidden_grad/pallas_call | solution.py:552
  431.7 6.8 attended_back.1
  441.9 11.1 %from_hidden.7.refs_12_.refs_0_ = bf16[1024,2048]{1,0:T(8,128)(2,1)} custom-call(bf16[1024,768]{1,0:T(8,128)(2,1)} %get-tuple-element.71.refs_0_.refs_3_, bf16[2048,2304]{1,0:T(8,128)(2,1)} %all-gather.6.cloned.1.call-done.refs_2_.refs_3_.refs_4_.refs_1_, f32[1024,2048]{1,0:T(8,128)} %from_hidden.5.refs_5_.refs_2_, bf16[256,512]{1,0:T(8,128)(2,1)} %get-tuple-element.74.refs_3_), custom_call_target="tpu_custom_call" | custom-call | flops 3221225472 | bytes 19398656 | tf_op jit(solution)/shard_map/from_hidden/pallas_call | solution.py:591
  458.4 9.3 %collective-permute-done.27 = bf16[128,2048]{1,0:T(8,128)(2,1)S(1)} collective-permute-done((bf16[128,2048]{1,0:T(8,128)(2,1)S(1)}, bf16[128,2048]{1,0:T(8,128)(2,1)S(1)}, u32[]{:S(2)}, u32[]{:S(2)}) %collective-permute-start.27) | collective-permute-done | bytes 524320 | tf_op jit(solution)/shard_map/ppermute | solution.py:708
  475.7 30.1 %attend_back.1 = (bf16[1024,512]{1,0:T(8,128)(2,1)}, f32[1024,1024]{1,0:T(8,128)}, f32[1024,1024]{1,0:T(8,128)}) custom-call(s32[4]{0:T(128)} %convert_reduce_fusion.low_ref.refs_0_, bf16[1024,512]{1,0:T(8,128)(2,1)} %get-tuple-element.64.q_ref.refs_1_, bf16[1024,1024]{1,0:T(8,128)(2,1)} %collective-permute-done.1.prev_ref.refs_2_, ...), custom_call_target="tpu_custom_call" | custom-call | flops 12884901888 | bytes 16777216 | tf_op jit(solution)/shard_map/attend_back/pallas_call | solution.py:400
  512.0 13.0 %adamw_hidden.2 = (f32[2,256,2048]{2,1,0:T(8,128)}, f32[2,256,2048]{2,1,0:T(8,128)}, f32[2,256,2048]{2,1,0:T(8,128)}, f32[2,256,2048]{2,1,0:T(8,128)}, f32[256,2...) custom-call(bf16[256,3840]{1,0:T(8,128)(2,1)} %reduce-scatter.4.cloned.1.call-done.g_ref, ...), custom_call_target="tpu_custom_call" | custom-call | flops 14745600 | bytes 29491200 | tf_op jit(solution)/shard_map/adamw_hidden/pallas_call | solution.py:677
  525.1 6.9 join_dproj.1.refs_1_
  532.0 10.6 %convolution_convert_fusion = bf16[2048,1536]{1,0:T(8,128)(2,1)} fusion(bf16[1024,2048]{1,0:T(8,128)(2,1)S(1)} %copy-done.20, bf16[1024,1536]{1,0:T(8,128)(2,1)} %join_dproj.1.refs_1_), kind=kOutput, calls=%fused_computation.6 | convolution fusion | flops 6445596672 | bytes 13631488 | tf_op jit(solution)/shard_map/dot_general | solution.py:72
  542.5 8.3 %pad_maximum_fusion = bf16[2048,2048]{1,0:T(8,128)(2,1)} fusion(bf16[2048,512]{1,0:T(8,128)(2,1)} %convolution_convert_fusion.1.refs_5_, bf16[2048,1536]{1,0:T(8,128)(2,1)} %convolution_convert_fusion), kind=kLoop, calls=%fused_computation.5 | loop fusion | flops 16777216 | bytes 16777216 | tf_op jit(solution)/shard_map/concatenate | solution.py:988
  581.7 7.5 %reduce-scatter.6.cloned.1.call-done.g_ref = bf16[256,2304]{1,0:T(8,128)(2,1)} async-done(((bf16[2048,2304]{1,0:T(8,128)(2,1)}), bf16[256,2304]{1,0:T(8,128)(2,1)}) %reduce-scatter.6.cloned.1.call-update) | async-done | bytes 1179664 | tf_op jit(solution)/shard_map/reduce_scatter | solution.py:952
  589.2 9.8 %adamw_hidden.3 = (f32[2,256,2048]{2,1,0:T(8,128)}, f32[2,256,2048]{2,1,0:T(8,128)}, f32[2,256,2048]{2,1,0:T(8,128)}, f32[2,256,2048]{2,1,0:T(8,128)}, f32[256,2...) custom-call(bf16[256,2304]{1,0:T(8,128)(2,1)} %reduce-scatter.6.clon, ...), custom_call_target="tpu_custom_call", output_to_operand_aliasing={{0}: (7, {}), {1}: (8, {}), {2}: (9, {}), {3}: (10, {}), {4... | custom-call | flops 8847360 | bytes 17694720 | tf_op jit(solution)/shard_map/adamw_hidden/pallas_call | solution.py:677
  620.2 14.3 %collective-permute-done.35 = bf16[128,2048]{1,0:T(8,128)(2,1)S(1)} collective-permute-done((bf16[128,2048]{1,0:T(8,128)(2,1)S(1)}, bf16[128,2048]{1,0:T(8,128)(2,1)S(1)}, u32[]{:S(2)}, u32[]{:S(2)}) %collective-permute-start.35) | collective-permute-done | bytes 524320 | tf_op jit(solution)/shard_map/ppermute | solution.py:708
  641.8 9.8 %collective-permute-done.38 = bf16[128,2048]{1,0:T(8,128)(2,1)S(1)} collective-permute-done((bf16[128,2048]{1,0:T(8,128)(2,1)S(1)}, bf16[128,2048]{1,0:T(8,128)(2,1)S(1)}, u32[]{:S(2)}, u32[]{:S(2)}) %collective-permute-start.38) | collective-permute-done | bytes 524320 | tf_op jit(solution)/shard_map/ppermute | solution.py:708
  690.8 6.7 adamw.2
  (349 shorter events, 268.1 us)
Async XLA Ops:
  7.2 87.9 %all-gather.4.cloned.1.call-start = ((), (), s32[]{:S(2)}) async-start(), calls=%async_computation.3 | async-start | bytes 9437184 | tf_op jit(solution)/shard_map/all_gather | solution.py:892
  10.2 244.6 %all-gather.8.cloned.1.call-start = ((), (), s32[]{:S(2)}) async-start(), calls=%async_computation.5 | async-start | bytes 17694720 | tf_op jit(solution)/shard_map/all_gather | solution.py:894
  14.4 317.4 %all-gather.6.cloned.1.call-start = ((), (), s32[]{:S(2)}) async-start(), calls=%async_computation.4 | async-start | bytes 10616832 | tf_op jit(solution)/shard_map/all_gather | solution.py:894
  18.4 493.6 %reduce-scatter.4.cloned.1.call-start = ((), (), s32[]{:S(2)}) async-start(), calls=%async_computation.6 | async-start | bytes 17694720 | tf_op jit(solution)/shard_map/reduce_scatter | solution.py:952
  106.4 34.6 %collective-permute-start.1 = (bf16[1024,1024]{1,0:T(8,128)(2,1)}, bf16[1024,1024]{1,0:T(8,128)(2,1)}, u32[]{:S(2)}, u32[]{:S(2)}) collective-permute-start(bf16[1024,1024]{1,0:T(8,128)(2,1)} %get-tuple-element.65.own_ref.refs_3_), channel_id=1, source_target_pairs={{0,4},{1,5},{2,6},{3,7},{8,12},{9,13},{10,14},{11,15},{16,20},{17,... | collective-permute-start | bytes 6291464 | tf_op jit(solution)/shard_map/ppermute | solution.py:925
  111.8 26.3 %collective-permute-start.8 = (bf16[1024,512]{1,0:T(8,128)(2,1)S(1)}, bf16[1024,512]{1,0:T(8,128)(2,1)}, u32[]{:S(2)}, u32[]{:S(2)}) collective-permute-start(bf16[1024,512]{1,0:T(8,128)(2,1)S(1)} %get-tuple-element.119.refs_1_.refs_2_), channel_id=1, source_target_pairs={{0,2},{1,3},{2,0},{3,1},{4,6},{5,7},{6,4},{7,5},{8,10},{9,11},{10,... | collective-permute-start | bytes 3145736 | tf_op jit(solution)/shard_map/ppermute | solution.py:708
  113.3 26.2 %collective-permute-start.5 = (bf16[1024,512]{1,0:T(8,128)(2,1)S(1)}, bf16[1024,512]{1,0:T(8,128)(2,1)}, u32[]{:S(2)}, u32[]{:S(2)}) collective-permute-start(bf16[1024,512]{1,0:T(8,128)(2,1)S(1)} %get-tuple-element.120.refs_0_.refs_1_), channel_id=1, source_target_pairs={{0,1},{1,0},{2,3},{3,2},{4,5},{5,4},{6,7},{7,6},{8,9},{9,8},{10,11... | collective-permute-start | bytes 3145736 | tf_op jit(solution)/shard_map/ppermute | solution.py:708
  119.7 84.8 %collective-permute-start.6 = (bf16[1024,512]{1,0:T(8,128)(2,1)S(1)}, bf16[1024,512]{1,0:T(8,128)(2,1)S(1)}, u32[]{:S(2)}, u32[]{:S(2)}) collective-permute-start(bf16[1024,512]{1,0:T(8,128)(2,1)S(1)} %get-tuple-element.119.refs_1_.refs_2_), channel_id=1, source_target_pairs={{0,1},{1,0},{2,3},{3,2},{4,5},{5,4},{6,7},{7,6},{8,9},{9,8},{10,11... | collective-permute-start | bytes 3145736 | tf_op jit(solution)/shard_map/ppermute | solution.py:708
  120.2 84.2 %collective-permute-start.7 = (bf16[1024,512]{1,0:T(8,128)(2,1)S(1)}, bf16[1024,512]{1,0:T(8,128)(2,1)S(1)}, u32[]{:S(2)}, u32[]{:S(2)}) collective-permute-start(bf16[1024,512]{1,0:T(8,128)(2,1)S(1)} %get-tuple-element.120.refs_0_.refs_1_), channel_id=1, source_target_pairs={{0,2},{1,3},{2,0},{3,1},{4,6},{5,7},{6,4},{7,5},{8,10},{9,11},{10,... | collective-permute-start | bytes 3145736 | tf_op jit(solution)/shard_map/ppermute | solution.py:708
  138.0 66.4 %collective-permute-start.10 = (bf16[1024,512]{1,0:T(8,128)(2,1)}, bf16[1024,512]{1,0:T(8,128)(2,1)S(1)}, u32[]{:S(2)}, u32[]{:S(2)}) collective-permute-start(bf16[1024,512]{1,0:T(8,128)(2,1)} %collective-permute-done.8.refs_5_.refs_6_), channel_id=1, source_target_pairs={{0,1},{1,0},{2,3},{3,2},{4,5},{5,4},{6,7},{7,6},{8,9},{9,8},{10,11... | collective-permute-start | bytes 3145736 | tf_op jit(solution)/shard_map/ppermute | solution.py:708
  139.5 64.9 %collective-permute-start.9 = (bf16[1024,512]{1,0:T(8,128)(2,1)}, bf16[1024,512]{1,0:T(8,128)(2,1)S(1)}, u32[]{:S(2)}, u32[]{:S(2)}) collective-permute-start(bf16[1024,512]{1,0:T(8,128)(2,1)} %collective-permute-done.5.refs_2_.refs_3_), channel_id=1, source_target_pairs={{0,2},{1,3},{2,0},{3,1},{4,6},{5,7},{6,4},{7,5},{8,10},{9,11},{10,... | collective-permute-start | bytes 3145736 | tf_op jit(solution)/shard_map/ppermute | solution.py:708
  157.6 29.3 %collective-permute-start.2 = (bf16[256,512]{1,0:T(8,128)(2,1)S(1)}, bf16[256,512]{1,0:T(8,128)(2,1)S(1)}, u32[]{:S(2)}, u32[]{:S(2)}) collective-permute-start(bf16[256,512]{1,0:T(8,128)(2,1)S(1)} %get-tuple-element.154), channel_id=1, source_target_pairs={{0,1},{1,0},{2,3},{3,2},{4,5},{5,4},{6,7},{7,6},{8,9},{9,8},{10,11... | collective-permute-start | bytes 786440 | tf_op jit(solution)/shard_map/ppermute | solution.py:708
  301.9 287.3 %reduce-scatter.6.cloned.1.call-start = ((), (), s32[]{:S(2)}) async-start(), calls=%async_computation.7 | async-start | bytes 10616832 | tf_op jit(solution)/shard_map/reduce_scatter | solution.py:952
  364.1 22.6 %collective-permute-start.17 = (bf16[128,2048]{1,0:T(8,128)(2,1)S(1)}, bf16[128,2048]{1,0:T(8,128)(2,1)S(1)}, u32[]{:S(2)}, u32[]{:S(2)}) collective-permute-start(bf16[128,2048]{1,0:T(8,128)(2,1)S(1)} %get-tuple-element.129), channel_id=1, source_target_pairs={{0,1},{1,0},{2,3},{3,2},{4,5},{5,4},{6,7},{7,6},{8,9},{9,8},{10,11... | collective-permute-start | bytes 1572872 | tf_op jit(solution)/shard_map/ppermute | solution.py:708
  423.4 264.2 %reduce-scatter.8.cloned.1.call-start = ((), (), s32[]{:S(2)}) async-start(), calls=%async_computation.8 | async-start | bytes 9437184 | tf_op jit(solution)/shard_map/reduce_scatter | solution.py:987
  430.3 26.0 %collective-permute-start.26 = (bf16[128,2048]{1,0:T(8,128)(2,1)S(1)}, bf16[128,2048]{1,0:T(8,128)(2,1)S(1)}, u32[]{:S(2)}, u32[]{:S(2)}) collective-permute-start(bf16[128,2048]{1,0:T(8,128)(2,1)S(1)} %get-tuple-element.148), channel_id=1, source_target_pairs={{0,1},{1,0},{2,3},{3,2},{4,5},{5,4},{6,7},{7,6},{8,9},{9,8},{10,11... | collective-permute-start | bytes 1572872 | tf_op jit(solution)/shard_map/ppermute | solution.py:708
  431.1 26.0 %collective-permute-start.29 = (bf16[128,2048]{1,0:T(8,128)(2,1)S(1)}, bf16[128,2048]{1,0:T(8,128)(2,1)S(1)}, u32[]{:S(2)}, u32[]{:S(2)}) collective-permute-start(bf16[128,2048]{1,0:T(8,128)(2,1)S(1)} %get-tuple-element.147), channel_id=1, source_target_pairs={{0,2},{1,3},{2,0},{3,1},{4,6},{5,7},{6,4},{7,5},{8,10},{9,11},{10,... | collective-permute-start | bytes 1572872 | tf_op jit(solution)/shard_map/ppermute | solution.py:708
  569.1 32.3 %collective-permute-start.39 = (bf16[128,2048]{1,0:T(8,128)(2,1)}, bf16[128,2048]{1,0:T(8,128)(2,1)}, u32[]{:S(2)}, u32[]{:S(2)}) collective-permute-start(bf16[128,2048]{1,0:T(8,128)(2,1)} %slice.233), channel_id=1, source_target_pairs={{0,1},{1,0},{2,3},{3,2},{4,5},{5,4},{6,7},{7,6},{8,9},{9,8},{10,11... | collective-permute-start | bytes 1572872 | tf_op jit(solution)/shard_map/ppermute | solution.py:708
  572.6 30.4 %collective-permute-start.42 = (bf16[128,2048]{1,0:T(8,128)(2,1)}, bf16[128,2048]{1,0:T(8,128)(2,1)}, u32[]{:S(2)}, u32[]{:S(2)}) collective-permute-start(bf16[128,2048]{1,0:T(8,128)(2,1)} %slice.237), channel_id=1, source_target_pairs={{0,2},{1,3},{2,0},{3,1},{4,6},{5,7},{6,4},{7,5},{8,10},{9,11},{10,... | collective-permute-start | bytes 1572872 | tf_op jit(solution)/shard_map/ppermute | solution.py:708
  575.5 23.6 %collective-permute-start.34 = (bf16[128,2048]{1,0:T(8,128)(2,1)}, bf16[128,2048]{1,0:T(8,128)(2,1)}, u32[]{:S(2)}, u32[]{:S(2)}) collective-permute-start(bf16[128,2048]{1,0:T(8,128)(2,1)} %get-tuple-element.126), channel_id=1, source_target_pairs={{0,1},{1,0},{2,3},{3,2},{4,5},{5,4},{6,7},{7,6},{8,9},{9,8},{10,11... | collective-permute-start | bytes 1572872 | tf_op jit(solution)/shard_map/ppermute | solution.py:708
  577.6 29.2 %collective-permute-start.44 = (bf16[128,2048]{1,0:T(8,128)(2,1)}, bf16[128,2048]{1,0:T(8,128)(2,1)}, u32[]{:S(2)}, u32[]{:S(2)}) collective-permute-start(bf16[128,2048]{1,0:T(8,128)(2,1)} %add_convert_fusion), channel_id=1, source_target_pairs={{0,1},{1,0},{2,3},{3,2},{4,5},{5,4},{6,7},{7,6},{8,9},{9,8},{10,11... | collective-permute-start | bytes 1572872 | tf_op jit(solution)/shard_map/ppermute | solution.py:708
  579.4 28.9 %collective-permute-start.41 = (bf16[128,2048]{1,0:T(8,128)(2,1)}, bf16[128,2048]{1,0:T(8,128)(2,1)}, u32[]{:S(2)}, u32[]{:S(2)}) collective-permute-start(bf16[128,2048]{1,0:T(8,128)(2,1)} %add_convert_fusion.1), channel_id=1, source_target_pairs={{0,2},{1,3},{2,0},{3,1},{4,6},{5,7},{6,4},{7,5},{8,10},{9,11},{10,... | collective-permute-start | bytes 1572872 | tf_op jit(solution)/shard_map/ppermute | solution.py:708
  603.0 38.2 %collective-permute-start.36 = (bf16[128,2048]{1,0:T(8,128)(2,1)}, bf16[128,2048]{1,0:T(8,128)(2,1)S(1)}, u32[]{:S(2)}, u32[]{:S(2)}) collective-permute-start(bf16[128,2048]{1,0:T(8,128)(2,1)} %get-tuple-element.125), channel_id=1, source_target_pairs={{0,2},{1,3},{2,0},{3,1},{4,6},{5,7},{6,4},{7,5},{8,10},{9,11},{10,... | collective-permute-start | bytes 1572872 | tf_op jit(solution)/shard_map/ppermute | solution.py:708
  606.8 27.7 %collective-permute-start.35 = (bf16[128,2048]{1,0:T(8,128)(2,1)S(1)}, bf16[128,2048]{1,0:T(8,128)(2,1)S(1)}, u32[]{:S(2)}, u32[]{:S(2)}) collective-permute-start(bf16[128,2048]{1,0:T(8,128)(2,1)S(1)} %add_convert_fusion.3), channel_id=1, source_target_pairs={{0,2},{1,3},{2,0},{3,1},{4,6},{5,7},{6,4},{7,5},{8,10},{9,11},{10,... | collective-permute-start | bytes 1572872 | tf_op jit(solution)/shard_map/ppermute | solution.py:708
  612.7 40.4 %collective-permute-start.45 = (bf16[128,2048]{1,0:T(8,128)(2,1)}, bf16[128,2048]{1,0:T(8,128)(2,1)S(1)}, u32[]{:S(2)}, u32[]{:S(2)}) collective-permute-start(bf16[128,2048]{1,0:T(8,128)(2,1)} %get-tuple-element.142), channel_id=1, source_target_pairs={{0,1},{1,0},{2,3},{3,2},{4,5},{5,4},{6,7},{7,6},{8,9},{9,8},{10,11... | collective-permute-start | bytes 1572872 | tf_op jit(solution)/shard_map/ppermute | solution.py:708
  617.9 54.6 %collective-permute-start.54 = (bf16[128,2048]{1,0:T(8,128)(2,1)}, bf16[128,2048]{1,0:T(8,128)(2,1)}, u32[]{:S(2)}, u32[]{:S(2)}) collective-permute-start(bf16[128,2048]{1,0:T(8,128)(2,1)} %get-tuple-element.142), channel_id=1, source_target_pairs={{0,2},{1,3},{2,0},{3,1},{4,6},{5,7},{6,4},{7,5},{8,10},{9,11},{10,... | collective-permute-start | bytes 1572872 | tf_op jit(solution)/shard_map/ppermute | solution.py:708
  619.4 50.3 %collective-permute-start.53 = (bf16[128,2048]{1,0:T(8,128)(2,1)}, bf16[128,2048]{1,0:T(8,128)(2,1)}, u32[]{:S(2)}, u32[]{:S(2)}) collective-permute-start(bf16[128,2048]{1,0:T(8,128)(2,1)} %get-tuple-element.141), channel_id=1, source_target_pairs={{0,1},{1,0},{2,3},{3,2},{4,5},{5,4},{6,7},{7,6},{8,9},{9,8},{10,11... | collective-permute-start | bytes 1572872 | tf_op jit(solution)/shard_map/ppermute | solution.py:708
  662.9 23.9 %collective-permute-start.49 = (bf16[128,2048]{1,0:T(8,128)(2,1)S(1)}, bf16[128,2048]{1,0:T(8,128)(2,1)S(1)}, u32[]{:S(2)}, u32[]{:S(2)}) collective-permute-start(bf16[128,2048]{1,0:T(8,128)(2,1)S(1)} %get-tuple-element.140), channel_id=1, source_target_pairs={{0,2},{1,3},{2,0},{3,1},{4,6},{5,7},{6,4},{7,5},{8,10},{9,11},{10,... | collective-permute-start | bytes 1572872 | tf_op jit(solution)/shard_map/ppermute | solution.py:708
  672.5 35.7 %collective-permute-start.55 = (bf16[128,2048]{1,0:T(8,128)(2,1)S(1)}, bf16[128,2048]{1,0:T(8,128)(2,1)}, u32[]{:S(2)}, u32[]{:S(2)}) collective-permute-start(bf16[128,2048]{1,0:T(8,128)(2,1)S(1)} %copy-done.22), channel_id=1, source_target_pairs={{0,2},{1,3},{2,0},{3,1},{4,6},{5,7},{6,4},{7,5},{8,10},{9,11},{10,... | collective-permute-start | bytes 1572872 | tf_op jit(solution)/shard_map/ppermute | solution.py:708
  676.4 37.4 %collective-permute-start.56 = (bf16[128,2048]{1,0:T(8,128)(2,1)S(1)}, bf16[128,2048]{1,0:T(8,128)(2,1)}, u32[]{:S(2)}, u32[]{:S(2)}) collective-permute-start(bf16[128,2048]{1,0:T(8,128)(2,1)S(1)} %copy-done.24), channel_id=1, source_target_pairs={{0,1},{1,0},{2,3},{3,2},{4,5},{5,4},{6,7},{7,6},{8,9},{9,8},{10,11... | collective-permute-start | bytes 1572872 | tf_op jit(solution)/shard_map/ppermute | solution.py:708
  683.6 32.2 %collective-permute-start.51 = (bf16[128,2048]{1,0:T(8,128)(2,1)S(1)}, bf16[128,2048]{1,0:T(8,128)(2,1)S(1)}, u32[]{:S(2)}, u32[]{:S(2)}) collective-permute-start(bf16[128,2048]{1,0:T(8,128)(2,1)S(1)} %collective-permute-done.47), channel_id=1, source_target_pairs={{0,2},{1,3},{2,0},{3,1},{4,6},{5,7},{6,4},{7,5},{8,10},{9,11},{10,... | collective-permute-start | bytes 1572872 | tf_op jit(solution)/shard_map/ppermute | solution.py:708
  686.0 36.6 %collective-permute-start.52 = (bf16[128,2048]{1,0:T(8,128)(2,1)S(1)}, bf16[128,2048]{1,0:T(8,128)(2,1)S(1)}, u32[]{:S(2)}, u32[]{:S(2)}) collective-permute-start(bf16[128,2048]{1,0:T(8,128)(2,1)S(1)} %collective-permute-done.50), channel_id=1, source_target_pairs={{0,1},{1,0},{2,3},{3,2},{4,5},{5,4},{6,7},{7,6},{8,9},{9,8},{10,11... | collective-permute-start | bytes 1572872 | tf_op jit(solution)/shard_map/ppermute | solution.py:708
  (89 other events, 1218.8 us)
Sparse Core Ops, SparseCore 0:
  10.3 84.7 all-gather.3
  97.3 141.0 all-gather.7
  240.6 88.9 all-gather.5
  331.8 157.3 reduce-scatter.3
  491.3 97.8 reduce-scatter.5
  591.4 87.9 reduce-scatter.7
